TPU v7x, 512 devices: a whole 4x4x16 slice. The times are simulated.
512 devices in a mesh: ctx: 32 (over y_lo, z), tp: 4 (over x), dp: 4 (over y_hi, core).
Axes of the slice: x: 4, y: 4 (y_hi: 2, y_lo: 2; y = y_hi * 2 + y_lo), z: 16, core: 2. Of those that a mesh axis runs over, the one named last changes fastest.
Arguments:
- queries: bfloat16 [4, 4096, 4096], P('dp', 'ctx', 'tp'), may hold values from -6 to 6
- keys: bfloat16 [4, 32, 4, 32, 128, 128], P('dp', None, 'tp', 'ctx'), may hold values from -6 to 6
- values: bfloat16 [4, 32, 4, 32, 128, 128], P('dp', None, 'tp', 'ctx'), may hold values from -6 to 6
- cotangent: bfloat16 [4, 4096, 4096], P('dp', 'ctx', 'tp'), may hold values from -6 to 6
- lengths: int32 [4, 64, 2], P('dp'), may hold values from 16 to 128
Outputs:
- attended: bfloat16 [4, 4096, 4096], P('dp', 'ctx', 'tp')
- grad_queries: bfloat16 [4, 4096, 4096], P('dp', 'ctx', 'tp')
- grad_keys: bfloat16 [4, 32, 4, 32, 128, 128], P('dp', None, 'tp', 'ctx')
- grad_values: bfloat16 [4, 32, 4, 32, 128, 128], P('dp', None, 'tp', 'ctx')
Inputs may be any that keep to these rules, and one draw needn't show every extreme that they name: Neighbour n of span u has its first lengths[u, n] tokens live; the others are padding.
All inputs are finite; a program needn't handle non-finite values.
Results may differ from a plain program's by a relative error of at most 0.012.
The roundings to bfloat16 on the way count: a program that leaves them out, or rounds other values in their place, can miss the bound.
Values may be sent and summed in bfloat16 or wider, within the bound.
No kernel may reach another device: no remote copies, remote signals or barrier semaphores. Data moves between devices by JAX's collectives and lax.ppermute only.
A program may use at most 64 MiB of HBM per device.

v0:
```python
import math

import jax
import jax.numpy as jnp
from jax import lax
from jax.sharding import PartitionSpec as P

DH = 128
SPAN = 64
NBR = 2
NEIGH = 128


def from_behind(block, axis, distance):
    devices = range(lax.axis_size(axis))
    route = [(i - distance, i) for i in devices if i - distance in devices]
    return lax.ppermute(block, axis, route)


def side_by_side(arrays, axis, split_dim, concat_dim, along):
    both = jnp.concatenate(arrays, axis=along)
    filled, at, outs = (
        lax.all_to_all(both, axis, split_axis=split_dim, concat_axis=concat_dim, tiled=True),
        0,
        [],
    )
    for a in arrays:
        outs.append(lax.slice_in_dim(filled, at, at + a.shape[along], axis=along))
        at += a.shape[along]
    return tuple(outs)


def rotate(tensor, direction):
    middle = tensor.shape[-1] // 2
    frequency = 10000.0 ** (-2.0 * jnp.arange(middle, dtype=jnp.float32) / tensor.shape[-1])
    angles = jnp.arange(tensor.shape[-2], dtype=jnp.float32)[:, None] * frequency[None, :]
    cosine = jnp.cos(angles)
    sine_part = direction * jnp.sin(angles)
    lower_part = tensor[..., :middle].astype(jnp.float32)
    upper_part = tensor[..., middle:].astype(jnp.float32)
    return jnp.concatenate(
        [
            lower_part * cosine - upper_part * sine_part,
            lower_part * sine_part + upper_part * cosine,
        ],
        axis=-1,
    )


def live_scores(query_rows, key_rows, key_counts):
    scaling = 1.0 / math.sqrt(query_rows.shape[-1])
    scores = (
        jnp.einsum("zhid,zhjd->zhij", query_rows, key_rows, preferred_element_type=jnp.float32)
        * scaling
    )
    usable = lax.broadcasted_iota(jnp.int32, scores.shape, 3) < key_counts[:, None, None, None]
    return jnp.where(usable, scores, -jnp.inf)


def neighbour_forward(query_rows, key_rows, value_rows, key_counts):
    scores = live_scores(query_rows, key_rows, key_counts)
    maxima = jnp.max(scores, axis=-1, keepdims=True)
    weights = jnp.exp(scores - maxima)
    totals = jnp.sum(weights, axis=-1)
    summed = jnp.einsum(
        "zhij,zhjd->zhid",
        weights.astype(jnp.bfloat16),
        value_rows,
        preferred_element_type=jnp.float32,
    )
    return (summed / totals[..., None], maxima[..., 0] + jnp.log(totals))


def neighbour_backward(
    query_rows, key_rows, value_rows, key_counts, grad_rows, log_totals, output_dots
):
    scaling = 1.0 / math.sqrt(query_rows.shape[-1])
    scores = live_scores(query_rows, key_rows, key_counts)
    chances = jnp.exp(scores - log_totals[..., None])
    grad_values = jnp.einsum(
        "zhij,zhid->zhjd",
        chances.astype(jnp.bfloat16),
        grad_rows,
        preferred_element_type=jnp.float32,
    )
    grad_weights = jnp.einsum(
        "zhid,zhjd->zhij", grad_rows, value_rows, preferred_element_type=jnp.float32
    )
    grad_scores = (chances * (grad_weights - output_dots[..., None]) * scaling).astype(jnp.bfloat16)
    grad_query = jnp.einsum(
        "zhij,zhjd->zhid", grad_scores, key_rows, preferred_element_type=jnp.float32
    ).astype(jnp.bfloat16)
    grad_key = jnp.einsum(
        "zhij,zhid->zhjd", grad_scores, query_rows, preferred_element_type=jnp.float32
    )
    return (grad_query, grad_key, grad_values)


def combine_pairs(partial_value, log_parts, blocks):
    partial_value = partial_value.reshape((blocks, NBR) + partial_value.shape[1:])
    log_parts = log_parts.reshape((blocks, NBR) + log_parts.shape[1:])
    log_whole = jax.nn.logsumexp(log_parts, axis=1)
    attended = jnp.sum(
        jnp.exp(log_parts - log_whole[:, None])[..., None] * partial_value, axis=1
    ).astype(jnp.bfloat16)
    return (attended, log_whole)


def window_of(tokens, tail_rows, blocks, heads_here):
    joined = jnp.concatenate([tokens[0, SPAN - 1 :], tail_rows[0]], axis=0)
    return joined.reshape(blocks, SPAN, heads_here, DH).transpose(0, 2, 1, 3)


def rows_of(window_rows):
    return window_rows.transpose(0, 2, 1, 3).reshape(
        window_rows.shape[0] * window_rows.shape[2], -1
    )


def shards(queries, keys, values, cotangent, lengths):
    rows_dev = queries.shape[1]
    blocks = rows_dev // SPAN
    heads_here = queries.shape[2] // DH
    rim_rows = SPAN - 1
    tail_queries, tail_grads = from_behind(
        (queries[:, :rim_rows], cotangent[:, :rim_rows]), "ctx", -1
    )
    query_turned = rotate(window_of(queries, tail_queries, blocks, heads_here), 1.0).astype(
        jnp.bfloat16
    )
    window_grads = window_of(cotangent, tail_grads, blocks, heads_here)
    query_copies = jnp.repeat(query_turned, NBR, axis=0)[None, None]
    grad_copies = jnp.repeat(window_grads, NBR, axis=0)[None, None]
    moved_once = side_by_side((query_copies, grad_copies), "tp", 2, 3, 0)
    query_far, grad_far = side_by_side((moved_once[0], moved_once[1]), "ctx", 3, 1, 0)
    block_total = keys.shape[1]
    passages_here = keys.shape[2]
    heads_far = keys.shape[3]
    groups = block_total * passages_here
    query_flat = query_far.reshape(groups, heads_far, SPAN, DH)
    key_turned = rotate(keys.reshape(groups, heads_far, NEIGH, DH), 1.0).astype(jnp.bfloat16)
    value_flat = values.reshape(groups, heads_far, NEIGH, DH)
    length_table = lengths[0].reshape(block_total, blocks * NBR)
    far_counts = lax.dynamic_slice_in_dim(
        length_table, lax.axis_index("tp") * passages_here, passages_here, 1
    ).reshape(-1)
    partial_value, log_parts = neighbour_forward(query_flat, key_turned, value_flat, far_counts)
    far_shape = (1, block_total, passages_here, heads_far, SPAN)
    back_part, back_logs = (
        lax.all_to_all(
            lax.all_to_all(
                partial_value.reshape(far_shape + (DH,)),
                "ctx",
                split_axis=1,
                concat_axis=3,
                tiled=True,
            ),
            "tp",
            split_axis=3,
            concat_axis=2,
            tiled=True,
        ),
        lax.all_to_all(
            lax.all_to_all(
                log_parts.reshape(far_shape), "ctx", split_axis=1, concat_axis=3, tiled=True
            ),
            "tp",
            split_axis=3,
            concat_axis=2,
            tiled=True,
        ),
    )
    attended, log_whole = combine_pairs(back_part[0, 0], back_logs[0, 0], blocks)
    output_dots = jnp.sum(window_grads.astype(jnp.float32) * attended.astype(jnp.float32), axis=-1)
    moved_stats = side_by_side(
        (
            jnp.repeat(log_whole, NBR, axis=0)[None, None],
            jnp.repeat(output_dots, NBR, axis=0)[None, None],
        ),
        "tp",
        2,
        3,
        0,
    )
    logs_far, dots_far = side_by_side((moved_stats[0], moved_stats[1]), "ctx", 3, 1, 0)
    grad_query, grad_key, grad_values = neighbour_backward(
        query_flat,
        key_turned,
        value_flat,
        far_counts,
        grad_far.reshape(groups, heads_far, SPAN, DH),
        logs_far.reshape(groups, heads_far, SPAN),
        dots_far.reshape(groups, heads_far, SPAN),
    )
    grad_keys = rotate(grad_key, -1.0).astype(jnp.bfloat16).reshape(keys.shape)
    grad_vals = grad_values.astype(jnp.bfloat16).reshape(values.shape)
    query_parts = lax.all_to_all(
        lax.all_to_all(
            grad_query.reshape(far_shape + (DH,)), "ctx", split_axis=1, concat_axis=3, tiled=True
        ),
        "tp",
        split_axis=3,
        concat_axis=2,
        tiled=True,
    )[0, 0]
    grad_sum = jnp.sum(
        query_parts.reshape(blocks, NBR, heads_here, SPAN, DH).astype(jnp.float32), axis=1
    )
    grad_window = rotate(grad_sum, -1.0).astype(jnp.bfloat16)
    attended_rows = rows_of(attended)
    grad_rows = rows_of(grad_window)
    carried_out = from_behind(attended_rows[rows_dev - rim_rows :], "ctx", 1)
    carried_grad = from_behind(grad_rows[rows_dev - rim_rows :], "ctx", 1)
    attended_tokens = jnp.concatenate([carried_out, attended_rows[: rows_dev - rim_rows]], axis=0)[
        None
    ]
    grad_tokens = jnp.concatenate([carried_grad, grad_rows[: rows_dev - rim_rows]], axis=0)[None]
    return (attended_tokens, grad_tokens, grad_keys, grad_vals)


def solution(mesh):
    in_specs = (
        P("dp", "ctx", "tp"),
        P("dp", None, "tp", "ctx", None, None),
        P("dp", None, "tp", "ctx", None, None),
        P("dp", "ctx", "tp"),
        P("dp", None, None),
    )
    out_specs = (
        P("dp", "ctx", "tp"),
        P("dp", "ctx", "tp"),
        P("dp", None, "tp", "ctx", None, None),
        P("dp", None, "tp", "ctx", None, None),
    )
    return jax.shard_map(shards, mesh=mesh, in_specs=in_specs, out_specs=out_specs, check_vma=False)
```

profile of v0, /device:TPU:8, one launch (start us, length us, event | category | flops | bytes accessed | tf_op | source)
XLA Modules:
  0.0 298.9 jit_solution(11426853437950012622)
XLA Ops:
  1.7 11.3 %collective-permute-start.1 = (bf16[1,63,1024]{2,1,0:T(8,128)(2,1)S(1)}, bf16[1,63,1024]{2,1,0:T(8,128)(2,1)S(1)}, u32[]{:S(2)}, u32[]{:S(2)}) collective-permute-start(bf16[1,63,1024]{2,1,0:T(8,128)(2,1)S(1)} %slice.97), channel_id=1, source_target_pairs={{16,0},{32,16},{48,32},{64,48},{80,64},{96,80},{112,96},{128,112},... | collective-permute-start | bytes 387080 | tf_op jit(solution)/shard_map/ppermute | solution.py:17
  13.9 2.9 collective-permute-start
  21.9 17.8 %all_to_all.49 = bf16[2,1,4,8,64,128]{5,4,3,1,0,2:T(8,128)(2,1)S(1)} all-to-all(bf16[2,1,4,8,64,128]{5,4,3,1,0,2:T(8,128)(2,1)S(1)} %pad_maximum_fusion), channel_id=1, replica_groups=mesh['ctx'=32,'tp'=4,'dp'=4] {'tp'}, dimensions={2} | all-to-all | bytes 2097152 | tf_op jit(solution)/shard_map/all_to_all | solution.py:23
  40.8 8.2 %all-to-all-start.1 = ((bf16[2,1,1,32,64,128]{5,4,2,1,0,3:T(8,128)(2,1)}), bf16[2,1,1,32,64,128]{5,4,2,1,0,3:T(8,128)(2,1)S(1)}, u32[]{:S(2)}, u32[]{:S(2)}) async-start(bf16[2,1,1,32,64,128]{5,4,2,1,0,3:T(8,128)(2,1)} %pad_maximum_fusion.1), calls=%async_computation.1 | async-start | bytes 2097152 | tf_op jit(solution)/shard_map/all_to_all | solution.py:23
  51.5 2.2 fusion.14
  53.7 44.4 %all-to-all-done.1 = bf16[2,1,1,32,64,128]{5,4,2,1,0,3:T(8,128)(2,1)S(1)} async-done(((bf16[2,1,1,32,64,128]{5,4,2,1,0,3:T(8,128)(2,1)}), bf16[2,1,1,32,64,128]{5,4,2,1,0,3:T(8,128)(2,1)S(1)}, u32[]{:S(2)}, u32[]{:S(2)}) %all-to-all-start.1) | async-done | bytes 1048608 | tf_op jit(solution)/shard_map/all_to_all | solution.py:23
  98.1 2.5 fusion.37
  101.9 19.1 %all_to_all.100 = f32[1,32,1,1,64]{4,3,2,0,1:T(1,128)S(1)} all-to-all(f32[1,32,1,1,64]{4,3,2,0,1:T(1,128)S(1)} %bitcast.157), channel_id=1, replica_groups=mesh['ctx'=32,'tp'=4,'dp'=4] {'ctx'}, dimensions={1} | all-to-all | bytes 16384 | tf_op jit(solution)/shard_map/all_to_all | solution.py:164
  125.5 3.8 %all-to-all-start.3 = ((f32[4,1,512]{2,1,0:T(1,128)}), f32[4,1,512]{2,1,0:T(1,128)}, u32[]{:S(2)}, u32[]{:S(2)}) async-start(f32[4,1,512]{2,1,0:T(1,128)} %reshape.409), calls=%async_computation.3 | async-start | bytes 16384 | tf_op jit(solution)/shard_map/all_to_all | solution.py:163
  129.3 2.2 fusion.7
  131.5 3.1 %all-to-all-done.3 = f32[4,1,512]{2,1,0:T(1,128)} async-done(((f32[4,1,512]{2,1,0:T(1,128)}), f32[4,1,512]{2,1,0:T(1,128)}, u32[]{:S(2)}, u32[]{:S(2)}) %all-to-all-start.3) | async-done | bytes 8224 | tf_op jit(solution)/shard_map/all_to_all | solution.py:163
  134.7 5.8 %all-to-all-start.4 = ((f32[1,32,1,1,64,128]{5,4,3,2,0,1:T(8,128)}), f32[1,32,1,1,64,128]{5,4,3,2,0,1:T(8,128)}, u32[]{:S(2)}, u32[]{:S(2)}) async-start(f32[1,32,1,1,64,128]{5,4,3,2,0,1:T(8,128)} %fusion.7), calls=%async_computation.4 | async-start | bytes 2097152 | tf_op jit(solution)/shard_map/all_to_all | solution.py:151
  143.8 45.5 %all-to-all-done.4 = f32[1,32,1,1,64,128]{5,4,3,2,0,1:T(8,128)} async-done(((f32[1,32,1,1,64,128]{5,4,3,2,0,1:T(8,128)}), f32[1,32,1,1,64,128]{5,4,3,2,0,1:T(8,128)}, u32[]{:S(2)}, u32[]{:S(2)}) %all-to-all-start.4) | async-done | bytes 1048608 | tf_op jit(solution)/shard_map/all_to_all | solution.py:151
  189.3 4.2 %all-to-all-start.5 = ((f32[1,1,1,32,64,128]{5,4,2,1,0,3:T(8,128)}), f32[1,1,1,32,64,128]{5,4,2,1,0,3:T(8,128)}, u32[]{:S(2)}, u32[]{:S(2)}) async-start(f32[1,1,1,32,64,128]{5,4,2,1,0,3:T(8,128)} %bitcast.24), calls=%async_computation.5 | async-start | bytes 2097152 | tf_op jit(solution)/shard_map/all_to_all | solution.py:150
  196.2 8.3 %all-to-all-done.5 = f32[1,1,1,32,64,128]{5,4,2,1,0,3:T(8,128)} async-done(((f32[1,1,1,32,64,128]{5,4,2,1,0,3:T(8,128)}), f32[1,1,1,32,64,128]{5,4,2,1,0,3:T(8,128)}, u32[]{:S(2)}, u32[]{:S(2)}) %all-to-all-start.5) | async-done | bytes 1048608 | tf_op jit(solution)/shard_map/all_to_all | solution.py:150
  207.6 7.7 %all_to_all.101 = f32[4,1,1024]{2,1,0:T(1,128)S(1)} all-to-all(f32[4,1,1024]{2,1,0:T(1,128)S(1)} %reshape.411), channel_id=1, replica_groups=mesh['ctx'=32,'tp'=4,'dp'=4] {'tp'}, dimensions={0} | all-to-all | bytes 32768 | tf_op jit(solution)/shard_map/all_to_all | solution.py:23
  216.9 22.2 %all_to_all.102 = f32[32,1,128]{2,1,0:T(1,128)S(1)} all-to-all(f32[32,1,128]{2,1,0:T(1,128)S(1)} %reshape.413), channel_id=1, replica_groups=mesh['ctx'=32,'tp'=4,'dp'=4] {'ctx'}, dimensions={0} | all-to-all | bytes 32768 | tf_op jit(solution)/shard_map/all_to_all | solution.py:23
  243.3 5.8 %all-to-all-start.8 = ((bf16[1,32,1,1,64,128]{5,4,3,2,0,1:T(8,128)(2,1)}), bf16[1,32,1,1,64,128]{5,4,3,2,0,1:T(8,128)(2,1)}, u32[]{:S(2)}, u32[]{:S(2)}) async-start(bf16[1,32,1,1,64,128]{5,4,3,2,0,1:T(8,128)(2,1)} %fusion.10), calls=%async_computation.8 | async-start | bytes 1048576 | tf_op jit(solution)/shard_map/all_to_all | solution.py:198
  250.0 3.4 %collective-permute-start.2 = (bf16[63,1024]{1,0:T(8,128)(2,1)}, bf16[63,1024]{1,0:T(8,128)(2,1)}, u32[]{:S(2)}, u32[]{:S(2)}) collective-permute-start(bf16[63,1024]{1,0:T(8,128)(2,1)} %slice.127), channel_id=1, source_target_pairs={{0,16},{16,32},{32,48},{48,64},{64,80},{80,96},{96,112},{112,128},... | collective-permute-start | bytes 387080 | tf_op jit(solution)/shard_map/ppermute | solution.py:17
  255.4 21.3 %all-to-all-done.8 = bf16[1,32,1,1,64,128]{5,4,3,2,0,1:T(8,128)(2,1)} async-done(((bf16[1,32,1,1,64,128]{5,4,3,2,0,1:T(8,128)(2,1)}), bf16[1,32,1,1,64,128]{5,4,3,2,0,1:T(8,128)(2,1)}, u32[]{:S(2)}, u32[]{:S(2)}) %all-to-all-start.8) | async-done | bytes 524320 | tf_op jit(solution)/shard_map/all_to_all | solution.py:198
  276.7 3.8 %all-to-all-start.9 = ((bf16[1,1,1,32,64,128]{5,4,2,1,0,3:T(8,128)(2,1)}), bf16[1,1,1,32,64,128]{5,4,2,1,0,3:T(8,128)(2,1)S(1)}, u32[]{:S(2)}, u32[]{:S(2)}) async-start(bf16[1,1,1,32,64,128]{5,4,2,1,0,3:T(8,128)(2,1)} %bitcast.40), calls=%async_computation.9 | async-start | bytes 1048576 | tf_op jit(solution)/shard_map/all_to_all | solution.py:197
  283.8 4.5 %all-to-all-done.9 = bf16[1,1,1,32,64,128]{5,4,2,1,0,3:T(8,128)(2,1)S(1)} async-done(((bf16[1,1,1,32,64,128]{5,4,2,1,0,3:T(8,128)(2,1)}), bf16[1,1,1,32,64,128]{5,4,2,1,0,3:T(8,128)(2,1)S(1)}, u32[]{:S(2)}, u32[]{:S(2)}) %all-to-all-start.9) | async-done | bytes 524320 | tf_op jit(solution)/shard_map/all_to_all | solution.py:197
  289.2 2.8 collective-permute-start.3
  295.2 2.9 collective-permute-done.3
  (99 shorter events, 41.9 us)
Async XLA Ops:
  0.6 128.7 %copy-start = (bf16[1,32,1,1,128,128]{5,4,3,2,1,0:T(8,128)(2,1)S(1)}, bf16[1,32,1,1,128,128]{5,4,3,2,1,0:T(8,128)(2,1)}, u32[]{:S(2)}) copy-start(bf16[1,32,1,1,128,128]{5,4,3,2,1,0:T(8,128)(2,1)} %param.7) | copy-start | bytes 3145732
  1.7 19.2 %collective-permute-start.1 = (bf16[1,63,1024]{2,1,0:T(8,128)(2,1)S(1)}, bf16[1,63,1024]{2,1,0:T(8,128)(2,1)S(1)}, u32[]{:S(2)}, u32[]{:S(2)}) collective-permute-start(bf16[1,63,1024]{2,1,0:T(8,128)(2,1)S(1)} %slice.97), channel_id=1, source_target_pairs={{16,0},{32,16},{48,32},{64,48},{80,64},{96,80},{112,96},{128,112},... | collective-permute-start | bytes 387080 | tf_op jit(solution)/shard_map/ppermute | solution.py:17
  13.9 6.9 %collective-permute-start = (bf16[1,63,1024]{2,1,0:T(8,128)(2,1)S(1)}, bf16[1,63,1024]{2,1,0:T(8,128)(2,1)S(1)}, u32[]{:S(2)}, u32[]{:S(2)}) collective-permute-start(bf16[1,63,1024]{2,1,0:T(8,128)(2,1)S(1)} %slice.93), channel_id=1, source_target_pairs={{16,0},{32,16},{48,32},{64,48},{80,64},{96,80},{112,96},{128,112},... | collective-permute-start | bytes 387080 | tf_op jit(solution)/shard_map/ppermute | solution.py:17
  16.8 4.5 %copy-start.11 = (f32[64]{0:T(128)}, f32[64]{0:T(128)S(1)}, u32[]{:S(2)}) copy-start(f32[64]{0:T(128)S(1)} %multiply_power_fusion) | copy-start | bytes 772
  39.7 9.3 %copy-start.12 = (s32[1,64,2]{1,2,0:T(2,128)S(1)}, s32[1,64,2]{1,2,0:T(2,128)}, u32[]{:S(2)}) copy-start(s32[1,64,2]{1,2,0:T(2,128)} %param.9) | copy-start | bytes 1540
  39.7 11.8 %copy-start.5 = (bf16[1,32,1,1,128,128]{5,4,3,2,1,0:T(8,128)(2,1)S(1)}, bf16[1,32,1,1,128,128]{5,4,3,2,1,0:T(8,128)(2,1)}, u32[]{:S(2)}) copy-start(bf16[1,32,1,1,128,128]{5,4,3,2,1,0:T(8,128)(2,1)} %param.6) | copy-start | bytes 3145732
  40.8 57.3 %all-to-all-start.1 = ((bf16[2,1,1,32,64,128]{5,4,2,1,0,3:T(8,128)(2,1)}), bf16[2,1,1,32,64,128]{5,4,2,1,0,3:T(8,128)(2,1)S(1)}, u32[]{:S(2)}, u32[]{:S(2)}) async-start(bf16[2,1,1,32,64,128]{5,4,2,1,0,3:T(8,128)(2,1)} %pad_maximum_fusion.1), calls=%async_computation.1 | async-start | bytes 2097152 | tf_op jit(solution)/shard_map/all_to_all | solution.py:23
  101.3 0.6 copy-start.10
  125.5 9.2 %all-to-all-start.3 = ((f32[4,1,512]{2,1,0:T(1,128)}), f32[4,1,512]{2,1,0:T(1,128)}, u32[]{:S(2)}, u32[]{:S(2)}) async-start(f32[4,1,512]{2,1,0:T(1,128)} %reshape.409), calls=%async_computation.3 | async-start | bytes 16384 | tf_op jit(solution)/shard_map/all_to_all | solution.py:163
  134.7 54.6 %all-to-all-start.4 = ((f32[1,32,1,1,64,128]{5,4,3,2,0,1:T(8,128)}), f32[1,32,1,1,64,128]{5,4,3,2,0,1:T(8,128)}, u32[]{:S(2)}, u32[]{:S(2)}) async-start(f32[1,32,1,1,64,128]{5,4,3,2,0,1:T(8,128)} %fusion.7), calls=%async_computation.4 | async-start | bytes 2097152 | tf_op jit(solution)/shard_map/all_to_all | solution.py:151
  189.3 15.2 %all-to-all-start.5 = ((f32[1,1,1,32,64,128]{5,4,2,1,0,3:T(8,128)}), f32[1,1,1,32,64,128]{5,4,2,1,0,3:T(8,128)}, u32[]{:S(2)}, u32[]{:S(2)}) async-start(f32[1,1,1,32,64,128]{5,4,2,1,0,3:T(8,128)} %bitcast.24), calls=%async_computation.5 | async-start | bytes 2097152 | tf_op jit(solution)/shard_map/all_to_all | solution.py:150
  195.0 0.6 copy-start.9
  206.1 0.7 copy-start.6
  239.9 1.9 copy-start.1
  239.9 1.9 copy-start.2
  240.9 0.8 copy-start.3
  241.7 7.3 %copy-start.7 = (bf16[2,8,64,128]{3,2,1,0:T(8,128)(2,1)S(1)}, bf16[2,8,64,128]{3,2,1,0:T(8,128)(2,1)}, u32[]{:S(2)}) copy-start(bf16[2,8,64,128]{3,2,1,0:T(8,128)(2,1)} %copy-done.6) | copy-start | bytes 786436
  243.3 33.4 %all-to-all-start.8 = ((bf16[1,32,1,1,64,128]{5,4,3,2,0,1:T(8,128)(2,1)}), bf16[1,32,1,1,64,128]{5,4,3,2,0,1:T(8,128)(2,1)}, u32[]{:S(2)}, u32[]{:S(2)}) async-start(bf16[1,32,1,1,64,128]{5,4,3,2,0,1:T(8,128)(2,1)} %fusion.10), calls=%async_computation.8 | async-start | bytes 1048576 | tf_op jit(solution)/shard_map/all_to_all | solution.py:198
  250.0 43.6 %collective-permute-start.2 = (bf16[63,1024]{1,0:T(8,128)(2,1)}, bf16[63,1024]{1,0:T(8,128)(2,1)}, u32[]{:S(2)}, u32[]{:S(2)}) collective-permute-start(bf16[63,1024]{1,0:T(8,128)(2,1)} %slice.127), channel_id=1, source_target_pairs={{0,16},{16,32},{32,48},{48,64},{64,80},{80,96},{96,112},{112,128},... | collective-permute-start | bytes 387080 | tf_op jit(solution)/shard_map/ppermute | solution.py:17
  276.7 5.3 %copy-start.8 = (f32[128,64]{1,0:T(8,128)S(1)}, f32[128,64]{1,0:T(8,128)}, u32[]{:S(2)}) copy-start(f32[128,64]{1,0:T(8,128)} %get-tuple-element.34) | copy-start | bytes 98308
  276.7 11.7 %all-to-all-start.9 = ((bf16[1,1,1,32,64,128]{5,4,2,1,0,3:T(8,128)(2,1)}), bf16[1,1,1,32,64,128]{5,4,2,1,0,3:T(8,128)(2,1)S(1)}, u32[]{:S(2)}, u32[]{:S(2)}) async-start(bf16[1,1,1,32,64,128]{5,4,2,1,0,3:T(8,128)(2,1)} %bitcast.40), calls=%async_computation.9 | async-start | bytes 1048576 | tf_op jit(solution)/shard_map/all_to_all | solution.py:197
  288.5 3.5 %copy-start.4 = (bf16[1,32,1,1,128,64]{5,4,1,3,2,0:T(8,128)(2,1)S(1)}, bf16[1,32,1,1,128,64]{5,4,1,3,2,0:T(8,128)(2,1)}, u32[]{:S(2)}) copy-start(bf16[1,32,1,1,128,64]{5,4,1,3,2,0:T(8,128)(2,1)} %get-tuple-element.21) | copy-start | bytes 1572868
  289.2 9.0 %collective-permute-start.3 = (bf16[63,1024]{1,0:T(8,128)(2,1)S(1)}, bf16[63,1024]{1,0:T(8,128)(2,1)S(1)}, u32[]{:S(2)}, u32[]{:S(2)}) collective-permute-start(bf16[63,1024]{1,0:T(8,128)(2,1)S(1)} %slice.136), channel_id=1, source_target_pairs={{0,16},{16,32},{32,48},{48,64},{64,80},{80,96},{96,112},{112,128},... | collective-permute-start | bytes 387080 | tf_op jit(solution)/shard_map/ppermute | solution.py:17
where the time goes:
time: 300 us; the launch traced here: 299 us
  waiting for transfers between devices  132 us (44%)
  blocking collectives  66.7 us (22%)
  starting transfers between devices  52 us (17%)
  other arithmetic  22.9 us (8%)
  local copies, waits for them, and re-layouts  13.3 us (4%)
  matrix products  10.8 us (4%)
    all_to_all x3, blocking collectives, side_by_side(): lax.all_to_all(both, axis, split_axis=split_dim, concat_axis=concat_dim,...  47.6 us
    all_to_all x1, waiting for transfers between devices, shards(): lax.all_to_all(partial_value.reshape(far_shape + (DH,)), 'ctx', split_axi...  45.5 us
    all_to_all x1, waiting for transfers between devices, side_by_side(): lax.all_to_all(both, axis, split_axis=split_dim, concat_axis=concat_dim,...  44.4 us
    all_to_all x1, waiting for transfers between devices, shards(): lax.all_to_all(grad_query.reshape(far_shape + (DH,)), 'ctx', split_axis=1...  21.3 us
    ppermute x4, starting transfers between devices, from_behind(): return lax.ppermute(block, axis, route)  20.4 us
    all_to_all x1, blocking collectives, shards(): lax.all_to_all(log_parts.reshape(far_shape), 'ctx', split_axis=1, concat_...  19.1 us
    all_to_all x1, waiting for transfers between devices, shards(): lax.all_to_all(lax.all_to_all(partial_value.reshape(far_shape + (DH,)), '...  8.32 us
    all_to_all x1, starting transfers between devices, side_by_side(): lax.all_to_all(both, axis, split_axis=split_dim, concat_axis=concat_dim,...  8.22 us
  transfers between devices with their start and end apart: 10, of which 8 were waited for; matrix products, arithmetic and copies ran while one was open for 9% of the time, Pallas kernels for 0%

commit v1 on v0

v1 whole, which is shorter than its diff:
```python
import functools
import math

import jax
import jax.numpy as jnp
import numpy as np
from jax import lax
from jax.experimental import pallas as pl
from jax.experimental.pallas import tpu as pltpu
from jax.sharding import PartitionSpec as P

DH = 128
SPAN = 64
NBR = 2
NEIGH = 128
N_Z = 16
N_CTX = 32
N_TP = 4
HEADS_HERE = 8
SCALE = 1.0 / math.sqrt(DH)
BF = jnp.bfloat16
F32 = jnp.float32
VMEM = pl.BlockSpec(memory_space=pltpu.VMEM)
SMEM = pl.BlockSpec(memory_space=pltpu.SMEM)
LIMIT = 40 * 1024 * 1024


def flat(ctx, tp):
    return ctx * N_TP + tp


def worker(ctx, t1, span):
    return flat(N_Z * t1 + ctx % N_Z, 2 * span + ((ctx // N_Z) ^ t1))


def routes():
    big, tiny = [], []
    for k in range(2):
        big.append([(flat(c, t), worker(c, t // 2, (t % 2) ^ k)) for c in range(N_CTX) for t in range(N_TP)])
        tiny.append([(flat(c, 2 * t1 + k), worker((c + 1) % N_CTX, t1, 1)) for c in range(N_CTX) for t1 in range(2)])
    return big, tiny


def turned_round(pairs):
    return [(b, a) for a, b in pairs]


def z_groups():
    groups = []
    for y in range(2):
        for t in range(N_TP):
            groups.append([flat(N_Z * y + (j ^ (8 * (t // 2))), t) for j in range(N_Z)])
    return groups


def tables(indices):
    freq = 10000.0 ** (-2.0 * np.arange(DH // 2, dtype=np.float64) / DH)
    angles = np.asarray(indices, np.float64)[:, None] * freq[None]
    cos, sin = np.cos(angles), np.sin(angles)
    return (
        np.concatenate([cos, cos], 1).astype(np.float32),
        np.concatenate([-sin, sin], 1).astype(np.float32),
    )


def half_turn(x):
    return pltpu.roll(x, DH // 2, 1)


def dot(a, b, da, db):
    return lax.dot_general(a, b, (((da,), (db,)), ((), ())), preferred_element_type=F32)


def block_of(span, y_half, slot):
    return lax.rem(N_Z * y_half + lax.bitwise_xor(slot, 8 * span) - span + N_CTX, N_CTX)


def pack_kernel(meta, q_ref, g_ref, r0_ref, r1_ref, t_ref):
    t0, ctx = meta[3], meta[4]
    last = lax.broadcasted_iota(jnp.int32, (SPAN, DH), 0) == SPAN - 1
    edges = []
    for h in range(HEADS_HERE):
        for a, ref in enumerate((q_ref, g_ref)):
            low = ref[0:SPAN, h * DH : (h + 1) * DH].astype(F32)
            high = ref[SPAN : 2 * SPAN, h * DH : (h + 1) * DH].astype(F32)
            edges.append(high[SPAN - 1 :])
            even = jnp.where(last, low[SPAN - 1 :], high).astype(BF)
            odd = jnp.where(ctx == 0, 0.0, low).astype(BF)

            @pl.when(t0 == 0)
            def _():
                r0_ref[h, a] = even
                r1_ref[h, a] = odd

            @pl.when(t0 != 0)
            def _():
                r0_ref[h, a] = odd
                r1_ref[h, a] = even

    t_ref[...] = jnp.concatenate(edges, axis=0).astype(BF)


def join_kernel(meta, r0_ref, r1_ref, t0_ref, t1_ref, out_ref):
    odd = meta[0] == 1
    last = jnp.logical_and(lax.broadcasted_iota(jnp.int32, (SPAN, DH), 0) == SPAN - 1, odd)
    for k, (r_ref, t_ref) in enumerate(((r0_ref, t1_ref), (r1_ref, t0_ref))):
        edge = t_ref[...].astype(F32)
        for h in range(HEADS_HERE):
            for a in range(2):
                row = edge[2 * h + a : 2 * h + a + 1]
                out_ref[8 * k + h, a] = jnp.where(last, row, r_ref[h, a].astype(F32)).astype(BF)


def prep_kernel(meta, k_ref, v_ref, cos_ref, sin_ref, kl_ref, vl_ref, send_ref):
    cos, sin = cos_ref[...], sin_ref[...]

    def turn(x):
        x = x.astype(F32)
        return (x * cos + half_turn(x) * sin).astype(BF)

    def step(j, carry):
        mine = block_of(meta[0], meta[1], j)
        theirs = block_of(meta[0], 1 - meta[1], j)
        kl_ref[j] = turn(k_ref[mine])
        vl_ref[j] = v_ref[mine]
        send_ref[0, j] = turn(k_ref[theirs])
        send_ref[1, j] = v_ref[theirs]
        return carry

    lax.fori_loop(0, N_Z, step, 0)


GROUP = 4


def main_kernel(
    meta, len_ref, x_ref, kl_ref, vl_ref, o_ref, qc_ref, qs_ref, kc_ref, ks_ref,
    out_ref, dk_ref, dv_ref, send_ref,
):
    span, y_half, nbr = meta[0], meta[1], meta[2]
    base = pl.program_id(0) * GROUP
    qc, qs = qc_ref[...], qs_ref[...]
    kc, ks = kc_ref[...], ks_ref[...]
    lane = lax.broadcasted_iota(jnp.int32, (SPAN, NEIGH), 1)
    for w in range(GROUP):
        unit = 2 * block_of(span, y_half, base + w) + span
        lens = (len_ref[NBR * unit + nbr], len_ref[NBR * unit + 1 - nbr])
        keys = (kl_ref[w], o_ref[0, w])
        vals = (vl_ref[w], o_ref[1, w])
        q = x_ref[w, 0].astype(F32)
        qw = (q * qc + half_turn(q) * qs).astype(BF)
        g = x_ref[w, 1]
        es, ms, ts, os = [], [], [], []
        for n in range(NBR):
            s = jnp.where(lane < lens[n], dot(qw, keys[n], 1, 1) * SCALE, -jnp.inf)
            m = jnp.max(s, axis=1, keepdims=True)
            e = jnp.exp(s - m)
            es.append(e)
            ms.append(m)
            ts.append(jnp.sum(e, axis=1, keepdims=True))
            os.append(dot(e.astype(BF), vals[n], 1, 0))
        top = jnp.maximum(ms[0], ms[1])
        parts = [jnp.exp(m - top) for m in ms]
        inv = 1.0 / (parts[0] * ts[0] + parts[1] * ts[1])
        ws = [p * inv for p in parts]
        att = (ws[0] * os[0] + ws[1] * os[1]).astype(BF)
        out_ref[w, 0] = att
        dots = jnp.sum(g.astype(F32) * att.astype(F32), axis=1, keepdims=True)
        gq = jnp.zeros((SPAN, DH), F32)
        for n in range(NBR):
            pr = es[n] * ws[n]
            gw = dot(g, vals[n], 1, 1)
            gs = (pr * (gw - dots) * SCALE).astype(BF)
            gq = gq + dot(gs, keys[n], 1, 0).astype(BF).astype(F32)
            dk = dot(gs, qw, 0, 0)
            dk = (dk * kc - half_turn(dk) * ks).astype(BF)
            dv = dot(pr.astype(BF), g, 0, 0).astype(BF)
            if n == 0:
                dk_ref[w] = dk
                dv_ref[w] = dv
            else:
                send_ref[0, w] = dk
                send_ref[1, w] = dv
        out_ref[w, 1] = (gq * qc - half_turn(gq) * qs).astype(BF)


def settle_kernel(meta, dk_ref, dv_ref, got_ref, gk_ref, gv_ref):
    def step(j, carry):
        mine = block_of(meta[0], meta[1], j)
        theirs = block_of(meta[0], 1 - meta[1], j)
        gk_ref[mine] = dk_ref[j]
        gv_ref[mine] = dv_ref[j]
        gk_ref[theirs] = got_ref[0, j]
        gv_ref[theirs] = got_ref[1, j]
        return carry

    lax.fori_loop(0, N_Z, step, 0)


def unpack_kernel(meta, r0_ref, r1_ref, t0_ref, t1_ref, att_ref, gq_ref):
    t0, ctx = meta[3], meta[4]
    last = lax.broadcasted_iota(jnp.int32, (SPAN, DH), 0) == SPAN - 1
    edge = jnp.where(t0 == 0, t1_ref[...].astype(F32), t0_ref[...].astype(F32))
    for h in range(HEADS_HERE):
        for a, ref in enumerate((att_ref, gq_ref)):
            one = r0_ref[h, a].astype(F32)
            two = r1_ref[h, a].astype(F32)
            even = jnp.where(t0 == 0, one, two)
            odd = jnp.where(t0 == 0, two, one)
            odd = jnp.where(ctx == 0, 0.0, odd)
            row = edge[2 * h + a : 2 * h + a + 1]
            ref[0:SPAN, h * DH : (h + 1) * DH] = jnp.where(last, even[SPAN - 1 :], odd).astype(BF)
            ref[SPAN : 2 * SPAN, h * DH : (h + 1) * DH] = jnp.where(last, row, even).astype(BF)


def shaped(*shape):
    return jax.ShapeDtypeStruct(shape, BF)


def call(kernel, outs, n_vmem, flops=1000, moved=1000, **more):
    return pl.pallas_call(
        kernel,
        out_shape=outs,
        in_specs=[SMEM] + [VMEM] * n_vmem,
        out_specs=jax.tree.map(lambda _: VMEM, outs),
        compiler_params=pltpu.CompilerParams(vmem_limit_bytes=LIMIT),
        cost_estimate=pl.CostEstimate(flops=flops, bytes_accessed=moved, transcendentals=0),
        **more,
    )


def shards(queries, keys, values, cotangent, lengths):
    both = ("ctx", "tp")
    ctx, tp = lax.axis_index("ctx"), lax.axis_index("tp")
    span, nbr = tp // 2, tp % 2
    meta = jnp.stack([span, (ctx // N_Z) ^ nbr, nbr, tp % 2, ctx]).astype(jnp.int32)
    big, tiny = routes()
    chunk = shaped(HEADS_HERE, 2, SPAN, DH)
    edge = shaped(2 * HEADS_HERE, DH)
    qc, qs = map(jnp.asarray, tables([*range(1, SPAN), 0]))
    kc, ks = map(jnp.asarray, tables(range(NEIGH)))

    r0, r1, t = call(pack_kernel, (chunk, chunk, edge), 2, moved=1 << 20)(meta, queries[0], cotangent[0])
    r0 = lax.ppermute(r0, both, big[0])
    r1 = lax.ppermute(r1, both, big[1])
    e0 = lax.ppermute(t, both, tiny[0])
    e1 = lax.ppermute(t, both, tiny[1])

    half = shaped(N_Z, NEIGH, DH)
    pair = shaped(2, N_Z, NEIGH, DH)
    k_mine, v_mine, kv_send = call(prep_kernel, (half, half, pair), 4, flops=1 << 24, moved=4 << 20)(
        meta, keys.reshape(N_CTX, NEIGH, DH), values.reshape(N_CTX, NEIGH, DH), kc, ks
    )
    joined = call(join_kernel, shaped(2 * HEADS_HERE, 2, SPAN, DH), 4, moved=1 << 20)(meta, r0, r1, e0, e1)
    kv_send, joined = lax.optimization_barrier((kv_send, joined))
    swap = [(i, i ^ 1) for i in range(N_TP)]
    kv_got = lax.ppermute(kv_send, "tp", swap)
    rows = lax.all_to_all(joined, both, 0, 0, axis_index_groups=z_groups(), tiled=True)

    steps = N_Z // GROUP
    by_slot = lambda *tail: pl.BlockSpec((GROUP,) + tail, lambda i, *_: (i,) + (0,) * len(tail))
    paired = pl.BlockSpec((2, GROUP, NEIGH, DH), lambda i, *_: (0, i, 0, 0))
    whole = lambda n: pl.BlockSpec((n, DH), lambda i, *_: (0, 0))
    out, dk, dv, d_send = pl.pallas_call(
        main_kernel,
        out_shape=(shaped(N_Z, 2, SPAN, DH), half, half, pair),
        grid_spec=pltpu.PrefetchScalarGridSpec(
            num_scalar_prefetch=2,
            grid=(steps,),
            in_specs=[
                by_slot(2, SPAN, DH), by_slot(NEIGH, DH), by_slot(NEIGH, DH), paired,
                whole(SPAN), whole(SPAN), whole(NEIGH), whole(NEIGH),
            ],
            out_specs=[by_slot(2, SPAN, DH), by_slot(NEIGH, DH), by_slot(NEIGH, DH), paired],
        ),
        compiler_params=pltpu.CompilerParams(vmem_limit_bytes=LIMIT),
        cost_estimate=pl.CostEstimate(flops=1 << 29, bytes_accessed=6 << 20, transcendentals=1 << 18),
    )(meta, lengths.reshape(-1), rows, k_mine, v_mine, kv_got, qc, qs, kc, ks)

    d_got = lax.ppermute(d_send, "tp", swap)
    back = lax.all_to_all(out, both, 0, 0, axis_index_groups=z_groups(), tiled=True)
    full = shaped(N_CTX, NEIGH, DH)
    gk, gv = call(settle_kernel, (full, full), 3, moved=4 << 20)(meta, dk, dv, d_got)

    r0 = lax.ppermute(back[:HEADS_HERE], both, turned_round(big[0]))
    r1 = lax.ppermute(back[HEADS_HERE:], both, turned_round(big[1]))
    rims = back[:, :, SPAN - 1, :].reshape(2, 2 * HEADS_HERE, DH)
    e1 = lax.ppermute(rims[0], both, turned_round(tiny[1]))
    e0 = lax.ppermute(rims[1], both, turned_round(tiny[0]))
    wide = shaped(2 * SPAN, HEADS_HERE * DH)
    att, gq = call(unpack_kernel, (wide, wide), 4, moved=1 << 20)(meta, r0, r1, e1, e0)
    return att[None], gq[None], gk.reshape(keys.shape), gv.reshape(values.shape)


def solution(mesh):
    in_specs = (
        P("dp", "ctx", "tp"),
        P("dp", None, "tp", "ctx", None, None),
        P("dp", None, "tp", "ctx", None, None),
        P("dp", "ctx", "tp"),
        P("dp", None, None),
    )
    out_specs = (
        P("dp", "ctx", "tp"),
        P("dp", "ctx", "tp"),
        P("dp", None, "tp", "ctx", None, None),
        P("dp", None, "tp", "ctx", None, None),
    )
    return jax.shard_map(shards, mesh=mesh, in_specs=in_specs, out_specs=out_specs, check_vma=False)
```

time: 300 us -> 146 us (0.49)
  the two profiles are of different devices: /device:TPU:8 before, /device:TPU:4 now
where the time goes in v1:
time: 146 us; the launch traced here: 145 us
  starting transfers between devices  61.6 us (42%)
  waiting for transfers between devices  47.6 us (33%)
  Pallas kernels  25.1 us (17%)
  local copies, waits for them, and re-layouts  9.36 us (6%)
    ppermute x1, waiting for transfers between devices, shards(): kv_got = lax.ppermute(kv_send, 'tp', swap)  21.9 us
    all_to_all x1, waiting for transfers between devices, shards(): lax.all_to_all(out, both, 0, 0, axis_index_groups=z_groups(), tiled=True)  18.2 us
    pallas_call x1, Pallas kernels, shards(): pl.pallas_call(main_kernel, out_shape=(shaped(N_Z, 2, SPAN, DH), half, ha...  17.2 us
    all_to_all x1, starting transfers between devices, shards(): lax.all_to_all(joined, both, 0, 0, axis_index_groups=z_groups(), tiled=True)  13.3 us
    all_to_all x1, starting transfers between devices, shards(): lax.all_to_all(out, both, 0, 0, axis_index_groups=z_groups(), tiled=True)  12.2 us
    unnamed x31, local copies, waits for them, and re-layouts  7.28 us
    ppermute x1, starting transfers between devices, shards(): e1 = lax.ppermute(rims[0], both, turned_round(tiny[1]))  5.55 us
    ppermute x1, starting transfers between devices, shards(): kv_got = lax.ppermute(kv_send, 'tp', swap)  5.41 us
  transfers between devices with their start and end apart: 12, of which 5 were waited for; matrix products, arithmetic and copies ran while one was open for 1% of the time, Pallas kernels for 3%

profile of v1, /device:TPU:4, one launch (start us, length us, event | category | flops | bytes accessed | tf_op | source)
XLA Modules:
  0.0 144.7 jit_solution(5690861725286845412)
XLA Ops:
  3.4 3.4 %collective-permute-start = (bf16[8,2,64,128]{3,2,1,0:T(8,128)(2,1)S(1)}, bf16[8,2,64,128]{3,2,1,0:T(8,128)(2,1)S(1)}, u32[]{:S(2)}, u32[]{:S(2)}) collective-permute-start(bf16[8,2,64,128]{3,2,1,0:T(8,128)(2,1)S(1)} %get-tuple-element.21), channel_id=1, source_target_pairs={{0,0},{4,8},{8,260},{12,268},{16,16},{20,24},{24,276},{28,284},{32... | collective-permute-start | bytes 786440 | tf_op jit(solution)/shard_map/ppermute | solution.py:244
  6.9 3.4 %collective-permute-start.1 = (bf16[8,2,64,128]{3,2,1,0:T(8,128)(2,1)S(1)}, bf16[8,2,64,128]{3,2,1,0:T(8,128)(2,1)S(1)}, u32[]{:S(2)}, u32[]{:S(2)}) collective-permute-start(bf16[8,2,64,128]{3,2,1,0:T(8,128)(2,1)S(1)} %get-tuple-element.22), channel_id=1, source_target_pairs={{0,8},{4,0},{8,268},{12,260},{16,24},{20,16},{24,284},{28,276},{32... | collective-permute-start | bytes 786440 | tf_op jit(solution)/shard_map/ppermute | solution.py:245
  10.3 1.3 collective-permute-start.3
  11.6 4.9 %collective-permute-start.2 = (bf16[16,128]{1,0:T(8,128)(2,1)S(1)}, bf16[16,128]{1,0:T(8,128)(2,1)S(1)}, u32[]{:S(2)}, u32[]{:S(2)}) collective-permute-start(bf16[16,128]{1,0:T(8,128)(2,1)S(1)} %get-tuple-element.23), channel_id=1, source_target_pairs={{0,24},{8,284},{16,40},{24,300},{32,56},{40,316},{48,72},{56,332},... | collective-permute-start | bytes 12296 | tf_op jit(solution)/shard_map/ppermute | solution.py:246
  16.6 1.2 copy-done
  17.8 1.2 copy-done.1
  19.0 2.1 %shard_map.120 = (bf16[16,128,128]{2,1,0:T(8,128)(2,1)S(1)}, bf16[16,128,128]{2,1,0:T(8,128)(2,1)S(1)}, bf16[2,16,128,128]{3,2,1,0:T(8,128)(2,1)S(1)}) custom-call(s32[5]{0:T(128)S(1)} %stack.20.meta, bf16[32,128,128]{2,1,0:T(8,128)(2,1)S(1)} %bitcast.18, bf16[32,128,128]{2,1,0:T(8,128)(2,1)S(1)} %bitcast.19, f32[128,128]{1,0:T(8,128)S(1)} %copy-done.6, ...), custom_call_target="tpu_custom_call" | custom-call | flops 16777216 | bytes 4194304 | tf_op jit(solution)/shard_map/pallas_call | solution.py:251
  21.1 1.5 %collective-permute-done.3.t1_ref = bf16[16,128]{1,0:T(8,128)(2,1)S(1)} collective-permute-done((bf16[16,128]{1,0:T(8,128)(2,1)S(1)}, bf16[16,128]{1,0:T(8,128)(2,1)S(1)}, u32[]{:S(2)}, u32[]{:S(2)}) %collective-permute-start.3) | collective-permute-done | bytes 4128 | tf_op jit(solution)/shard_map/ppermute | solution.py:247
  22.6 2.8 %collective-permute-done.2.t0_ref = bf16[16,128]{1,0:T(8,128)(2,1)S(1)} collective-permute-done((bf16[16,128]{1,0:T(8,128)(2,1)S(1)}, bf16[16,128]{1,0:T(8,128)(2,1)S(1)}, u32[]{:S(2)}, u32[]{:S(2)}) %collective-permute-start.2) | collective-permute-done | bytes 4128 | tf_op jit(solution)/shard_map/ppermute | solution.py:246
  25.5 1.4 shard_map.122
  26.9 13.3 %all-to-all-start = ((bf16[16,2,64,128]{3,2,1,0:T(8,128)(2,1)}), bf16[16,2,64,128]{3,2,1,0:T(8,128)(2,1)S(1)}, u32[]{:S(2)}, u32[]{:S(2)}) async-start(bf16[16,2,64,128]{3,2,1,0:T(8,128)(2,1)} %shard_map.122), calls=%async_computation | async-start | bytes 1048576 | tf_op jit(solution)/shard_map/all_to_all | solution.py:258
  40.3 5.4 %collective-permute-start.4 = (bf16[2,16,128,128]{3,2,1,0:T(8,128)(2,1)S(1)}, bf16[2,16,128,128]{3,2,1,0:T(8,128)(2,1)S(1)}, u32[]{:S(2)}, u32[]{:S(2)}) collective-permute-start(bf16[2,16,128,128]{3,2,1,0:T(8,128)(2,1)S(1)} %get-tuple-element.27), channel_id=1, source_target_pairs={{0,4},{4,0},{8,12},{12,8},{1,5},{5,1},{9,13},{13,9},{2,6},{6,2},{1... | collective-permute-start | bytes 3145736 | tf_op jit(solution)/shard_map/ppermute | solution.py:257
  45.9 21.9 %collective-permute-done.4.o_ref = bf16[2,16,128,128]{3,2,1,0:T(8,128)(2,1)S(1)} collective-permute-done((bf16[2,16,128,128]{3,2,1,0:T(8,128)(2,1)S(1)}, bf16[2,16,128,128]{3,2,1,0:T(8,128)(2,1)S(1)}, u32[]{:S(2)}, u32[]{:S(2)}) %collective-permute-start.4) | collective-permute-done | bytes 1048608 | tf_op jit(solution)/shard_map/ppermute | solution.py:257
  68.9 17.2 %shard_map.123 = (bf16[16,2,64,128]{3,2,1,0:T(8,128)(2,1)S(1)}, bf16[16,128,128]{2,1,0:T(8,128)(2,1)S(1)}, bf16[16,128,128]{2,1,0:T(8,128)(2,1)S(1)}, bf16[2,16,128,128]{3,2,1,0:T(8,128)(2,1)S(1)}) custom-call(s32[5]{0:T(128)S(1)} %stack.20.meta, s32[128]{0:T(128)S(1)} %reshape.27.len_ref, bf16[16,2,64,128]{3,2,1,0:T(8,128)(2,1)S(1)} %all-to-all-done.x_ref, ...), custom_call_target="tpu_custom_call" | custom-call | flops 536870912 | bytes 6291456 | tf_op jit(solution)/shard_map/pallas_call | solution.py:264
  87.8 12.2 %all-to-all-start.1 = ((bf16[16,2,64,128]{3,2,1,0:T(8,128)(2,1)}), bf16[16,2,64,128]{3,2,1,0:T(8,128)(2,1)}, u32[]{:S(2)}, u32[]{:S(2)}) async-start(bf16[16,2,64,128]{3,2,1,0:T(8,128)(2,1)} %copy-done.4), calls=%async_computation.1 | async-start | bytes 1048576 | tf_op jit(solution)/shard_map/all_to_all | solution.py:281
  100.0 3.6 %collective-permute-start.9 = (bf16[2,16,128,128]{3,2,1,0:T(8,128)(2,1)S(1)}, bf16[2,16,128,128]{3,2,1,0:T(8,128)(2,1)S(1)}, u32[]{:S(2)}, u32[]{:S(2)}) collective-permute-start(bf16[2,16,128,128]{3,2,1,0:T(8,128)(2,1)S(1)} %copy-done.12), channel_id=1, source_target_pairs={{0,4},{4,0},{8,12},{12,8},{1,5},{5,1},{9,13},{13,9},{2,6},{6,2},{1... | collective-permute-start | bytes 3145736 | tf_op jit(solution)/shard_map/ppermute | solution.py:280
  103.7 18.2 %all-to-all-done.1 = bf16[16,2,64,128]{3,2,1,0:T(8,128)(2,1)} async-done(((bf16[16,2,64,128]{3,2,1,0:T(8,128)(2,1)}), bf16[16,2,64,128]{3,2,1,0:T(8,128)(2,1)}, u32[]{:S(2)}, u32[]{:S(2)}) %all-to-all-start.1) | async-done | bytes 524320 | tf_op jit(solution)/shard_map/all_to_all | solution.py:281
  122.9 2.2 %collective-permute-start.6 = (bf16[8,2,64,128]{3,2,1,0:T(8,128)(2,1)S(1)}, bf16[8,2,64,128]{3,2,1,0:T(8,128)(2,1)S(1)}, u32[]{:S(2)}, u32[]{:S(2)}) collective-permute-start(bf16[8,2,64,128]{3,2,1,0:T(8,128)(2,1)S(1)} %get-tuple-element.46), channel_id=1, source_target_pairs={{8,0},{0,4},{268,8},{260,12},{24,16},{16,20},{284,24},{276,28},{40... | collective-permute-start | bytes 786440 | tf_op jit(solution)/shard_map/ppermute | solution.py:286
  125.1 4.4 %collective-permute-start.5 = (bf16[8,2,64,128]{3,2,1,0:T(8,128)(2,1)S(1)}, bf16[8,2,64,128]{3,2,1,0:T(8,128)(2,1)S(1)}, u32[]{:S(2)}, u32[]{:S(2)}) collective-permute-start(bf16[8,2,64,128]{3,2,1,0:T(8,128)(2,1)S(1)} %get-tuple-element.47), channel_id=1, source_target_pairs={{0,0},{8,4},{260,8},{268,12},{16,16},{24,20},{276,24},{284,28},{32... | collective-permute-start | bytes 786440 | tf_op jit(solution)/shard_map/ppermute | solution.py:285
  130.3 5.5 %collective-permute-start.7 = (bf16[16,128]{1,0:T(8,128)(2,1)S(1)}, bf16[16,128]{1,0:T(8,128)(2,1)S(1)}, u32[]{:S(2)}, u32[]{:S(2)}) collective-permute-start(bf16[16,128]{1,0:T(8,128)(2,1)S(1)} %bitcast.23), channel_id=1, source_target_pairs={{24,4},{284,12},{40,20},{300,28},{56,36},{316,44},{72,52},{332,60}... | collective-permute-start | bytes 12296 | tf_op jit(solution)/shard_map/ppermute | solution.py:288
  135.9 1.9 %collective-permute-start.8 = (bf16[16,128]{1,0:T(8,128)(2,1)S(1)}, bf16[16,128]{1,0:T(8,128)(2,1)S(1)}, u32[]{:S(2)}, u32[]{:S(2)}) collective-permute-start(bf16[16,128]{1,0:T(8,128)(2,1)S(1)} %bitcast.22), channel_id=1, source_target_pairs={{24,0},{284,8},{40,16},{300,24},{56,32},{316,40},{72,48},{332,56},... | collective-permute-start | bytes 12296 | tf_op jit(solution)/shard_map/ppermute | solution.py:289
  137.8 2.2 %shard_map.125 = (bf16[32,128,128]{2,1,0:T(8,128)(2,1)}, bf16[32,128,128]{2,1,0:T(8,128)(2,1)}) custom-call(s32[5]{0:T(128)S(1)} %stack.20.meta, bf16[16,128,128]{2,1,0:T(8,128)(2,1)S(1)} %get-tuple-element.31.dk_ref, bf16[16,128,128]{2,1,0:T(8,128)(2,1)S(1)} %get-tuple-element.32.dv_ref, bf16[2,16,128,128]{3,2,1,0:T(8,128)(2,1)S(1)} %collective-permute-done.9.got_ref), custom_call_target="tpu_custom_call" | custom-call | flops 1000 | bytes 4194304 | tf_op jit(solution)/shard_map/pallas_call | solution.py:283
  140.0 3.2 %collective-permute-done.8.t1_ref = bf16[16,128]{1,0:T(8,128)(2,1)S(1)} collective-permute-done((bf16[16,128]{1,0:T(8,128)(2,1)S(1)}, bf16[16,128]{1,0:T(8,128)(2,1)S(1)}, u32[]{:S(2)}, u32[]{:S(2)}) %collective-permute-start.8) | collective-permute-done | bytes 4128 | tf_op jit(solution)/shard_map/ppermute | solution.py:289
  143.2 1.5 %shard_map.124 = (bf16[128,1024]{1,0:T(8,128)(2,1)}, bf16[128,1024]{1,0:T(8,128)(2,1)}) custom-call(s32[5]{0:T(128)S(1)} %stack.20.meta, bf16[8,2,64,128]{3,2,1,0:T(8,128)(2,1)S(1)} %collective-permute-done.5.r0_ref, bf16[8,2,64,128]{3,2,1,0:T(8,128)(2,1)S(1)} %collective-permute-done.6.r1_ref, bf16[16,128]{1,0:T(8,128)(2,1)S(1)} %collective-permute-done.7.t0_ref, ...), custom_call_target="tpu_custom_call" | custom-call | flops 1000 | bytes 1048576 | tf_op jit(solution)/shard_map/pallas_call | solution.py:291
  (41 shorter events, 7.7 us)
Async XLA Ops:
  0.7 1.0 copy-start.7
  2.6 13.9 %copy-start.5 = (f32[128,128]{1,0:T(8,128)S(1)}, f32[128,128]{1,0:T(8,128)}, u32[]{:S(2)}) copy-start(f32[128,128]{1,0:T(8,128)} %constant.59.clone.sin_ref.ks_ref) | copy-start | bytes 196612
  2.6 13.9 %copy-start.6 = (f32[128,128]{1,0:T(8,128)S(1)}, f32[128,128]{1,0:T(8,128)}, u32[]{:S(2)}) copy-start(f32[128,128]{1,0:T(8,128)} %constant.58.clone.cos_ref.kc_ref) | copy-start | bytes 196612
  3.4 22.0 %collective-permute-start = (bf16[8,2,64,128]{3,2,1,0:T(8,128)(2,1)S(1)}, bf16[8,2,64,128]{3,2,1,0:T(8,128)(2,1)S(1)}, u32[]{:S(2)}, u32[]{:S(2)}) collective-permute-start(bf16[8,2,64,128]{3,2,1,0:T(8,128)(2,1)S(1)} %get-tuple-element.21), channel_id=1, source_target_pairs={{0,0},{4,8},{8,260},{12,268},{16,16},{20,24},{24,276},{28,284},{32... | collective-permute-start | bytes 786440 | tf_op jit(solution)/shard_map/ppermute | solution.py:244
  6.9 18.6 %collective-permute-start.1 = (bf16[8,2,64,128]{3,2,1,0:T(8,128)(2,1)S(1)}, bf16[8,2,64,128]{3,2,1,0:T(8,128)(2,1)S(1)}, u32[]{:S(2)}, u32[]{:S(2)}) collective-permute-start(bf16[8,2,64,128]{3,2,1,0:T(8,128)(2,1)S(1)} %get-tuple-element.22), channel_id=1, source_target_pairs={{0,8},{4,0},{8,268},{12,260},{16,24},{20,16},{24,284},{28,276},{32... | collective-permute-start | bytes 786440 | tf_op jit(solution)/shard_map/ppermute | solution.py:245
  10.3 12.3 %collective-permute-start.3 = (bf16[16,128]{1,0:T(8,128)(2,1)S(1)}, bf16[16,128]{1,0:T(8,128)(2,1)S(1)}, u32[]{:S(2)}, u32[]{:S(2)}) collective-permute-start(bf16[16,128]{1,0:T(8,128)(2,1)S(1)} %get-tuple-element.23), channel_id=1, source_target_pairs={{4,24},{12,284},{20,40},{28,300},{36,56},{44,316},{52,72},{60,332}... | collective-permute-start | bytes 12296 | tf_op jit(solution)/shard_map/ppermute | solution.py:247
  11.6 13.9 %collective-permute-start.2 = (bf16[16,128]{1,0:T(8,128)(2,1)S(1)}, bf16[16,128]{1,0:T(8,128)(2,1)S(1)}, u32[]{:S(2)}, u32[]{:S(2)}) collective-permute-start(bf16[16,128]{1,0:T(8,128)(2,1)S(1)} %get-tuple-element.23), channel_id=1, source_target_pairs={{0,24},{8,284},{16,40},{24,300},{32,56},{40,316},{48,72},{56,332},... | collective-permute-start | bytes 12296 | tf_op jit(solution)/shard_map/ppermute | solution.py:246
  16.6 1.2 copy-start
  17.8 1.2 copy-start.1
  21.1 5.8 %copy-start.2 = (bf16[16,128,128]{2,1,0:T(8,128)(2,1)}, bf16[16,128,128]{2,1,0:T(8,128)(2,1)S(1)}, u32[]{:S(2)}) copy-start(bf16[16,128,128]{2,1,0:T(8,128)(2,1)S(1)} %get-tuple-element.26.vl_ref) | copy-start | bytes 1572868
  26.9 18.8 %copy-start.13 = (s32[1,64,2]{1,2,0:T(2,128)S(1)}, s32[1,64,2]{1,2,0:T(2,128)}, u32[]{:S(2)}) copy-start(s32[1,64,2]{1,2,0:T(2,128)} %param.13) | copy-start | bytes 1540
  26.9 40.9 %all-to-all-start = ((bf16[16,2,64,128]{3,2,1,0:T(8,128)(2,1)}), bf16[16,2,64,128]{3,2,1,0:T(8,128)(2,1)S(1)}, u32[]{:S(2)}, u32[]{:S(2)}) async-start(bf16[16,2,64,128]{3,2,1,0:T(8,128)(2,1)} %shard_map.122), calls=%async_computation | async-start | bytes 1048576 | tf_op jit(solution)/shard_map/all_to_all | solution.py:258
  40.2 27.6 %copy-start.9 = (f32[64,128]{1,0:T(8,128)S(1)}, f32[64,128]{1,0:T(8,128)}, u32[]{:S(2)}) copy-start(f32[64,128]{1,0:T(8,128)} %constant.57.clone.qs_ref) | copy-start | bytes 98308
  40.2 27.6 %copy-start.10 = (f32[64,128]{1,0:T(8,128)S(1)}, f32[64,128]{1,0:T(8,128)}, u32[]{:S(2)}) copy-start(f32[64,128]{1,0:T(8,128)} %constant.56.clone.qc_ref) | copy-start | bytes 98308
  40.3 27.6 %collective-permute-start.4 = (bf16[2,16,128,128]{3,2,1,0:T(8,128)(2,1)S(1)}, bf16[2,16,128,128]{3,2,1,0:T(8,128)(2,1)S(1)}, u32[]{:S(2)}, u32[]{:S(2)}) collective-permute-start(bf16[2,16,128,128]{3,2,1,0:T(8,128)(2,1)S(1)} %get-tuple-element.27), channel_id=1, source_target_pairs={{0,4},{4,0},{8,12},{12,8},{1,5},{5,1},{9,13},{13,9},{2,6},{6,2},{1... | collective-permute-start | bytes 3145736 | tf_op jit(solution)/shard_map/ppermute | solution.py:257
  67.8 1.0 copy-start.3
  86.9 1.0 copy-start.11
  87.8 12.2 %copy-start.12 = (bf16[2,16,128,128]{3,2,1,0:T(8,128)(2,1)S(1)}, bf16[2,16,128,128]{3,2,1,0:T(8,128)(2,1)}, u32[]{:S(2)}) copy-start(bf16[2,16,128,128]{3,2,1,0:T(8,128)(2,1)} %copy-done.11) | copy-start | bytes 3145732
  87.8 34.0 %all-to-all-start.1 = ((bf16[16,2,64,128]{3,2,1,0:T(8,128)(2,1)}), bf16[16,2,64,128]{3,2,1,0:T(8,128)(2,1)}, u32[]{:S(2)}, u32[]{:S(2)}) async-start(bf16[16,2,64,128]{3,2,1,0:T(8,128)(2,1)} %copy-done.4), calls=%async_computation.1 | async-start | bytes 1048576 | tf_op jit(solution)/shard_map/all_to_all | solution.py:281
  100.0 37.8 %collective-permute-start.9 = (bf16[2,16,128,128]{3,2,1,0:T(8,128)(2,1)S(1)}, bf16[2,16,128,128]{3,2,1,0:T(8,128)(2,1)S(1)}, u32[]{:S(2)}, u32[]{:S(2)}) collective-permute-start(bf16[2,16,128,128]{3,2,1,0:T(8,128)(2,1)S(1)} %copy-done.12), channel_id=1, source_target_pairs={{0,4},{4,0},{8,12},{12,8},{1,5},{5,1},{9,13},{13,9},{2,6},{6,2},{1... | collective-permute-start | bytes 3145736 | tf_op jit(solution)/shard_map/ppermute | solution.py:280
  122.9 20.3 %collective-permute-start.6 = (bf16[8,2,64,128]{3,2,1,0:T(8,128)(2,1)S(1)}, bf16[8,2,64,128]{3,2,1,0:T(8,128)(2,1)S(1)}, u32[]{:S(2)}, u32[]{:S(2)}) collective-permute-start(bf16[8,2,64,128]{3,2,1,0:T(8,128)(2,1)S(1)} %get-tuple-element.46), channel_id=1, source_target_pairs={{8,0},{0,4},{268,8},{260,12},{24,16},{16,20},{284,24},{276,28},{40... | collective-permute-start | bytes 786440 | tf_op jit(solution)/shard_map/ppermute | solution.py:286
  125.1 18.0 %collective-permute-start.5 = (bf16[8,2,64,128]{3,2,1,0:T(8,128)(2,1)S(1)}, bf16[8,2,64,128]{3,2,1,0:T(8,128)(2,1)S(1)}, u32[]{:S(2)}, u32[]{:S(2)}) collective-permute-start(bf16[8,2,64,128]{3,2,1,0:T(8,128)(2,1)S(1)} %get-tuple-element.47), channel_id=1, source_target_pairs={{0,0},{8,4},{260,8},{268,12},{16,16},{24,20},{276,24},{284,28},{32... | collective-permute-start | bytes 786440 | tf_op jit(solution)/shard_map/ppermute | solution.py:285
  130.3 9.6 %collective-permute-start.7 = (bf16[16,128]{1,0:T(8,128)(2,1)S(1)}, bf16[16,128]{1,0:T(8,128)(2,1)S(1)}, u32[]{:S(2)}, u32[]{:S(2)}) collective-permute-start(bf16[16,128]{1,0:T(8,128)(2,1)S(1)} %bitcast.23), channel_id=1, source_target_pairs={{24,4},{284,12},{40,20},{300,28},{56,36},{316,44},{72,52},{332,60}... | collective-permute-start | bytes 12296 | tf_op jit(solution)/shard_map/ppermute | solution.py:288
  135.9 7.3 %collective-permute-start.8 = (bf16[16,128]{1,0:T(8,128)(2,1)S(1)}, bf16[16,128]{1,0:T(8,128)(2,1)S(1)}, u32[]{:S(2)}, u32[]{:S(2)}) collective-permute-start(bf16[16,128]{1,0:T(8,128)(2,1)S(1)} %bitcast.22), channel_id=1, source_target_pairs={{24,0},{284,8},{40,16},{300,24},{56,32},{316,40},{72,48},{332,56},... | collective-permute-start | bytes 12296 | tf_op jit(solution)/shard_map/ppermute | solution.py:289
  (2 other events, 1.7 us)

commit v2 on v1

v2 whole, which is shorter than its diff:
```python
import functools
import math

import jax
import jax.numpy as jnp
import numpy as np
from jax import lax
from jax.experimental import pallas as pl
from jax.experimental.pallas import tpu as pltpu
from jax.sharding import PartitionSpec as P

DH = 128
SPAN = 64
NBR = 2
NEIGH = 128
N_Z = 16
N_CTX = 32
N_TP = 4
HEADS_HERE = 8
WINDOWS = N_Z + 1
GROUP = 6
SLOTS = 18
SCALE = 1.0 / math.sqrt(DH)
BF = jnp.bfloat16
F32 = jnp.float32
VMEM = pl.BlockSpec(memory_space=pltpu.VMEM)
SMEM = pl.BlockSpec(memory_space=pltpu.SMEM)
HBM = pl.BlockSpec(memory_space=pltpu.HBM)
LIMIT = 12 * 1024 * 1024
TURN_COST = 11 << 30
TURN_BYTES = 2 << 20


def flat(ctx, tp):
    return ctx * N_TP + tp


def worker(ctx, t1, span):
    return flat(N_Z * t1 + ctx % N_Z, 2 * span + ((ctx // N_Z) ^ t1))


def routes():
    return [
        [(flat(c, t), worker(c, t // 2, (t % 2) ^ k)) for c in range(N_CTX) for t in range(N_TP)]
        for k in range(2)
    ]


def turned_round(pairs):
    return [(b, a) for a, b in pairs]


def z_groups():
    groups = []
    for y in range(2):
        for t in range(N_TP):
            groups.append([flat(N_Z * y + (j ^ (8 * (t // 2))), t) for j in range(N_Z)])
    return groups


def tables(indices):
    freq = 10000.0 ** (-2.0 * np.arange(DH // 2, dtype=np.float64) / DH)
    angles = np.asarray(indices, np.float64)[:, None] * freq[None]
    cos, sin = np.cos(angles), np.sin(angles)
    return (
        np.concatenate([cos, cos], 1).astype(np.float32),
        np.concatenate([-sin, sin], 1).astype(np.float32),
    )


def half_turn(x):
    return pltpu.roll(x, DH // 2, 1)


def dot(a, b, da, db):
    return lax.dot_general(a, b, (((da,), (db,)), ((), ())), preferred_element_type=F32)


def block_of(span, y_half, w):
    return jnp.clip(N_Z * y_half - span + w, 0, N_CTX - 1)


def place(z, span):
    return lax.bitwise_xor(z, 8 * span)


def is_last():
    return lax.broadcasted_iota(jnp.int32, (SPAN, DH), 0) == SPAN - 1


def pack_kernel(meta, q_ref, g_ref, r0_ref, r1_ref):
    t0, ctx = meta[3], meta[4]
    last = is_last()
    gone = jnp.logical_and(ctx == 0, jnp.logical_not(last))
    for h in range(HEADS_HERE):
        for a, ref in enumerate((q_ref, g_ref)):
            low = ref[0:SPAN, h * DH : (h + 1) * DH].astype(F32)
            high = ref[SPAN : 2 * SPAN, h * DH : (h + 1) * DH].astype(F32)
            even = jnp.where(last, low, high)
            odd = jnp.where(gone, 0.0, jnp.where(last, high, low))
            r0_ref[h, a] = jnp.where(t0 == 0, even, odd).astype(BF)
            r1_ref[h, a] = jnp.where(t0 == 0, odd, even).astype(BF)


def first_of(span, y_half):
    return jnp.clip(N_Z * y_half - span, 0, N_Z - 1)


def send_kernel(meta, k_ref, v_ref, out_ref, sem):
    blocks = pl.ds(first_of(meta[0], 1 - meta[1]), WINDOWS)
    copies = [pltpu.make_async_copy(ref.at[blocks], out_ref.at[n], sem.at[n]) for n, ref in enumerate((k_ref, v_ref))]
    for copy in copies:
        copy.start()
    for copy in copies:
        copy.wait()


def turn_kernel(meta, k_ref, v_ref, got_ref, cos_ref, sin_ref, out_ref):
    cos, sin = cos_ref[...], sin_ref[...]

    def turn(x):
        x = x.astype(F32)
        return (x * cos + half_turn(x) * sin).astype(BF)

    def step(w, carry):
        block = block_of(meta[0], meta[1], w)
        far = block - first_of(meta[0], meta[1])
        out_ref[w, 0] = turn(k_ref[block])
        out_ref[w, 1] = turn(got_ref[0, far])
        out_ref[w, 2] = v_ref[block]
        out_ref[w, 3] = got_ref[1, far]
        return carry

    lax.fori_loop(0, WINDOWS, step, 0)


def main_kernel(
    meta, len_ref, x_ref, kv_ref, qc_ref, qs_ref, kc_ref, ks_ref,
    out_hbm, local_hbm, send_hbm, out_ref, local_ref, send_ref, done_ref, out_sem, grad_sem,
):
    span, y_half, nbr = meta[0], meta[1], meta[2]
    qc, qs = qc_ref[...], qs_ref[...]
    kc, ks = kc_ref[...], ks_ref[...]
    lane = lax.broadcasted_iota(jnp.int32, (SPAN, NEIGH), 1)
    last = is_last()
    these = range(GROUP)
    each = [(i, n) for i in these for n in range(NBR)]

    def group(step, carry):
        places = [step * GROUP + i for i in these]
        slots = [jnp.minimum(w, WINDOWS - 1) for w in places]
        blocks = [block_of(span, y_half, w) for w in slots]

        def rows(w, a):
            body = jnp.where(w < N_Z, x_ref[place(jnp.minimum(w, N_Z - 1), span), a].astype(F32), 0.0)
            v = w - span
            edge = jnp.logical_and(v >= 0, v < N_Z)
            edge = jnp.where(edge, x_ref[place(jnp.clip(v, 0, N_Z - 1), span), a].astype(F32), 0.0)
            return jnp.where(last, edge, body)

        def live(i, n):
            unit = NBR * (2 * blocks[i] + span)
            return lane < len_ref[unit + (nbr if n == 0 else 1 - nbr)]

        keys = {(i, n): kv_ref[slots[i], n] for i, n in each}
        vals = {(i, n): kv_ref[slots[i], 2 + n] for i, n in each}
        q = [rows(w, 0) for w in places]
        gf = [rows(w, 1) for w in places]
        qw = [(x * qc + half_turn(x) * qs).astype(BF) for x in q]
        g = [x.astype(BF) for x in gf]
        s = {k: dot(qw[k[0]], keys[k], 1, 1) for k in each}
        gv = {k: dot(g[k[0]], vals[k], 1, 1) for k in each}
        s = {k: jnp.where(live(*k), s[k] * SCALE, -jnp.inf) for k in each}
        m = {k: jnp.max(s[k], axis=1, keepdims=True) for k in each}
        e = {k: jnp.exp(s[k] - m[k]) for k in each}
        total = {k: jnp.sum(e[k], axis=1, keepdims=True) for k in each}
        o = {k: dot(e[k].astype(BF), vals[k], 1, 0) for k in each}
        top = [jnp.maximum(m[i, 0], m[i, 1]) for i in these]
        part = {k: jnp.exp(m[k] - top[k[0]]) for k in each}
        inv = [1.0 / (part[i, 0] * total[i, 0] + part[i, 1] * total[i, 1]) for i in these]
        share = {k: part[k] * inv[k[0]] for k in each}
        att = [(share[i, 0] * o[i, 0] + share[i, 1] * o[i, 1]).astype(BF) for i in these]
        dots = [jnp.sum(gf[i] * att[i].astype(F32), axis=1, keepdims=True) for i in these]
        pr = {k: e[k] * share[k] for k in each}
        gs = {k: (pr[k] * (gv[k] - dots[k[0]]) * SCALE).astype(BF) for k in each}
        gq = {k: dot(gs[k], keys[k], 1, 0).astype(BF).astype(F32) for k in each}
        gq = [gq[i, 0] + gq[i, 1] for i in these]
        dk = {k: dot(gs[k], qw[k[0]], 0, 0) for k in each}
        dv = {k: dot(pr[k].astype(BF), g[k[0]], 0, 0).astype(BF) for k in each}
        dk = {k: (dk[k] * kc - half_turn(dk[k]) * ks).astype(BF) for k in each}
        for i, w in enumerate(places):
            done_ref[w, 0] = att[i]
            done_ref[w, 1] = (gq[i] * qc - half_turn(gq[i]) * qs).astype(BF)
            local_ref[w, 0] = dk[i, 0]
            local_ref[w, 1] = dv[i, 0]
            send_ref[w, 0] = dk[i, 1]
            send_ref[w, 1] = dv[i, 1]
        for copy in grads(step):
            copy.start()

        def whole(z, carry):
            for a in range(2):
                mine, edge = done_ref[z, a].astype(F32), done_ref[z + span, a].astype(F32)
                out_ref[z, a] = jnp.where(last, edge, mine).astype(BF)
            rows_out(z).start()
            return carry

        end = jnp.minimum(GROUP * (step + 1) - 1, N_Z)
        lax.fori_loop(jnp.maximum(GROUP * step - 1, 0), end, whole, 0)
        return carry

    def grads(step):
        these_slots = pl.ds(step * GROUP, GROUP)
        return [
            pltpu.make_async_copy(ref.at[these_slots], hbm.at[these_slots], grad_sem.at[step, n])
            for n, (ref, hbm) in enumerate(((local_ref, local_hbm), (send_ref, send_hbm)))
        ]

    def rows_out(z):
        return pltpu.make_async_copy(out_ref.at[z], out_hbm.at[place(z, span)], out_sem.at[z])

    lax.fori_loop(0, SLOTS // GROUP, group, 0)

    def finish(step, carry):
        for copy in grads(step):
            copy.wait()
        return carry

    lax.fori_loop(0, SLOTS // GROUP, finish, 0)

    def finish_rows(z, carry):
        rows_out(z).wait()
        return carry

    lax.fori_loop(0, N_Z, finish_rows, 0)


def settle_kernel(meta, local_ref, got_ref, gk_ref, gv_ref):
    span, y_half = meta[0], meta[1]

    def step(i, carry):
        mine, theirs = N_Z * y_half + i, N_Z * (1 - y_half) + i
        for n, ref in enumerate((gk_ref, gv_ref)):
            ref[mine] = local_ref[i + span, n]
            ref[theirs] = got_ref[i + span, n]
        return carry

    lax.fori_loop(0, N_Z, step, 0, unroll=4)

    @pl.when(span == 1)
    def _():
        mine, theirs = jnp.where(y_half == 0, N_Z, 0), jnp.where(y_half == 0, 0, N_Z)
        for n, ref in enumerate((gk_ref, gv_ref)):
            ref[N_Z - 1] = (local_ref[mine, n].astype(F32) + got_ref[theirs, n].astype(F32)).astype(BF)


def unpack_kernel(meta, r0_ref, r1_ref, att_ref, gq_ref):
    t0, ctx = meta[3], meta[4]
    last = is_last()
    gone = jnp.logical_and(ctx == 0, jnp.logical_not(last))
    for h in range(HEADS_HERE):
        for a, ref in enumerate((att_ref, gq_ref)):
            one = r0_ref[h, a].astype(F32)
            two = r1_ref[h, a].astype(F32)
            even = jnp.where(t0 == 0, one, two)
            odd = jnp.where(gone, 0.0, jnp.where(t0 == 0, two, one))
            ref[0:SPAN, h * DH : (h + 1) * DH] = jnp.where(last, even, odd).astype(BF)
            ref[SPAN : 2 * SPAN, h * DH : (h + 1) * DH] = jnp.where(last, odd, even).astype(BF)


def shaped(*shape):
    return jax.ShapeDtypeStruct(shape, BF)


def in_hbm(*shape):
    return pltpu.HBM(shape, BF)


def call(kernel, outs, n_vmem, flops=1000, moved=1000, **more):
    return pl.pallas_call(
        kernel,
        out_shape=outs,
        in_specs=[SMEM] + [VMEM] * n_vmem,
        out_specs=jax.tree.map(lambda _: VMEM, outs),
        compiler_params=pltpu.CompilerParams(vmem_limit_bytes=LIMIT),
        cost_estimate=pl.CostEstimate(flops=flops, bytes_accessed=moved, transcendentals=0),
        **more,
    )


def shards(queries, keys, values, cotangent, lengths):
    both = ("ctx", "tp")
    ctx, tp = lax.axis_index("ctx"), lax.axis_index("tp")
    span, nbr = tp // 2, tp % 2
    meta = jnp.stack([span, (ctx // N_Z) ^ nbr, nbr, tp % 2, ctx]).astype(jnp.int32)
    routes_out = routes()
    chunk = shaped(HEADS_HERE, 2, SPAN, DH)
    qc, qs = map(jnp.asarray, tables([*range(1, SPAN), 0]))
    kc, ks = map(jnp.asarray, tables(range(NEIGH)))
    swap = [(i, i ^ 1) for i in range(N_TP)]

    r0, r1 = call(pack_kernel, (chunk, chunk), 2, moved=1 << 20)(meta, queries[0], cotangent[0])
    r0, r1, meta_then = lax.optimization_barrier((r0, r1, meta))
    r0 = lax.ppermute(r0, both, routes_out[0])
    r1 = lax.ppermute(r1, both, routes_out[1])

    pair = shaped(2, WINDOWS, NEIGH, DH)
    keys_here, values_here = keys.reshape(N_CTX, NEIGH, DH), values.reshape(N_CTX, NEIGH, DH)
    kv_send = pl.pallas_call(
        send_kernel,
        out_shape=pair,
        in_specs=[SMEM, HBM, HBM],
        out_specs=VMEM,
        scratch_shapes=[pltpu.SemaphoreType.DMA((2,))],
        compiler_params=pltpu.CompilerParams(vmem_limit_bytes=LIMIT),
        cost_estimate=pl.CostEstimate(flops=0, bytes_accessed=2 << 20, transcendentals=0),
    )(meta_then, *(pltpu.with_memory_space_constraint(x, pltpu.HBM) for x in (keys_here, values_here)))
    kv_got = lax.ppermute(kv_send, "tp", swap)
    turned = call(turn_kernel, shaped(WINDOWS, 4, NEIGH, DH), 5, flops=TURN_COST, moved=TURN_BYTES)(
        meta, keys_here, values_here, kv_got, kc, ks
    )
    joined = jnp.concatenate([r0, r1], axis=0)
    rows = lax.all_to_all(joined, both, 0, 0, axis_index_groups=z_groups(), tiled=True)

    grads = shaped(SLOTS, 2, NEIGH, DH)
    row_set = (N_Z, 2, SPAN, DH)
    out, d_local, d_send = pl.pallas_call(
        main_kernel,
        out_shape=(in_hbm(*row_set), in_hbm(*grads.shape), in_hbm(*grads.shape)),
        in_specs=[SMEM, SMEM] + [VMEM] * 6,
        out_specs=(HBM,) * 3,
        scratch_shapes=[
            pltpu.VMEM(row_set, BF),
            pltpu.VMEM(grads.shape, BF),
            pltpu.VMEM(grads.shape, BF),
            pltpu.VMEM((SLOTS, 2, SPAN, DH), BF),
            pltpu.SemaphoreType.DMA((N_Z,)),
            pltpu.SemaphoreType.DMA((SLOTS // GROUP, 2)),
        ],
        compiler_params=pltpu.CompilerParams(vmem_limit_bytes=LIMIT),
        cost_estimate=pl.CostEstimate(flops=1 << 29, bytes_accessed=6 << 20, transcendentals=1 << 18),
    )(meta, lengths.reshape(-1), rows, turned, qc, qs, kc, ks)

    back = lax.all_to_all(out, both, 0, 0, axis_index_groups=z_groups(), tiled=True)
    d_got = lax.ppermute(d_send, "tp", swap)
    full = shaped(N_CTX, NEIGH, DH)
    gk, gv = call(settle_kernel, (full, full), 2, moved=4 << 20)(meta, d_local, d_got)

    r0 = lax.ppermute(back[:HEADS_HERE], both, turned_round(routes_out[0]))
    r1 = lax.ppermute(back[HEADS_HERE:], both, turned_round(routes_out[1]))
    wide = shaped(2 * SPAN, HEADS_HERE * DH)
    att, gq = call(unpack_kernel, (wide, wide), 2, moved=1 << 20)(meta, r0, r1)
    return att[None], gq[None], gk.reshape(keys.shape), gv.reshape(values.shape)


def solution(mesh):
    in_specs = (
        P("dp", "ctx", "tp"),
        P("dp", None, "tp", "ctx", None, None),
        P("dp", None, "tp", "ctx", None, None),
        P("dp", "ctx", "tp"),
        P("dp", None, None),
    )
    out_specs = (
        P("dp", "ctx", "tp"),
        P("dp", "ctx", "tp"),
        P("dp", None, "tp", "ctx", None, None),
        P("dp", None, "tp", "ctx", None, None),
    )
    return jax.shard_map(shards, mesh=mesh, in_specs=in_specs, out_specs=out_specs, check_vma=False)
```

time: 146 us -> 126 us (0.86)
  the two profiles are of different devices: /device:TPU:4 before, /device:TPU:6 now
where the time goes in v2:
time: 126 us
  starting transfers between devices  51.5 us (41%)
  waiting for transfers between devices  51.1 us (41%)
  Pallas kernels  14.4 us (11%)
  local copies, waits for them, and re-layouts  7 us (6%)
    all_to_all x1, waiting for transfers between devices, shards(): lax.all_to_all(out, both, 0, 0, axis_index_groups=z_groups(), tiled=True)  21.6 us
    all_to_all x1, starting transfers between devices, shards(): lax.all_to_all(joined, both, 0, 0, axis_index_groups=z_groups(), tiled=True)  18.9 us
    all_to_all x1, waiting for transfers between devices, shards(): lax.all_to_all(joined, both, 0, 0, axis_index_groups=z_groups(), tiled=True)  16.3 us
    all_to_all x1, starting transfers between devices, shards(): lax.all_to_all(out, both, 0, 0, axis_index_groups=z_groups(), tiled=True)  12.2 us
    unnamed x25, local copies, waits for them, and re-layouts  6.73 us
    pallas_call x1, Pallas kernels, shards(): pl.pallas_call(main_kernel, out_shape=(in_hbm(*row_set), in_hbm(*grads.sh...  6.23 us
    ppermute x1, starting transfers between devices, shards(): r1 = lax.ppermute(r1, both, routes_out[1])  4.76 us
    ppermute x1, starting transfers between devices, shards(): r1 = lax.ppermute(back[HEADS_HERE:], both, turned_round(routes_out[1]))  4.51 us
  transfers between devices with their start and end apart: 8, of which 6 were waited for; matrix products, arithmetic and copies ran while one was open for 1% of the time, Pallas kernels for 5%

profile of v2, /device:TPU:6, one launch (start us, length us, event | category | flops | bytes accessed | tf_op | source)
XLA Modules:
  0.0 125.7 jit_solution(14609046952325092674)
XLA Ops:
  0.7 0.9 copy-done.3
  3.3 3.5 %collective-permute-start = (bf16[8,2,64,128]{3,2,1,0:T(8,128)(2,1)S(1)}, bf16[8,2,64,128]{3,2,1,0:T(8,128)(2,1)S(1)}, u32[]{:S(2)}, u32[]{:S(2)}) collective-permute-start(bf16[8,2,64,128]{3,2,1,0:T(8,128)(2,1)S(1)} %get-tuple-element.18), channel_id=1, source_target_pairs={{0,0},{4,8},{8,260},{12,268},{16,16},{20,24},{24,276},{28,284},{32... | collective-permute-start | bytes 786440 | tf_op jit(solution)/shard_map/ppermute | solution.py:304
  6.8 4.8 %collective-permute-start.1 = (bf16[8,2,64,128]{3,2,1,0:T(8,128)(2,1)S(1)}, bf16[8,2,64,128]{3,2,1,0:T(8,128)(2,1)S(1)}, u32[]{:S(2)}, u32[]{:S(2)}) collective-permute-start(bf16[8,2,64,128]{3,2,1,0:T(8,128)(2,1)S(1)} %get-tuple-element.19), channel_id=1, source_target_pairs={{0,8},{4,0},{8,268},{12,260},{16,24},{20,16},{24,284},{28,276},{32... | collective-permute-start | bytes 786440 | tf_op jit(solution)/shard_map/ppermute | solution.py:305
  11.6 1.8 %shard_map.121 = bf16[2,17,128,128]{3,2,1,0:T(8,128)(2,1)S(1)} custom-call(s32[5]{0:T(128)S(1)} %stack.20.meta, bf16[32,128,128]{2,1,0:T(8,128)(2,1)} %bitcast.16, bf16[32,128,128]{2,1,0:T(8,128)(2,1)} %bitcast.18), custom_call_target="tpu_custom_call" | custom-call | bytes 2097152 | tf_op jit(solution)/shard_map/pallas_call | solution.py:309
  13.4 2.1 %collective-permute-start.2 = (bf16[2,17,128,128]{3,2,1,0:T(8,128)(2,1)S(1)}, bf16[2,17,128,128]{3,2,1,0:T(8,128)(2,1)S(1)}, u32[]{:S(2)}, u32[]{:S(2)}) collective-permute-start(bf16[2,17,128,128]{3,2,1,0:T(8,128)(2,1)S(1)} %shard_map.121), channel_id=1, source_target_pairs={{0,4},{4,0},{8,12},{12,8},{1,5},{5,1},{9,13},{13,9},{2,6},{6,2},{1... | collective-permute-start | bytes 3342344 | tf_op jit(solution)/shard_map/ppermute | solution.py:318
  15.5 2.5 %collective-permute-done = bf16[8,2,64,128]{3,2,1,0:T(8,128)(2,1)S(1)} collective-permute-done((bf16[8,2,64,128]{3,2,1,0:T(8,128)(2,1)S(1)}, bf16[8,2,64,128]{3,2,1,0:T(8,128)(2,1)S(1)}, u32[]{:S(2)}, u32[]{:S(2)}) %collective-permute-start) | collective-permute-done | bytes 262176 | tf_op jit(solution)/shard_map/ppermute | solution.py:304
  18.0 3.3 %collective-permute-done.1 = bf16[8,2,64,128]{3,2,1,0:T(8,128)(2,1)S(1)} collective-permute-done((bf16[8,2,64,128]{3,2,1,0:T(8,128)(2,1)S(1)}, bf16[8,2,64,128]{3,2,1,0:T(8,128)(2,1)S(1)}, u32[]{:S(2)}, u32[]{:S(2)}) %collective-permute-start.1) | collective-permute-done | bytes 262176 | tf_op jit(solution)/shard_map/ppermute | solution.py:305
  22.1 18.9 %all-to-all-start = ((bf16[16,2,64,128]{3,2,1,0:T(8,128)(2,1)}), bf16[16,2,64,128]{3,2,1,0:T(8,128)(2,1)S(1)}, u32[]{:S(2)}, u32[]{:S(2)}) async-start(bf16[16,2,64,128]{3,2,1,0:T(8,128)(2,1)} %pad_maximum_fusion), calls=%async_computation | async-start | bytes 1048576 | tf_op jit(solution)/shard_map/all_to_all | solution.py:323
  41.2 1.0 copy-done.9
  42.2 1.2 copy-done.1
  43.5 1.2 copy-done.2
  44.7 1.2 copy-done.10
  45.9 2.2 %shard_map.122.kv_ref = bf16[17,4,128,128]{3,2,1,0:T(8,128)(2,1)S(1)} custom-call(s32[5]{0:T(128)S(1)} %stack.20.meta, bf16[32,128,128]{2,1,0:T(8,128)(2,1)S(1)} %bitcast.17, bf16[32,128,128]{2,1,0:T(8,128)(2,1)S(1)} %bitcast.19, bf16[2,17,128,128]{3,2,1,0:T(8,128)(2,1)S(1)} %copy-done.10, f32[128,128]{1,0:T(8,128)S(1)} %copy-done.6, f32[128,128]{1,0:T(8,128)S(1)} %copy-done.5), custom_call_target="tpu_custom_call" | custom-call | flops 11811160064 | bytes 2097152 | tf_op jit(solution)/shard_map/pallas_call | solution.py:319
  48.2 16.3 %all-to-all-done.x_ref = bf16[16,2,64,128]{3,2,1,0:T(8,128)(2,1)S(1)} async-done(((bf16[16,2,64,128]{3,2,1,0:T(8,128)(2,1)}), bf16[16,2,64,128]{3,2,1,0:T(8,128)(2,1)S(1)}, u32[]{:S(2)}, u32[]{:S(2)}) %all-to-all-start) | async-done | bytes 524320 | tf_op jit(solution)/shard_map/all_to_all | solution.py:323
  64.5 6.2 %shard_map.123 = (bf16[16,2,64,128]{3,2,1,0:T(8,128)(2,1)}, bf16[18,2,128,128]{3,2,1,0:T(8,128)(2,1)}, bf16[18,2,128,128]{3,2,1,0:T(8,128)(2,1)}) custom-call(s32[5]{0:T(128)S(1)} %stack.20.meta, s32[128]{0:T(128)S(1)} %reshape.23.len_ref, bf16[16,2,64,128]{3,2,1,0:T(8,128)(2,1)S(1)} %all-to-all-done.x_ref, bf16[17,4,128,128]{3,2,1,0:T(8,128)(2,1)S(1)} %shard_map.122.kv_ref, ...), custom_call_target="tpu_custom_call" | custom-call | flops 536870912 | bytes 6291456 | tf_op jit(solution)/shard_map/pallas_call | solution.py:327
  70.8 12.2 %all-to-all-start.1 = ((bf16[16,2,64,128]{3,2,1,0:T(8,128)(2,1)}), bf16[16,2,64,128]{3,2,1,0:T(8,128)(2,1)S(1)}, u32[]{:S(2)}, u32[]{:S(2)}) async-start(bf16[16,2,64,128]{3,2,1,0:T(8,128)(2,1)} %get-tuple-element.21), calls=%async_computation.1 | async-start | bytes 1048576 | tf_op jit(solution)/shard_map/all_to_all | solution.py:344
  82.9 1.9 %collective-permute-start.5 = (bf16[18,2,128,128]{3,2,1,0:T(8,128)(2,1)}, bf16[18,2,128,128]{3,2,1,0:T(8,128)(2,1)S(1)}, u32[]{:S(2)}, u32[]{:S(2)}) collective-permute-start(bf16[18,2,128,128]{3,2,1,0:T(8,128)(2,1)} %get-tuple-element.25), channel_id=1, source_target_pairs={{0,4},{4,0},{8,12},{12,8},{1,5},{5,1},{9,13},{13,9},{2,6},{6,2},{1... | collective-permute-start | bytes 3538952 | tf_op jit(solution)/shard_map/ppermute | solution.py:345
  84.9 21.6 %all-to-all-done.1 = bf16[16,2,64,128]{3,2,1,0:T(8,128)(2,1)S(1)} async-done(((bf16[16,2,64,128]{3,2,1,0:T(8,128)(2,1)}), bf16[16,2,64,128]{3,2,1,0:T(8,128)(2,1)S(1)}, u32[]{:S(2)}, u32[]{:S(2)}) %all-to-all-start.1) | async-done | bytes 524320 | tf_op jit(solution)/shard_map/all_to_all | solution.py:344
  106.5 4.5 %collective-permute-start.4 = (bf16[8,2,64,128]{3,2,1,0:T(8,128)(2,1)S(1)}, bf16[8,2,64,128]{3,2,1,0:T(8,128)(2,1)S(1)}, u32[]{:S(2)}, u32[]{:S(2)}) collective-permute-start(bf16[8,2,64,128]{3,2,1,0:T(8,128)(2,1)S(1)} %get-tuple-element.36), channel_id=1, source_target_pairs={{8,0},{0,4},{268,8},{260,12},{24,16},{16,20},{284,24},{276,28},{40... | collective-permute-start | bytes 786440 | tf_op jit(solution)/shard_map/ppermute | solution.py:350
  111.0 3.7 %collective-permute-start.3 = (bf16[8,2,64,128]{3,2,1,0:T(8,128)(2,1)S(1)}, bf16[8,2,64,128]{3,2,1,0:T(8,128)(2,1)S(1)}, u32[]{:S(2)}, u32[]{:S(2)}) collective-permute-start(bf16[8,2,64,128]{3,2,1,0:T(8,128)(2,1)S(1)} %get-tuple-element.37), channel_id=1, source_target_pairs={{0,0},{8,4},{260,8},{268,12},{16,16},{24,20},{276,24},{284,28},{32... | collective-permute-start | bytes 786440 | tf_op jit(solution)/shard_map/ppermute | solution.py:349
  114.8 2.0 %shard_map.125 = (bf16[32,128,128]{2,1,0:T(8,128)(2,1)}, bf16[32,128,128]{2,1,0:T(8,128)(2,1)}) custom-call(s32[5]{0:T(128)S(1)} %stack.20.meta, bf16[18,2,128,128]{3,2,1,0:T(8,128)(2,1)S(1)} %copy-done, bf16[18,2,128,128]{3,2,1,0:T(8,128)(2,1)S(1)} %collective-permute-done.5.got_ref), custom_call_target="tpu_custom_call" | custom-call | flops 1000 | bytes 4194304 | tf_op jit(solution)/shard_map/pallas_call | solution.py:347
  116.8 3.2 %collective-permute-done.4.r1_ref = bf16[8,2,64,128]{3,2,1,0:T(8,128)(2,1)S(1)} collective-permute-done((bf16[8,2,64,128]{3,2,1,0:T(8,128)(2,1)S(1)}, bf16[8,2,64,128]{3,2,1,0:T(8,128)(2,1)S(1)}, u32[]{:S(2)}, u32[]{:S(2)}) %collective-permute-start.4) | collective-permute-done | bytes 262176 | tf_op jit(solution)/shard_map/ppermute | solution.py:350
  120.1 4.1 %collective-permute-done.3.r0_ref = bf16[8,2,64,128]{3,2,1,0:T(8,128)(2,1)S(1)} collective-permute-done((bf16[8,2,64,128]{3,2,1,0:T(8,128)(2,1)S(1)}, bf16[8,2,64,128]{3,2,1,0:T(8,128)(2,1)S(1)}, u32[]{:S(2)}, u32[]{:S(2)}) %collective-permute-start.3) | collective-permute-done | bytes 262176 | tf_op jit(solution)/shard_map/ppermute | solution.py:349
  124.2 1.5 %shard_map.124 = (bf16[128,1024]{1,0:T(8,128)(2,1)}, bf16[128,1024]{1,0:T(8,128)(2,1)}) custom-call(s32[5]{0:T(128)S(1)} %stack.20.meta, bf16[8,2,64,128]{3,2,1,0:T(8,128)(2,1)S(1)} %collective-permute-done.3.r0_ref, bf16[8,2,64,128]{3,2,1,0:T(8,128)(2,1)S(1)} %collective-permute-done.4.r1_ref), custom_call_target="tpu_custom_call" | custom-call | flops 1000 | bytes 1048576 | tf_op jit(solution)/shard_map/pallas_call | solution.py:352
  (27 shorter events, 2.8 us)
Async XLA Ops:
  0.7 1.0 copy-start.3
  1.7 0.9 copy-start.4
  3.3 14.7 %collective-permute-start = (bf16[8,2,64,128]{3,2,1,0:T(8,128)(2,1)S(1)}, bf16[8,2,64,128]{3,2,1,0:T(8,128)(2,1)S(1)}, u32[]{:S(2)}, u32[]{:S(2)}) collective-permute-start(bf16[8,2,64,128]{3,2,1,0:T(8,128)(2,1)S(1)} %get-tuple-element.18), channel_id=1, source_target_pairs={{0,0},{4,8},{8,260},{12,268},{16,16},{20,24},{24,276},{28,284},{32... | collective-permute-start | bytes 786440 | tf_op jit(solution)/shard_map/ppermute | solution.py:304
  6.8 14.5 %collective-permute-start.1 = (bf16[8,2,64,128]{3,2,1,0:T(8,128)(2,1)S(1)}, bf16[8,2,64,128]{3,2,1,0:T(8,128)(2,1)S(1)}, u32[]{:S(2)}, u32[]{:S(2)}) collective-permute-start(bf16[8,2,64,128]{3,2,1,0:T(8,128)(2,1)S(1)} %get-tuple-element.19), channel_id=1, source_target_pairs={{0,8},{4,0},{8,268},{12,260},{16,24},{20,16},{24,284},{28,276},{32... | collective-permute-start | bytes 786440 | tf_op jit(solution)/shard_map/ppermute | solution.py:305
  13.4 27.6 %copy-start.11 = (s32[1,64,2]{1,2,0:T(2,128)S(1)}, s32[1,64,2]{1,2,0:T(2,128)}, u32[]{:S(2)}) copy-start(s32[1,64,2]{1,2,0:T(2,128)} %param.13) | copy-start | bytes 1540
  13.4 28.9 %copy-start.5 = (f32[128,128]{1,0:T(8,128)S(1)}, f32[128,128]{1,0:T(8,128)}, u32[]{:S(2)}) copy-start(f32[128,128]{1,0:T(8,128)} %constant.59.clone.sin_ref.ks_ref) | copy-start | bytes 196612
  13.4 28.8 %copy-start.6 = (f32[128,128]{1,0:T(8,128)S(1)}, f32[128,128]{1,0:T(8,128)}, u32[]{:S(2)}) copy-start(f32[128,128]{1,0:T(8,128)} %constant.58.clone.cos_ref.kc_ref) | copy-start | bytes 196612
  13.4 27.8 %collective-permute-start.2 = (bf16[2,17,128,128]{3,2,1,0:T(8,128)(2,1)S(1)}, bf16[2,17,128,128]{3,2,1,0:T(8,128)(2,1)S(1)}, u32[]{:S(2)}, u32[]{:S(2)}) collective-permute-start(bf16[2,17,128,128]{3,2,1,0:T(8,128)(2,1)S(1)} %shard_map.121), channel_id=1, source_target_pairs={{0,4},{4,0},{8,12},{12,8},{1,5},{5,1},{9,13},{13,9},{2,6},{6,2},{1... | collective-permute-start | bytes 3342344 | tf_op jit(solution)/shard_map/ppermute | solution.py:318
  22.1 42.4 %all-to-all-start = ((bf16[16,2,64,128]{3,2,1,0:T(8,128)(2,1)}), bf16[16,2,64,128]{3,2,1,0:T(8,128)(2,1)S(1)}, u32[]{:S(2)}, u32[]{:S(2)}) async-start(bf16[16,2,64,128]{3,2,1,0:T(8,128)(2,1)} %pad_maximum_fusion), calls=%async_computation | async-start | bytes 1048576 | tf_op jit(solution)/shard_map/all_to_all | solution.py:323
  41.2 1.0 copy-start.9
  42.2 1.2 copy-start.1
  43.5 1.2 copy-start.2
  44.7 1.2 copy-start.10
  45.9 18.6 %copy-start.7 = (f32[64,128]{1,0:T(8,128)S(1)}, f32[64,128]{1,0:T(8,128)}, u32[]{:S(2)}) copy-start(f32[64,128]{1,0:T(8,128)} %constant.57.clone.qs_ref) | copy-start | bytes 98308
  45.9 18.6 %copy-start.8 = (f32[64,128]{1,0:T(8,128)S(1)}, f32[64,128]{1,0:T(8,128)}, u32[]{:S(2)}) copy-start(f32[64,128]{1,0:T(8,128)} %constant.56.clone.qc_ref) | copy-start | bytes 98308
  70.8 44.0 %copy-start = (bf16[18,2,128,128]{3,2,1,0:T(8,128)(2,1)S(1)}, bf16[18,2,128,128]{3,2,1,0:T(8,128)(2,1)}, u32[]{:S(2)}) copy-start(bf16[18,2,128,128]{3,2,1,0:T(8,128)(2,1)} %get-tuple-element.24.local_ref) | copy-start | bytes 3538948
  70.8 35.7 %all-to-all-start.1 = ((bf16[16,2,64,128]{3,2,1,0:T(8,128)(2,1)}), bf16[16,2,64,128]{3,2,1,0:T(8,128)(2,1)S(1)}, u32[]{:S(2)}, u32[]{:S(2)}) async-start(bf16[16,2,64,128]{3,2,1,0:T(8,128)(2,1)} %get-tuple-element.21), calls=%async_computation.1 | async-start | bytes 1048576 | tf_op jit(solution)/shard_map/all_to_all | solution.py:344
  82.9 31.8 %collective-permute-start.5 = (bf16[18,2,128,128]{3,2,1,0:T(8,128)(2,1)}, bf16[18,2,128,128]{3,2,1,0:T(8,128)(2,1)S(1)}, u32[]{:S(2)}, u32[]{:S(2)}) collective-permute-start(bf16[18,2,128,128]{3,2,1,0:T(8,128)(2,1)} %get-tuple-element.25), channel_id=1, source_target_pairs={{0,4},{4,0},{8,12},{12,8},{1,5},{5,1},{9,13},{13,9},{2,6},{6,2},{1... | collective-permute-start | bytes 3538952 | tf_op jit(solution)/shard_map/ppermute | solution.py:345
  106.5 13.5 %collective-permute-start.4 = (bf16[8,2,64,128]{3,2,1,0:T(8,128)(2,1)S(1)}, bf16[8,2,64,128]{3,2,1,0:T(8,128)(2,1)S(1)}, u32[]{:S(2)}, u32[]{:S(2)}) collective-permute-start(bf16[8,2,64,128]{3,2,1,0:T(8,128)(2,1)S(1)} %get-tuple-element.36), channel_id=1, source_target_pairs={{8,0},{0,4},{268,8},{260,12},{24,16},{16,20},{284,24},{276,28},{40... | collective-permute-start | bytes 786440 | tf_op jit(solution)/shard_map/ppermute | solution.py:350
  111.0 13.1 %collective-permute-start.3 = (bf16[8,2,64,128]{3,2,1,0:T(8,128)(2,1)S(1)}, bf16[8,2,64,128]{3,2,1,0:T(8,128)(2,1)S(1)}, u32[]{:S(2)}, u32[]{:S(2)}) collective-permute-start(bf16[8,2,64,128]{3,2,1,0:T(8,128)(2,1)S(1)} %get-tuple-element.37), channel_id=1, source_target_pairs={{0,0},{8,4},{260,8},{268,12},{16,16},{24,20},{276,24},{284,28},{32... | collective-permute-start | bytes 786440 | tf_op jit(solution)/shard_map/ppermute | solution.py:349

commit v3 on v2

--- a/solution.py
+++ b/solution.py
@@ -16,6 +16,7 @@
 N_Z = 16
 N_CTX = 32
 N_TP = 4
+N_DP = 4
 HEADS_HERE = 8
 WINDOWS = N_Z + 1
 GROUP = 6
@@ -106,32 +107,41 @@
     return jnp.clip(N_Z * y_half - span, 0, N_Z - 1)
 
 
-def send_kernel(meta, k_ref, v_ref, out_ref, sem):
+def send_kernel(core, meta, k_ref, v_ref, out_ref, sem):
     blocks = pl.ds(first_of(meta[0], 1 - meta[1]), WINDOWS)
-    copies = [pltpu.make_async_copy(ref.at[blocks], out_ref.at[n], sem.at[n]) for n, ref in enumerate((k_ref, v_ref))]
-    for copy in copies:
-        copy.start()
-    for copy in copies:
-        copy.wait()
-
-
-def turn_kernel(meta, k_ref, v_ref, got_ref, cos_ref, sin_ref, out_ref):
+
+    @pl.when(meta[5] == core)
+    def _():
+        copies = [
+            pltpu.make_async_copy(ref.at[blocks], out_ref.at[n], sem.at[n]) for n, ref in enumerate((k_ref, v_ref))
+        ]
+        for copy in copies:
+            copy.start()
+        for copy in copies:
+            copy.wait()
+
+
+def turn_kernel(meta, k_ref, v_ref, got0_ref, got1_ref, cos_ref, sin_ref, out_ref):
     cos, sin = cos_ref[...], sin_ref[...]
 
     def turn(x):
         x = x.astype(F32)
         return (x * cos + half_turn(x) * sin).astype(BF)
 
-    def step(w, carry):
-        block = block_of(meta[0], meta[1], w)
-        far = block - first_of(meta[0], meta[1])
-        out_ref[w, 0] = turn(k_ref[block])
-        out_ref[w, 1] = turn(got_ref[0, far])
-        out_ref[w, 2] = v_ref[block]
-        out_ref[w, 3] = got_ref[1, far]
-        return carry
-
-    lax.fori_loop(0, WINDOWS, step, 0)
+    for core, got_ref in enumerate((got0_ref, got1_ref)):
+
+        @pl.when(meta[5] == core)
+        def _():
+            def step(w, carry):
+                block = block_of(meta[0], meta[1], w)
+                far = block - first_of(meta[0], meta[1])
+                out_ref[w, 0] = turn(k_ref[block])
+                out_ref[w, 1] = turn(got_ref[0, far])
+                out_ref[w, 2] = v_ref[block]
+                out_ref[w, 3] = got_ref[1, far]
+                return carry
+
+            lax.fori_loop(0, WINDOWS, step, 0)
 
 
 def main_kernel(
@@ -292,7 +302,8 @@
     both = ("ctx", "tp")
     ctx, tp = lax.axis_index("ctx"), lax.axis_index("tp")
     span, nbr = tp // 2, tp % 2
-    meta = jnp.stack([span, (ctx // N_Z) ^ nbr, nbr, tp % 2, ctx]).astype(jnp.int32)
+    core = lax.axis_index("dp") % 2
+    meta = jnp.stack([span, (ctx // N_Z) ^ nbr, nbr, tp % 2, ctx, core]).astype(jnp.int32)
     routes_out = routes()
     chunk = shaped(HEADS_HERE, 2, SPAN, DH)
     qc, qs = map(jnp.asarray, tables([*range(1, SPAN), 0]))
@@ -300,24 +311,29 @@
     swap = [(i, i ^ 1) for i in range(N_TP)]
 
     r0, r1 = call(pack_kernel, (chunk, chunk), 2, moved=1 << 20)(meta, queries[0], cotangent[0])
-    r0, r1, meta_then = lax.optimization_barrier((r0, r1, meta))
+    pair = shaped(2, WINDOWS, NEIGH, DH)
+    keys_here, values_here = keys.reshape(N_CTX, NEIGH, DH), values.reshape(N_CTX, NEIGH, DH)
+
+    def swap_of(which, facts):
+        sent = pl.pallas_call(
+            functools.partial(send_kernel, which),
+            out_shape=pair,
+            in_specs=[SMEM, HBM, HBM],
+            out_specs=VMEM,
+            scratch_shapes=[pltpu.SemaphoreType.DMA((2,))],
+            compiler_params=pltpu.CompilerParams(vmem_limit_bytes=LIMIT),
+            cost_estimate=pl.CostEstimate(flops=0, bytes_accessed=2 << 20, transcendentals=0),
+        )(facts, *(pltpu.with_memory_space_constraint(x, pltpu.HBM) for x in (keys_here, values_here)))
+        pairs = [(N_DP * a + d, N_DP * b + d) for a, b in swap for d in (which, which + 2)]
+        return lax.ppermute(sent, ("tp", "dp"), pairs)
+
+    got1 = swap_of(1, meta)
+    r0, r1, got1, meta_then = lax.optimization_barrier((r0, r1, got1, meta))
     r0 = lax.ppermute(r0, both, routes_out[0])
     r1 = lax.ppermute(r1, both, routes_out[1])
-
-    pair = shaped(2, WINDOWS, NEIGH, DH)
-    keys_here, values_here = keys.reshape(N_CTX, NEIGH, DH), values.reshape(N_CTX, NEIGH, DH)
-    kv_send = pl.pallas_call(
-        send_kernel,
-        out_shape=pair,
-        in_specs=[SMEM, HBM, HBM],
-        out_specs=VMEM,
-        scratch_shapes=[pltpu.SemaphoreType.DMA((2,))],
-        compiler_params=pltpu.CompilerParams(vmem_limit_bytes=LIMIT),
-        cost_estimate=pl.CostEstimate(flops=0, bytes_accessed=2 << 20, transcendentals=0),
-    )(meta_then, *(pltpu.with_memory_space_constraint(x, pltpu.HBM) for x in (keys_here, values_here)))
-    kv_got = lax.ppermute(kv_send, "tp", swap)
-    turned = call(turn_kernel, shaped(WINDOWS, 4, NEIGH, DH), 5, flops=TURN_COST, moved=TURN_BYTES)(
-        meta, keys_here, values_here, kv_got, kc, ks
+    got0 = swap_of(0, meta_then)
+    turned = call(turn_kernel, shaped(WINDOWS, 4, NEIGH, DH), 6, flops=TURN_COST, moved=TURN_BYTES)(
+        meta, keys_here, values_here, got0, got1, kc, ks
     )
     joined = jnp.concatenate([r0, r1], axis=0)
     rows = lax.all_to_all(joined, both, 0, 0, axis_index_groups=z_groups(), tiled=True)

time: 126 us -> 120 us (0.952)
  the two profiles are of different devices: /device:TPU:6 before, /device:TPU:41 now
where the time goes in v3:
time: 120 us
  waiting for transfers between devices  55.8 us (46%)
  starting transfers between devices  40.9 us (34%)
  Pallas kernels  16.6 us (14%)
  local copies, waits for them, and re-layouts  4.68 us (4%)
    ppermute x2, waiting for transfers between devices, swap_of(): return lax.ppermute(sent, ('tp', 'dp'), pairs)  18.1 us
    all_to_all x1, waiting for transfers between devices, shards(): lax.all_to_all(out, both, 0, 0, axis_index_groups=z_groups(), tiled=True)  16.5 us
    all_to_all x1, starting transfers between devices, shards(): lax.all_to_all(joined, both, 0, 0, axis_index_groups=z_groups(), tiled=True)  14.8 us
    all_to_all x1, waiting for transfers between devices, shards(): lax.all_to_all(joined, both, 0, 0, axis_index_groups=z_groups(), tiled=True)  12.7 us
    ppermute x1, starting transfers between devices, shards(): r1 = lax.ppermute(r1, both, routes_out[1])  6.18 us
    pallas_call x1, Pallas kernels, shards(): pl.pallas_call(main_kernel, out_shape=(in_hbm(*row_set), in_hbm(*grads.sh...  6.15 us
    all_to_all x1, starting transfers between devices, shards(): lax.all_to_all(out, both, 0, 0, axis_index_groups=z_groups(), tiled=True)  5.97 us
    ppermute x2, starting transfers between devices, swap_of(): return lax.ppermute(sent, ('tp', 'dp'), pairs)  4.91 us
  transfers between devices with their start and end apart: 9, of which 7 were waited for; matrix products, arithmetic and copies ran while one was open for 1% of the time, Pallas kernels for 6%

profile of v3, /device:TPU:41, one launch (start us, length us, event | category | flops | bytes accessed | tf_op | source)
XLA Modules:
  0.0 119.7 jit_solution(7756123943413190158)
XLA Ops:
  0.8 1.8 %shard_map.121 = bf16[2,17,128,128]{3,2,1,0:T(8,128)(2,1)S(1)} custom-call(s32[6]{0:T(128)S(1)} %stack.24.meta, bf16[32,128,128]{2,1,0:T(8,128)(2,1)} %bitcast.17, bf16[32,128,128]{2,1,0:T(8,128)(2,1)} %bitcast.20), custom_call_target="tpu_custom_call" | custom-call | bytes 2097152 | tf_op jit(solution)/shard_map/pallas_call | solution.py:318
  2.6 3.1 %collective-permute-start = (bf16[2,17,128,128]{3,2,1,0:T(8,128)(2,1)S(1)}, bf16[2,17,128,128]{3,2,1,0:T(8,128)(2,1)S(1)}, u32[]{:S(2)}, u32[]{:S(2)}) collective-permute-start(bf16[2,17,128,128]{3,2,1,0:T(8,128)(2,1)S(1)} %shard_map.121), channel_id=1, source_target_pairs={{1,5},{3,7},{5,1},{7,3},{9,13},{11,15},{13,9},{15,11},{17,21},{19,... | collective-permute-start | bytes 3342344 | tf_op jit(solution)/shard_map/ppermute | solution.py:328
  6.4 18.1 %collective-permute-done.got1_ref = bf16[2,17,128,128]{3,2,1,0:T(8,128)(2,1)S(1)} collective-permute-done((bf16[2,17,128,128]{3,2,1,0:T(8,128)(2,1)S(1)}, bf16[2,17,128,128]{3,2,1,0:T(8,128)(2,1)S(1)}, u32[]{:S(2)}, u32[]{:S(2)}) %collective-permute-start) | collective-permute-done | bytes 1114144 | tf_op jit(solution)/shard_map/ppermute | solution.py:328
  24.4 3.3 %collective-permute-start.1 = (bf16[8,2,64,128]{3,2,1,0:T(8,128)(2,1)S(1)}, bf16[8,2,64,128]{3,2,1,0:T(8,128)(2,1)S(1)}, u32[]{:S(2)}, u32[]{:S(2)}) collective-permute-start(bf16[8,2,64,128]{3,2,1,0:T(8,128)(2,1)S(1)} %get-tuple-element.19), channel_id=1, source_target_pairs={{0,0},{4,8},{8,260},{12,268},{16,16},{20,24},{24,276},{28,284},{32... | collective-permute-start | bytes 786440 | tf_op jit(solution)/shard_map/ppermute | solution.py:332
  27.7 6.2 %collective-permute-start.2 = (bf16[8,2,64,128]{3,2,1,0:T(8,128)(2,1)S(1)}, bf16[8,2,64,128]{3,2,1,0:T(8,128)(2,1)S(1)}, u32[]{:S(2)}, u32[]{:S(2)}) collective-permute-start(bf16[8,2,64,128]{3,2,1,0:T(8,128)(2,1)S(1)} %get-tuple-element.20), channel_id=1, source_target_pairs={{0,8},{4,0},{8,268},{12,260},{16,24},{20,16},{24,284},{28,276},{32... | collective-permute-start | bytes 786440 | tf_op jit(solution)/shard_map/ppermute | solution.py:333
  33.9 1.6 %shard_map.122 = bf16[2,17,128,128]{3,2,1,0:T(8,128)(2,1)} custom-call(s32[6]{0:T(128)S(1)} %stack.24.meta, bf16[32,128,128]{2,1,0:T(8,128)(2,1)} %bitcast.18, bf16[32,128,128]{2,1,0:T(8,128)(2,1)} %bitcast.21), custom_call_target="tpu_custom_call" | custom-call | bytes 2097152 | tf_op jit(solution)/shard_map/pallas_call | solution.py:318
  35.6 1.8 %collective-permute-start.3 = (bf16[2,17,128,128]{3,2,1,0:T(8,128)(2,1)}, bf16[2,17,128,128]{3,2,1,0:T(8,128)(2,1)}, u32[]{:S(2)}, u32[]{:S(2)}) collective-permute-start(bf16[2,17,128,128]{3,2,1,0:T(8,128)(2,1)} %shard_map.122), channel_id=1, source_target_pairs={{0,4},{2,6},{4,0},{6,2},{8,12},{10,14},{12,8},{14,10},{16,20},{18,... | collective-permute-start | bytes 3342344 | tf_op jit(solution)/shard_map/ppermute | solution.py:328
  38.5 1.2 %collective-permute-done.2 = bf16[8,2,64,128]{3,2,1,0:T(8,128)(2,1)S(1)} collective-permute-done((bf16[8,2,64,128]{3,2,1,0:T(8,128)(2,1)S(1)}, bf16[8,2,64,128]{3,2,1,0:T(8,128)(2,1)S(1)}, u32[]{:S(2)}, u32[]{:S(2)}) %collective-permute-start.2) | collective-permute-done | bytes 262176 | tf_op jit(solution)/shard_map/ppermute | solution.py:333
  40.6 14.8 %all-to-all-start = ((bf16[16,2,64,128]{3,2,1,0:T(8,128)(2,1)}), bf16[16,2,64,128]{3,2,1,0:T(8,128)(2,1)S(1)}, u32[]{:S(2)}, u32[]{:S(2)}) async-start(bf16[16,2,64,128]{3,2,1,0:T(8,128)(2,1)} %pad_maximum_fusion), calls=%async_computation | async-start | bytes 1048576 | tf_op jit(solution)/shard_map/all_to_all | solution.py:339
  55.7 1.2 %copy-done.12 = bf16[2,17,128,128]{3,2,1,0:T(8,128)(2,1)S(1)} copy-done((bf16[2,17,128,128]{3,2,1,0:T(8,128)(2,1)S(1)}, bf16[2,17,128,128]{3,2,1,0:T(8,128)(2,1)}, u32[]{:S(2)}) %copy-start.12) | copy-done | bytes 1114136
  56.9 2.9 %shard_map.123.kv_ref = bf16[17,4,128,128]{3,2,1,0:T(8,128)(2,1)S(1)} custom-call(s32[6]{0:T(128)S(1)} %stack.24.meta, bf16[32,128,128]{2,1,0:T(8,128)(2,1)S(1)} %bitcast.19, bf16[32,128,128]{2,1,0:T(8,128)(2,1)S(1)} %bitcast.22, bf16[2,17,128,128]{3,2,1,0:T(8,128)(2,1)} %collective-permute-done.3.got0_ref, bf16[2,17,128,128]{3,2,1,0:T(8,128)(2,1)S(1)} %copy-done.12, ...), custom_call_target="tpu_custom_call" | custom-call | flops 11811160064 | bytes 2097152 | tf_op jit(solution)/shard_map/pallas_call | solution.py:335
  59.9 1.4 %copy-done.2 = bf16[17,4,128,128]{3,2,1,0:T(8,128)(2,1)} copy-done((bf16[17,4,128,128]{3,2,1,0:T(8,128)(2,1)}, bf16[17,4,128,128]{3,2,1,0:T(8,128)(2,1)S(1)}, u32[]{:S(2)}) %copy-start.2) | copy-done | bytes 2228248
  61.3 12.7 %all-to-all-done.x_ref = bf16[16,2,64,128]{3,2,1,0:T(8,128)(2,1)S(1)} async-done(((bf16[16,2,64,128]{3,2,1,0:T(8,128)(2,1)}), bf16[16,2,64,128]{3,2,1,0:T(8,128)(2,1)S(1)}, u32[]{:S(2)}, u32[]{:S(2)}) %all-to-all-start) | async-done | bytes 524320 | tf_op jit(solution)/shard_map/all_to_all | solution.py:339
  74.0 1.6 %copy-done.3 = bf16[17,4,128,128]{3,2,1,0:T(8,128)(2,1)S(1)} copy-done((bf16[17,4,128,128]{3,2,1,0:T(8,128)(2,1)S(1)}, bf16[17,4,128,128]{3,2,1,0:T(8,128)(2,1)}, u32[]{:S(2)}) %copy-start.3) | copy-done | bytes 2228248
  75.6 6.2 %shard_map.124 = (bf16[16,2,64,128]{3,2,1,0:T(8,128)(2,1)}, bf16[18,2,128,128]{3,2,1,0:T(8,128)(2,1)}, bf16[18,2,128,128]{3,2,1,0:T(8,128)(2,1)}) custom-call(s32[6]{0:T(128)S(1)} %stack.24.meta, s32[128]{0:T(128)S(1)} %reshape.23.len_ref, bf16[16,2,64,128]{3,2,1,0:T(8,128)(2,1)S(1)} %all-to-all-done.x_ref, bf16[17,4,128,128]{3,2,1,0:T(8,128)(2,1)S(1)} %copy-done.3, ...), custom_call_target="tpu_custom_call" | custom-call | flops 536870912 | bytes 6291456 | tf_op jit(solution)/shard_map/pallas_call | solution.py:343
  81.8 6.0 %all-to-all-start.1 = ((bf16[16,2,64,128]{3,2,1,0:T(8,128)(2,1)}), bf16[16,2,64,128]{3,2,1,0:T(8,128)(2,1)S(1)}, u32[]{:S(2)}, u32[]{:S(2)}) async-start(bf16[16,2,64,128]{3,2,1,0:T(8,128)(2,1)} %get-tuple-element.23), calls=%async_computation.1 | async-start | bytes 1048576 | tf_op jit(solution)/shard_map/all_to_all | solution.py:360
  87.7 1.9 %collective-permute-start.6 = (bf16[18,2,128,128]{3,2,1,0:T(8,128)(2,1)}, bf16[18,2,128,128]{3,2,1,0:T(8,128)(2,1)S(1)}, u32[]{:S(2)}, u32[]{:S(2)}) collective-permute-start(bf16[18,2,128,128]{3,2,1,0:T(8,128)(2,1)} %get-tuple-element.27), channel_id=1, source_target_pairs={{0,4},{4,0},{8,12},{12,8},{1,5},{5,1},{9,13},{13,9},{2,6},{6,2},{1... | collective-permute-start | bytes 3538952 | tf_op jit(solution)/shard_map/ppermute | solution.py:361
  89.7 16.5 %all-to-all-done.1 = bf16[16,2,64,128]{3,2,1,0:T(8,128)(2,1)S(1)} async-done(((bf16[16,2,64,128]{3,2,1,0:T(8,128)(2,1)}), bf16[16,2,64,128]{3,2,1,0:T(8,128)(2,1)S(1)}, u32[]{:S(2)}, u32[]{:S(2)}) %all-to-all-start.1) | async-done | bytes 524320 | tf_op jit(solution)/shard_map/all_to_all | solution.py:360
  106.2 1.9 %collective-permute-start.5 = (bf16[8,2,64,128]{3,2,1,0:T(8,128)(2,1)S(1)}, bf16[8,2,64,128]{3,2,1,0:T(8,128)(2,1)S(1)}, u32[]{:S(2)}, u32[]{:S(2)}) collective-permute-start(bf16[8,2,64,128]{3,2,1,0:T(8,128)(2,1)S(1)} %get-tuple-element.38), channel_id=1, source_target_pairs={{8,0},{0,4},{268,8},{260,12},{24,16},{16,20},{284,24},{276,28},{40... | collective-permute-start | bytes 786440 | tf_op jit(solution)/shard_map/ppermute | solution.py:366
  108.1 1.9 %collective-permute-start.4 = (bf16[8,2,64,128]{3,2,1,0:T(8,128)(2,1)S(1)}, bf16[8,2,64,128]{3,2,1,0:T(8,128)(2,1)S(1)}, u32[]{:S(2)}, u32[]{:S(2)}) collective-permute-start(bf16[8,2,64,128]{3,2,1,0:T(8,128)(2,1)S(1)} %get-tuple-element.39), channel_id=1, source_target_pairs={{0,0},{8,4},{260,8},{268,12},{16,16},{24,20},{276,24},{284,28},{32... | collective-permute-start | bytes 786440 | tf_op jit(solution)/shard_map/ppermute | solution.py:365
  110.1 2.0 %shard_map.126 = (bf16[32,128,128]{2,1,0:T(8,128)(2,1)}, bf16[32,128,128]{2,1,0:T(8,128)(2,1)}) custom-call(s32[6]{0:T(128)S(1)} %stack.24.meta, bf16[18,2,128,128]{3,2,1,0:T(8,128)(2,1)S(1)} %copy-done.4, bf16[18,2,128,128]{3,2,1,0:T(8,128)(2,1)S(1)} %collective-permute-done.6.got_ref), custom_call_target="tpu_custom_call" | custom-call | flops 1000 | bytes 4194304 | tf_op jit(solution)/shard_map/pallas_call | solution.py:363
  112.1 4.9 %collective-permute-done.5.r1_ref = bf16[8,2,64,128]{3,2,1,0:T(8,128)(2,1)S(1)} collective-permute-done((bf16[8,2,64,128]{3,2,1,0:T(8,128)(2,1)S(1)}, bf16[8,2,64,128]{3,2,1,0:T(8,128)(2,1)S(1)}, u32[]{:S(2)}, u32[]{:S(2)}) %collective-permute-start.5) | collective-permute-done | bytes 262176 | tf_op jit(solution)/shard_map/ppermute | solution.py:366
  117.0 1.3 %collective-permute-done.4.r0_ref = bf16[8,2,64,128]{3,2,1,0:T(8,128)(2,1)S(1)} collective-permute-done((bf16[8,2,64,128]{3,2,1,0:T(8,128)(2,1)S(1)}, bf16[8,2,64,128]{3,2,1,0:T(8,128)(2,1)S(1)}, u32[]{:S(2)}, u32[]{:S(2)}) %collective-permute-start.4) | collective-permute-done | bytes 262176 | tf_op jit(solution)/shard_map/ppermute | solution.py:365
  118.2 1.5 %shard_map.125 = (bf16[128,1024]{1,0:T(8,128)(2,1)}, bf16[128,1024]{1,0:T(8,128)(2,1)}) custom-call(s32[6]{0:T(128)S(1)} %stack.24.meta, bf16[8,2,64,128]{3,2,1,0:T(8,128)(2,1)S(1)} %collective-permute-done.4.r0_ref, bf16[8,2,64,128]{3,2,1,0:T(8,128)(2,1)S(1)} %collective-permute-done.5.r1_ref), custom_call_target="tpu_custom_call" | custom-call | flops 1000 | bytes 1048576 | tf_op jit(solution)/shard_map/pallas_call | solution.py:368
  (34 shorter events, 3.1 us)
Async XLA Ops:
  0.8 4.9 %copy-start.5 = (bf16[1,128,1024]{2,1,0:T(8,128)(2,1)S(1)}, bf16[1,128,1024]{2,1,0:T(8,128)(2,1)}, u32[]{:S(2)}) copy-start(bf16[1,128,1024]{2,1,0:T(8,128)(2,1)} %param.9) | copy-start | bytes 786436
  0.8 4.9 %copy-start.6 = (bf16[1,128,1024]{2,1,0:T(8,128)(2,1)S(1)}, bf16[1,128,1024]{2,1,0:T(8,128)(2,1)}, u32[]{:S(2)}) copy-start(bf16[1,128,1024]{2,1,0:T(8,128)(2,1)} %param.12) | copy-start | bytes 786436
  2.6 21.9 %collective-permute-start = (bf16[2,17,128,128]{3,2,1,0:T(8,128)(2,1)S(1)}, bf16[2,17,128,128]{3,2,1,0:T(8,128)(2,1)S(1)}, u32[]{:S(2)}, u32[]{:S(2)}) collective-permute-start(bf16[2,17,128,128]{3,2,1,0:T(8,128)(2,1)S(1)} %shard_map.121), channel_id=1, source_target_pairs={{1,5},{3,7},{5,1},{7,3},{9,13},{11,15},{13,9},{15,11},{17,21},{19,... | collective-permute-start | bytes 3342344 | tf_op jit(solution)/shard_map/ppermute | solution.py:328
  24.4 11.1 %copy-start.11 = (bf16[2,17,128,128]{3,2,1,0:T(8,128)(2,1)}, bf16[2,17,128,128]{3,2,1,0:T(8,128)(2,1)S(1)}, u32[]{:S(2)}) copy-start(bf16[2,17,128,128]{3,2,1,0:T(8,128)(2,1)S(1)} %collective-permute-done.got1_ref) | copy-start | bytes 3342340
  24.4 14.1 %collective-permute-start.1 = (bf16[8,2,64,128]{3,2,1,0:T(8,128)(2,1)S(1)}, bf16[8,2,64,128]{3,2,1,0:T(8,128)(2,1)S(1)}, u32[]{:S(2)}, u32[]{:S(2)}) collective-permute-start(bf16[8,2,64,128]{3,2,1,0:T(8,128)(2,1)S(1)} %get-tuple-element.19), channel_id=1, source_target_pairs={{0,0},{4,8},{8,260},{12,268},{16,16},{20,24},{24,276},{28,284},{32... | collective-permute-start | bytes 786440 | tf_op jit(solution)/shard_map/ppermute | solution.py:332
  27.7 12.0 %collective-permute-start.2 = (bf16[8,2,64,128]{3,2,1,0:T(8,128)(2,1)S(1)}, bf16[8,2,64,128]{3,2,1,0:T(8,128)(2,1)S(1)}, u32[]{:S(2)}, u32[]{:S(2)}) collective-permute-start(bf16[8,2,64,128]{3,2,1,0:T(8,128)(2,1)S(1)} %get-tuple-element.20), channel_id=1, source_target_pairs={{0,8},{4,0},{8,268},{12,260},{16,24},{20,16},{24,284},{28,276},{32... | collective-permute-start | bytes 786440 | tf_op jit(solution)/shard_map/ppermute | solution.py:333
  33.9 21.5 %copy-start.13 = (s32[1,64,2]{1,2,0:T(2,128)S(1)}, s32[1,64,2]{1,2,0:T(2,128)}, u32[]{:S(2)}) copy-start(s32[1,64,2]{1,2,0:T(2,128)} %param.13) | copy-start | bytes 1540
  33.9 21.7 %copy-start.8 = (f32[128,128]{1,0:T(8,128)S(1)}, f32[128,128]{1,0:T(8,128)}, u32[]{:S(2)}) copy-start(f32[128,128]{1,0:T(8,128)} %constant.64.clone.cos_ref.kc_ref) | copy-start | bytes 196612
  35.5 20.1 %copy-start = (bf16[1,32,1,1,128,128]{5,4,3,2,1,0:T(8,128)(2,1)S(1)}, bf16[1,32,1,1,128,128]{5,4,3,2,1,0:T(8,128)(2,1)}, u32[]{:S(2)}) copy-start(bf16[1,32,1,1,128,128]{5,4,3,2,1,0:T(8,128)(2,1)} %param.10) | copy-start | bytes 3145732
  35.5 20.1 %copy-start.1 = (bf16[1,32,1,1,128,128]{5,4,3,2,1,0:T(8,128)(2,1)S(1)}, bf16[1,32,1,1,128,128]{5,4,3,2,1,0:T(8,128)(2,1)}, u32[]{:S(2)}) copy-start(bf16[1,32,1,1,128,128]{5,4,3,2,1,0:T(8,128)(2,1)} %param.11) | copy-start | bytes 3145732
  35.5 20.1 %copy-start.7 = (f32[128,128]{1,0:T(8,128)S(1)}, f32[128,128]{1,0:T(8,128)}, u32[]{:S(2)}) copy-start(f32[128,128]{1,0:T(8,128)} %constant.65.clone.sin_ref.ks_ref) | copy-start | bytes 196612
  35.6 20.1 %collective-permute-start.3 = (bf16[2,17,128,128]{3,2,1,0:T(8,128)(2,1)}, bf16[2,17,128,128]{3,2,1,0:T(8,128)(2,1)}, u32[]{:S(2)}, u32[]{:S(2)}) collective-permute-start(bf16[2,17,128,128]{3,2,1,0:T(8,128)(2,1)} %shard_map.122), channel_id=1, source_target_pairs={{0,4},{2,6},{4,0},{6,2},{8,12},{10,14},{12,8},{14,10},{16,20},{18,... | collective-permute-start | bytes 3342344 | tf_op jit(solution)/shard_map/ppermute | solution.py:328
  40.6 33.4 %all-to-all-start = ((bf16[16,2,64,128]{3,2,1,0:T(8,128)(2,1)}), bf16[16,2,64,128]{3,2,1,0:T(8,128)(2,1)S(1)}, u32[]{:S(2)}, u32[]{:S(2)}) async-start(bf16[16,2,64,128]{3,2,1,0:T(8,128)(2,1)} %pad_maximum_fusion), calls=%async_computation | async-start | bytes 1048576 | tf_op jit(solution)/shard_map/all_to_all | solution.py:339
  55.6 18.4 %copy-start.9 = (f32[64,128]{1,0:T(8,128)S(1)}, f32[64,128]{1,0:T(8,128)}, u32[]{:S(2)}) copy-start(f32[64,128]{1,0:T(8,128)} %constant.63.clone.qs_ref) | copy-start | bytes 98308
  55.6 18.4 %copy-start.10 = (f32[64,128]{1,0:T(8,128)S(1)}, f32[64,128]{1,0:T(8,128)}, u32[]{:S(2)}) copy-start(f32[64,128]{1,0:T(8,128)} %constant.62.clone.qc_ref) | copy-start | bytes 98308
  55.7 1.2 %copy-start.12 = (bf16[2,17,128,128]{3,2,1,0:T(8,128)(2,1)S(1)}, bf16[2,17,128,128]{3,2,1,0:T(8,128)(2,1)}, u32[]{:S(2)}) copy-start(bf16[2,17,128,128]{3,2,1,0:T(8,128)(2,1)} %copy-done.11) | copy-start | bytes 3342340
  59.9 1.4 %copy-start.2 = (bf16[17,4,128,128]{3,2,1,0:T(8,128)(2,1)}, bf16[17,4,128,128]{3,2,1,0:T(8,128)(2,1)S(1)}, u32[]{:S(2)}) copy-start(bf16[17,4,128,128]{3,2,1,0:T(8,128)(2,1)S(1)} %shard_map.123.kv_ref) | copy-start | bytes 6684676
  74.0 1.6 %copy-start.3 = (bf16[17,4,128,128]{3,2,1,0:T(8,128)(2,1)S(1)}, bf16[17,4,128,128]{3,2,1,0:T(8,128)(2,1)}, u32[]{:S(2)}) copy-start(bf16[17,4,128,128]{3,2,1,0:T(8,128)(2,1)} %copy-done.2) | copy-start | bytes 6684676
  81.8 28.3 %copy-start.4 = (bf16[18,2,128,128]{3,2,1,0:T(8,128)(2,1)S(1)}, bf16[18,2,128,128]{3,2,1,0:T(8,128)(2,1)}, u32[]{:S(2)}) copy-start(bf16[18,2,128,128]{3,2,1,0:T(8,128)(2,1)} %get-tuple-element.26.local_ref) | copy-start | bytes 3538948
  81.8 24.4 %all-to-all-start.1 = ((bf16[16,2,64,128]{3,2,1,0:T(8,128)(2,1)}), bf16[16,2,64,128]{3,2,1,0:T(8,128)(2,1)S(1)}, u32[]{:S(2)}, u32[]{:S(2)}) async-start(bf16[16,2,64,128]{3,2,1,0:T(8,128)(2,1)} %get-tuple-element.23), calls=%async_computation.1 | async-start | bytes 1048576 | tf_op jit(solution)/shard_map/all_to_all | solution.py:360
  87.7 22.3 %collective-permute-start.6 = (bf16[18,2,128,128]{3,2,1,0:T(8,128)(2,1)}, bf16[18,2,128,128]{3,2,1,0:T(8,128)(2,1)S(1)}, u32[]{:S(2)}, u32[]{:S(2)}) collective-permute-start(bf16[18,2,128,128]{3,2,1,0:T(8,128)(2,1)} %get-tuple-element.27), channel_id=1, source_target_pairs={{0,4},{4,0},{8,12},{12,8},{1,5},{5,1},{9,13},{13,9},{2,6},{6,2},{1... | collective-permute-start | bytes 3538952 | tf_op jit(solution)/shard_map/ppermute | solution.py:361
  106.2 10.8 %collective-permute-start.5 = (bf16[8,2,64,128]{3,2,1,0:T(8,128)(2,1)S(1)}, bf16[8,2,64,128]{3,2,1,0:T(8,128)(2,1)S(1)}, u32[]{:S(2)}, u32[]{:S(2)}) collective-permute-start(bf16[8,2,64,128]{3,2,1,0:T(8,128)(2,1)S(1)} %get-tuple-element.38), channel_id=1, source_target_pairs={{8,0},{0,4},{268,8},{260,12},{24,16},{16,20},{284,24},{276,28},{40... | collective-permute-start | bytes 786440 | tf_op jit(solution)/shard_map/ppermute | solution.py:366
  108.1 10.1 %collective-permute-start.4 = (bf16[8,2,64,128]{3,2,1,0:T(8,128)(2,1)S(1)}, bf16[8,2,64,128]{3,2,1,0:T(8,128)(2,1)S(1)}, u32[]{:S(2)}, u32[]{:S(2)}) collective-permute-start(bf16[8,2,64,128]{3,2,1,0:T(8,128)(2,1)S(1)} %get-tuple-element.39), channel_id=1, source_target_pairs={{0,0},{8,4},{260,8},{268,12},{16,16},{24,20},{276,24},{284,28},{32... | collective-permute-start | bytes 786440 | tf_op jit(solution)/shard_map/ppermute | solution.py:365

commit v4 on v3

--- a/solution.py
+++ b/solution.py
@@ -21,6 +21,7 @@
 WINDOWS = N_Z + 1
 GROUP = 6
 SLOTS = 18
+EARLY = 8
 SCALE = 1.0 / math.sqrt(DH)
 BF = jnp.bfloat16
 F32 = jnp.float32
@@ -28,7 +29,7 @@
 SMEM = pl.BlockSpec(memory_space=pltpu.SMEM)
 HBM = pl.BlockSpec(memory_space=pltpu.HBM)
 LIMIT = 12 * 1024 * 1024
-TURN_COST = 11 << 30
+TURN_COST = 49 << 28
 TURN_BYTES = 2 << 20
 
 
@@ -107,13 +108,14 @@
     return jnp.clip(N_Z * y_half - span, 0, N_Z - 1)
 
 
-def send_kernel(core, meta, k_ref, v_ref, out_ref, sem):
-    blocks = pl.ds(first_of(meta[0], 1 - meta[1]), WINDOWS)
+def first_send_kernel(core, meta, k_ref, v_ref, out_ref, sem):
+    first = first_of(meta[0], 1 - meta[1])
 
     @pl.when(meta[5] == core)
     def _():
         copies = [
-            pltpu.make_async_copy(ref.at[blocks], out_ref.at[n], sem.at[n]) for n, ref in enumerate((k_ref, v_ref))
+            pltpu.make_async_copy(k_ref.at[pl.ds(first, WINDOWS)], out_ref.at[pl.ds(0, WINDOWS)], sem.at[0]),
+            pltpu.make_async_copy(v_ref.at[pl.ds(first, EARLY)], out_ref.at[pl.ds(WINDOWS, EARLY)], sem.at[1]),
         ]
         for copy in copies:
             copy.start()
@@ -121,6 +123,13 @@
             copy.wait()
 
 
+def last_send_kernel(meta, v_ref, out_ref, sem):
+    first = first_of(meta[0], 1 - meta[1])
+    copy = pltpu.make_async_copy(v_ref.at[pl.ds(first + EARLY, WINDOWS - EARLY)], out_ref, sem)
+    copy.start()
+    copy.wait()
+
+
 def turn_kernel(meta, k_ref, v_ref, got0_ref, got1_ref, cos_ref, sin_ref, out_ref):
     cos, sin = cos_ref[...], sin_ref[...]
 
@@ -134,32 +143,55 @@
         def _():
             def step(w, carry):
                 block = block_of(meta[0], meta[1], w)
-                far = block - first_of(meta[0], meta[1])
+                far = jnp.minimum(block - first_of(meta[0], meta[1]), WINDOWS - 1)
                 out_ref[w, 0] = turn(k_ref[block])
-                out_ref[w, 1] = turn(got_ref[0, far])
+                out_ref[w, 1] = turn(got_ref[far])
                 out_ref[w, 2] = v_ref[block]
-                out_ref[w, 3] = got_ref[1, far]
+                out_ref[w, 3] = got_ref[WINDOWS + jnp.minimum(far, EARLY - 1)]
                 return carry
 
-            lax.fori_loop(0, WINDOWS, step, 0)
+            lax.fori_loop(0, SLOTS, step, 0)
 
 
 def main_kernel(
-    meta, len_ref, x_ref, kv_ref, qc_ref, qs_ref, kc_ref, ks_ref,
-    out_hbm, local_hbm, send_hbm, out_ref, local_ref, send_ref, done_ref, out_sem, grad_sem,
+    meta, len_ref, x_ref, kv_hbm, late_hbm, tab_hbm,
+    out_hbm, local_hbm, send_hbm, late_ref, tab_ref, kv_ref, out_ref, local_ref, send_ref, done_ref, one_sem, kv_sem, out_sem, grad_sem,
 ):
     span, y_half, nbr = meta[0], meta[1], meta[2]
-    qc, qs = qc_ref[...], qs_ref[...]
-    kc, ks = kc_ref[...], ks_ref[...]
     lane = lax.broadcasted_iota(jnp.int32, (SPAN, NEIGH), 1)
     last = is_last()
     these = range(GROUP)
     each = [(i, n) for i in these for n in range(NBR)]
 
+    def kv_in(step):
+        slots = pl.ds(step * GROUP, GROUP)
+        return pltpu.make_async_copy(kv_hbm.at[slots], kv_ref.at[slots], kv_sem.at[step])
+
+    firsts = [
+        pltpu.make_async_copy(tab_hbm, tab_ref, one_sem.at[0]),
+        pltpu.make_async_copy(late_hbm, late_ref, one_sem.at[1]),
+    ]
+    firsts[0].start()
+    kv_in(0).start()
+    firsts[1].start()
+    for step in range(1, SLOTS // GROUP):
+        kv_in(step).start()
+    for copy in firsts:
+        copy.wait()
+    qc, qs = tab_ref[0:SPAN], tab_ref[SPAN : 2 * SPAN]
+    kc, ks = tab_ref[2 * SPAN : 2 * SPAN + NEIGH], tab_ref[2 * SPAN + NEIGH :]
+
     def group(step, carry):
         places = [step * GROUP + i for i in these]
-        slots = [jnp.minimum(w, WINDOWS - 1) for w in places]
-        blocks = [block_of(span, y_half, w) for w in slots]
+        blocks = [block_of(span, y_half, w) for w in places]
+        kv_in(step).wait()
+        for w, block in zip(places, blocks):
+            far = jnp.minimum(block - first_of(span, y_half), WINDOWS - 1)
+
+            @pl.when(far >= EARLY)
+            def _():
+                kv_ref[w, 3] = late_ref[far - EARLY]
+
 
         def rows(w, a):
             body = jnp.where(w < N_Z, x_ref[place(jnp.minimum(w, N_Z - 1), span), a].astype(F32), 0.0)
@@ -172,8 +204,8 @@
             unit = NBR * (2 * blocks[i] + span)
             return lane < len_ref[unit + (nbr if n == 0 else 1 - nbr)]
 
-        keys = {(i, n): kv_ref[slots[i], n] for i, n in each}
-        vals = {(i, n): kv_ref[slots[i], 2 + n] for i, n in each}
+        keys = {(i, n): kv_ref[places[i], n] for i, n in each}
+        vals = {(i, n): kv_ref[places[i], 2 + n] for i, n in each}
         q = [rows(w, 0) for w in places]
         gf = [rows(w, 1) for w in places]
         qw = [(x * qc + half_turn(x) * qs).astype(BF) for x in q]
@@ -306,24 +338,29 @@
     meta = jnp.stack([span, (ctx // N_Z) ^ nbr, nbr, tp % 2, ctx, core]).astype(jnp.int32)
     routes_out = routes()
     chunk = shaped(HEADS_HERE, 2, SPAN, DH)
-    qc, qs = map(jnp.asarray, tables([*range(1, SPAN), 0]))
-    kc, ks = map(jnp.asarray, tables(range(NEIGH)))
+    kc, ks = tables(range(NEIGH))
+    tab = jnp.asarray(np.concatenate([*tables([*range(1, SPAN), 0]), kc, ks]))
+    kc, ks = jnp.asarray(kc), jnp.asarray(ks)
     swap = [(i, i ^ 1) for i in range(N_TP)]
 
     r0, r1 = call(pack_kernel, (chunk, chunk), 2, moved=1 << 20)(meta, queries[0], cotangent[0])
-    pair = shaped(2, WINDOWS, NEIGH, DH)
     keys_here, values_here = keys.reshape(N_CTX, NEIGH, DH), values.reshape(N_CTX, NEIGH, DH)
-
-    def swap_of(which, facts):
-        sent = pl.pallas_call(
-            functools.partial(send_kernel, which),
-            out_shape=pair,
-            in_specs=[SMEM, HBM, HBM],
+    in_place = lambda x: pltpu.with_memory_space_constraint(x, pltpu.HBM)
+
+    def sender(kernel, facts, arrays, blocks, sems):
+        return pl.pallas_call(
+            kernel,
+            out_shape=shaped(blocks, NEIGH, DH),
+            in_specs=[SMEM] + [HBM] * len(arrays),
             out_specs=VMEM,
-            scratch_shapes=[pltpu.SemaphoreType.DMA((2,))],
+            scratch_shapes=[sems],
             compiler_params=pltpu.CompilerParams(vmem_limit_bytes=LIMIT),
             cost_estimate=pl.CostEstimate(flops=0, bytes_accessed=2 << 20, transcendentals=0),
-        )(facts, *(pltpu.with_memory_space_constraint(x, pltpu.HBM) for x in (keys_here, values_here)))
+        )(facts, *map(in_place, arrays))
+
+    def swap_of(which, facts):
+        kernel = functools.partial(first_send_kernel, which)
+        sent = sender(kernel, facts, (keys_here, values_here), WINDOWS + EARLY, pltpu.SemaphoreType.DMA((2,)))
         pairs = [(N_DP * a + d, N_DP * b + d) for a, b in swap for d in (which, which + 2)]
         return lax.ppermute(sent, ("tp", "dp"), pairs)
 
@@ -332,7 +369,9 @@
     r0 = lax.ppermute(r0, both, routes_out[0])
     r1 = lax.ppermute(r1, both, routes_out[1])
     got0 = swap_of(0, meta_then)
-    turned = call(turn_kernel, shaped(WINDOWS, 4, NEIGH, DH), 6, flops=TURN_COST, moved=TURN_BYTES)(
+    late = sender(last_send_kernel, meta_then, (values_here,), WINDOWS - EARLY, pltpu.SemaphoreType.DMA)
+    late = lax.ppermute(late, "tp", swap)
+    turned = call(turn_kernel, shaped(SLOTS, 4, NEIGH, DH), 6, flops=TURN_COST, moved=TURN_BYTES)(
         meta, keys_here, values_here, got0, got1, kc, ks
     )
     joined = jnp.concatenate([r0, r1], axis=0)
@@ -343,19 +382,24 @@
     out, d_local, d_send = pl.pallas_call(
         main_kernel,
         out_shape=(in_hbm(*row_set), in_hbm(*grads.shape), in_hbm(*grads.shape)),
-        in_specs=[SMEM, SMEM] + [VMEM] * 6,
+        in_specs=[SMEM, SMEM, VMEM, HBM, HBM, HBM],
         out_specs=(HBM,) * 3,
         scratch_shapes=[
+            pltpu.VMEM((WINDOWS - EARLY, NEIGH, DH), BF),
+            pltpu.VMEM(tab.shape, F32),
+            pltpu.VMEM((SLOTS, 4, NEIGH, DH), BF),
             pltpu.VMEM(row_set, BF),
             pltpu.VMEM(grads.shape, BF),
             pltpu.VMEM(grads.shape, BF),
             pltpu.VMEM((SLOTS, 2, SPAN, DH), BF),
+            pltpu.SemaphoreType.DMA((2,)),
+            pltpu.SemaphoreType.DMA((SLOTS // GROUP,)),
             pltpu.SemaphoreType.DMA((N_Z,)),
             pltpu.SemaphoreType.DMA((SLOTS // GROUP, 2)),
         ],
         compiler_params=pltpu.CompilerParams(vmem_limit_bytes=LIMIT),
         cost_estimate=pl.CostEstimate(flops=1 << 29, bytes_accessed=6 << 20, transcendentals=1 << 18),
-    )(meta, lengths.reshape(-1), rows, turned, qc, qs, kc, ks)
+    )(meta, lengths.reshape(-1), rows, in_place(turned), in_place(late), in_place(tab))
 
     back = lax.all_to_all(out, both, 0, 0, axis_index_groups=z_groups(), tiled=True)
     d_got = lax.ppermute(d_send, "tp", swap)

time: 120 us -> 116 us (0.967)
  waiting for transfers between devices: 55.8 us -> 48.9 us
  Pallas kernels: 16.6 us -> 18.7 us
  starting transfers between devices: 40.9 us -> 42.8 us
  local copies, waits for them, and re-layouts: 4.68 us -> 2.97 us
    ppermute x2, waiting for transfers between devices: 18.1 us -> 13.2 us  [swap_of(): return lax.ppermute(sent, ('tp', 'dp'), pairs)]
    all_to_all x1, waiting for transfers between devices: 12.7 us -> 9.03 us  [shards(): lax.all_to_all(joined, both, 0, 0, axis_index_groups=z_groups(), tiled=True)]
    ppermute x0 -> x1, starting transfers between devices: none -> 1.92 us  [shards(): late = lax.ppermute(late, 'tp', swap)]
    ppermute x1, waiting for transfers between devices: 4.89 us -> 6.79 us  [shards(): r1 = lax.ppermute(back[HEADS_HERE:], both, turned_round(routes_out[1]))]
    unnamed x29 -> x23, local copies, waits for them, and re-layouts: 4.41 us -> 2.71 us
    pallas_call x1, Pallas kernels: 6.15 us -> 7.85 us  [shards(): pl.pallas_call(main_kernel, out_shape=(in_hbm(*row_set), in_hbm(*grads.sh...]
    ppermute x1, starting transfers between devices: 3.27 us -> 1.91 us  [shards(): r0 = lax.ppermute(r0, both, routes_out[0])]
    ppermute x1, starting transfers between devices: 6.18 us -> 7.54 us  [shards(): r1 = lax.ppermute(r1, both, routes_out[1])]
  transfers between devices with their start and end apart: 9 -> 10, of which waited for: 7 -> 7; matrix products, arithmetic and copies ran while one was open for 1% -> 1% of each run, Pallas kernels for 6% -> 7%
where the time goes in v4:
time: 116 us; the launch traced here: 115 us
  waiting for transfers between devices  48.9 us (42%)
  starting transfers between devices  42.8 us (37%)
  Pallas kernels  18.7 us (16%)
  local copies, waits for them, and re-layouts  2.97 us (3%)
    all_to_all x1, waiting for transfers between devices, shards(): lax.all_to_all(out, both, 0, 0, axis_index_groups=z_groups(), tiled=True)  16.3 us
    all_to_all x1, starting transfers between devices, shards(): lax.all_to_all(joined, both, 0, 0, axis_index_groups=z_groups(), tiled=True)  15.1 us
    ppermute x2, waiting for transfers between devices, swap_of(): return lax.ppermute(sent, ('tp', 'dp'), pairs)  13.2 us
    all_to_all x1, waiting for transfers between devices, shards(): lax.all_to_all(joined, both, 0, 0, axis_index_groups=z_groups(), tiled=True)  9.03 us
    pallas_call x1, Pallas kernels, shards(): pl.pallas_call(main_kernel, out_shape=(in_hbm(*row_set), in_hbm(*grads.sh...  7.85 us
    ppermute x1, starting transfers between devices, shards(): r1 = lax.ppermute(r1, both, routes_out[1])  7.54 us
    ppermute x1, waiting for transfers between devices, shards(): r1 = lax.ppermute(back[HEADS_HERE:], both, turned_round(routes_out[1]))  6.79 us
    all_to_all x1, starting transfers between devices, shards(): lax.all_to_all(out, both, 0, 0, axis_index_groups=z_groups(), tiled=True)  5.9 us
  transfers between devices with their start and end apart: 10, of which 7 were waited for; matrix products, arithmetic and copies ran while one was open for 1% of the time, Pallas kernels for 7%

profile of v4, /device:TPU:41, one launch (start us, length us, event | category | flops | bytes accessed | tf_op | source)
XLA Modules:
  0.0 115.1 jit_solution(8517975541780502689)
XLA Ops:
  0.8 1.7 %shard_map.112 = bf16[25,128,128]{2,1,0:T(8,128)(2,1)S(1)} custom-call(s32[6]{0:T(128)S(1)} %stack.24.meta, bf16[32,128,128]{2,1,0:T(8,128)(2,1)} %bitcast.21, bf16[32,128,128]{2,1,0:T(8,128)(2,1)} %bitcast.17), custom_call_target="tpu_custom_call" | custom-call | bytes 2097152 | tf_op jit(solution)/shard_map/pallas_call | solution.py:351
  2.4 3.1 %collective-permute-start = (bf16[25,128,128]{2,1,0:T(8,128)(2,1)S(1)}, bf16[25,128,128]{2,1,0:T(8,128)(2,1)S(1)}, u32[]{:S(2)}, u32[]{:S(2)}) collective-permute-start(bf16[25,128,128]{2,1,0:T(8,128)(2,1)S(1)} %shard_map.112), channel_id=1, source_target_pairs={{1,5},{3,7},{5,1},{7,3},{9,13},{11,15},{13,9},{15,11},{17,21},{19,... | collective-permute-start | bytes 2457608 | tf_op jit(solution)/shard_map/ppermute | solution.py:365
  6.3 13.2 %collective-permute-done.got1_ref = bf16[25,128,128]{2,1,0:T(8,128)(2,1)S(1)} collective-permute-done((bf16[25,128,128]{2,1,0:T(8,128)(2,1)S(1)}, bf16[25,128,128]{2,1,0:T(8,128)(2,1)S(1)}, u32[]{:S(2)}, u32[]{:S(2)}) %collective-permute-start) | collective-permute-done | bytes 819232 | tf_op jit(solution)/shard_map/ppermute | solution.py:365
  19.4 1.9 %collective-permute-start.1 = (bf16[8,2,64,128]{3,2,1,0:T(8,128)(2,1)S(1)}, bf16[8,2,64,128]{3,2,1,0:T(8,128)(2,1)S(1)}, u32[]{:S(2)}, u32[]{:S(2)}) collective-permute-start(bf16[8,2,64,128]{3,2,1,0:T(8,128)(2,1)S(1)} %get-tuple-element.19), channel_id=1, source_target_pairs={{0,0},{4,8},{8,260},{12,268},{16,16},{20,24},{24,276},{28,284},{32... | collective-permute-start | bytes 786440 | tf_op jit(solution)/shard_map/ppermute | solution.py:369
  21.3 7.5 %collective-permute-start.2 = (bf16[8,2,64,128]{3,2,1,0:T(8,128)(2,1)S(1)}, bf16[8,2,64,128]{3,2,1,0:T(8,128)(2,1)S(1)}, u32[]{:S(2)}, u32[]{:S(2)}) collective-permute-start(bf16[8,2,64,128]{3,2,1,0:T(8,128)(2,1)S(1)} %get-tuple-element.20), channel_id=1, source_target_pairs={{0,8},{4,0},{8,268},{12,260},{16,24},{20,16},{24,284},{28,276},{32... | collective-permute-start | bytes 786440 | tf_op jit(solution)/shard_map/ppermute | solution.py:370
  29.5 1.6 %collective-permute-start.3 = (bf16[25,128,128]{2,1,0:T(8,128)(2,1)S(1)}, bf16[25,128,128]{2,1,0:T(8,128)(2,1)}, u32[]{:S(2)}, u32[]{:S(2)}) collective-permute-start(bf16[25,128,128]{2,1,0:T(8,128)(2,1)S(1)} %shard_map.113), channel_id=1, source_target_pairs={{0,4},{2,6},{4,0},{6,2},{8,12},{10,14},{12,8},{14,10},{16,20},{18,... | collective-permute-start | bytes 2457608 | tf_op jit(solution)/shard_map/ppermute | solution.py:365
  31.1 1.2 %collective-permute-done.1 = bf16[8,2,64,128]{3,2,1,0:T(8,128)(2,1)S(1)} collective-permute-done((bf16[8,2,64,128]{3,2,1,0:T(8,128)(2,1)S(1)}, bf16[8,2,64,128]{3,2,1,0:T(8,128)(2,1)S(1)}, u32[]{:S(2)}, u32[]{:S(2)}) %collective-permute-start.1) | collective-permute-done | bytes 262176 | tf_op jit(solution)/shard_map/ppermute | solution.py:369
  32.2 2.3 %collective-permute-done.2 = bf16[8,2,64,128]{3,2,1,0:T(8,128)(2,1)S(1)} collective-permute-done((bf16[8,2,64,128]{3,2,1,0:T(8,128)(2,1)S(1)}, bf16[8,2,64,128]{3,2,1,0:T(8,128)(2,1)S(1)}, u32[]{:S(2)}, u32[]{:S(2)}) %collective-permute-start.2) | collective-permute-done | bytes 262176 | tf_op jit(solution)/shard_map/ppermute | solution.py:370
  35.4 15.1 %all-to-all-start = ((bf16[16,2,64,128]{3,2,1,0:T(8,128)(2,1)}), bf16[16,2,64,128]{3,2,1,0:T(8,128)(2,1)S(1)}, u32[]{:S(2)}, u32[]{:S(2)}) async-start(bf16[16,2,64,128]{3,2,1,0:T(8,128)(2,1)} %pad_maximum_fusion), calls=%async_computation | async-start | bytes 1048576 | tf_op jit(solution)/shard_map/all_to_all | solution.py:378
  50.7 1.5 %shard_map.115 = bf16[9,128,128]{2,1,0:T(8,128)(2,1)S(1)} custom-call(s32[6]{0:T(128)S(1)} %stack.24.meta, bf16[32,128,128]{2,1,0:T(8,128)(2,1)} %bitcast.19), custom_call_target="tpu_custom_call" | custom-call | bytes 2097152 | tf_op jit(solution)/shard_map/pallas_call | solution.py:351
  52.3 1.9 %collective-permute-start.4 = (bf16[9,128,128]{2,1,0:T(8,128)(2,1)S(1)}, bf16[9,128,128]{2,1,0:T(8,128)(2,1)}, u32[]{:S(2)}, u32[]{:S(2)}) collective-permute-start(bf16[9,128,128]{2,1,0:T(8,128)(2,1)S(1)} %shard_map.115), channel_id=1, source_target_pairs={{0,4},{4,0},{8,12},{12,8},{1,5},{5,1},{9,13},{13,9},{2,6},{6,2},{1... | collective-permute-start | bytes 884744 | tf_op jit(solution)/shard_map/ppermute | solution.py:373
  54.3 1.1 copy-done.7
  55.4 2.9 %shard_map.114.kv_hbm = bf16[18,4,128,128]{3,2,1,0:T(8,128)(2,1)S(1)} custom-call(s32[6]{0:T(128)S(1)} %stack.24.meta, bf16[32,128,128]{2,1,0:T(8,128)(2,1)S(1)} %bitcast.23, bf16[32,128,128]{2,1,0:T(8,128)(2,1)S(1)} %bitcast.20, bf16[25,128,128]{2,1,0:T(8,128)(2,1)} %collective-permute-done.3.got0_ref, bf16[25,128,128]{2,1,0:T(8,128)(2,1)S(1)} %copy-done.7, ...), custom_call_target="tpu_custom_call" | custom-call | flops 13153337344 | bytes 2097152 | tf_op jit(solution)/shard_map/pallas_call | solution.py:374
  58.3 1.4 %copy-done.2 = bf16[18,4,128,128]{3,2,1,0:T(8,128)(2,1)} copy-done((bf16[18,4,128,128]{3,2,1,0:T(8,128)(2,1)}, bf16[18,4,128,128]{3,2,1,0:T(8,128)(2,1)S(1)}, u32[]{:S(2)}) %copy-start.2) | copy-done | bytes 2359320
  59.8 9.0 %all-to-all-done.x_ref = bf16[16,2,64,128]{3,2,1,0:T(8,128)(2,1)S(1)} async-done(((bf16[16,2,64,128]{3,2,1,0:T(8,128)(2,1)}), bf16[16,2,64,128]{3,2,1,0:T(8,128)(2,1)S(1)}, u32[]{:S(2)}, u32[]{:S(2)}) %all-to-all-start) | async-done | bytes 524320 | tf_op jit(solution)/shard_map/all_to_all | solution.py:378
  68.9 7.8 %shard_map.116 = (bf16[16,2,64,128]{3,2,1,0:T(8,128)(2,1)}, bf16[18,2,128,128]{3,2,1,0:T(8,128)(2,1)}, bf16[18,2,128,128]{3,2,1,0:T(8,128)(2,1)}) custom-call(s32[6]{0:T(128)S(1)} %stack.24.meta, s32[128]{0:T(128)S(1)} %reshape.23.len_ref, bf16[16,2,64,128]{3,2,1,0:T(8,128)(2,1)S(1)} %all-to-all-done.x_ref, bf16[18,4,128,128]{3,2,1,0:T(8,128)(2,1)} %copy-done.2, ...), custom_call_target="tpu_custom_call" | custom-call | flops 536870912 | bytes 6291456 | tf_op jit(solution)/shard_map/pallas_call | solution.py:382
  76.7 5.9 %all-to-all-start.1 = ((bf16[16,2,64,128]{3,2,1,0:T(8,128)(2,1)}), bf16[16,2,64,128]{3,2,1,0:T(8,128)(2,1)S(1)}, u32[]{:S(2)}, u32[]{:S(2)}) async-start(bf16[16,2,64,128]{3,2,1,0:T(8,128)(2,1)} %get-tuple-element.23), calls=%async_computation.1 | async-start | bytes 1048576 | tf_op jit(solution)/shard_map/all_to_all | solution.py:404
  82.6 1.9 %collective-permute-start.7 = (bf16[18,2,128,128]{3,2,1,0:T(8,128)(2,1)}, bf16[18,2,128,128]{3,2,1,0:T(8,128)(2,1)S(1)}, u32[]{:S(2)}, u32[]{:S(2)}) collective-permute-start(bf16[18,2,128,128]{3,2,1,0:T(8,128)(2,1)} %get-tuple-element.27), channel_id=1, source_target_pairs={{0,4},{4,0},{8,12},{12,8},{1,5},{5,1},{9,13},{13,9},{2,6},{6,2},{1... | collective-permute-start | bytes 3538952 | tf_op jit(solution)/shard_map/ppermute | solution.py:405
  84.6 16.3 %all-to-all-done.1 = bf16[16,2,64,128]{3,2,1,0:T(8,128)(2,1)S(1)} async-done(((bf16[16,2,64,128]{3,2,1,0:T(8,128)(2,1)}), bf16[16,2,64,128]{3,2,1,0:T(8,128)(2,1)S(1)}, u32[]{:S(2)}, u32[]{:S(2)}) %all-to-all-start.1) | async-done | bytes 524320 | tf_op jit(solution)/shard_map/all_to_all | solution.py:404
  100.9 1.9 %collective-permute-start.6 = (bf16[8,2,64,128]{3,2,1,0:T(8,128)(2,1)S(1)}, bf16[8,2,64,128]{3,2,1,0:T(8,128)(2,1)S(1)}, u32[]{:S(2)}, u32[]{:S(2)}) collective-permute-start(bf16[8,2,64,128]{3,2,1,0:T(8,128)(2,1)S(1)} %get-tuple-element.38), channel_id=1, source_target_pairs={{8,0},{0,4},{268,8},{260,12},{24,16},{16,20},{284,24},{276,28},{40... | collective-permute-start | bytes 786440 | tf_op jit(solution)/shard_map/ppermute | solution.py:410
  102.9 1.9 %collective-permute-start.5 = (bf16[8,2,64,128]{3,2,1,0:T(8,128)(2,1)S(1)}, bf16[8,2,64,128]{3,2,1,0:T(8,128)(2,1)S(1)}, u32[]{:S(2)}, u32[]{:S(2)}) collective-permute-start(bf16[8,2,64,128]{3,2,1,0:T(8,128)(2,1)S(1)} %get-tuple-element.39), channel_id=1, source_target_pairs={{0,0},{8,4},{260,8},{268,12},{16,16},{24,20},{276,24},{284,28},{32... | collective-permute-start | bytes 786440 | tf_op jit(solution)/shard_map/ppermute | solution.py:409
  104.8 2.0 %shard_map.118 = (bf16[32,128,128]{2,1,0:T(8,128)(2,1)}, bf16[32,128,128]{2,1,0:T(8,128)(2,1)}) custom-call(s32[6]{0:T(128)S(1)} %stack.24.meta, bf16[18,2,128,128]{3,2,1,0:T(8,128)(2,1)S(1)} %copy-done.3, bf16[18,2,128,128]{3,2,1,0:T(8,128)(2,1)S(1)} %collective-permute-done.7.got_ref), custom_call_target="tpu_custom_call" | custom-call | flops 1000 | bytes 4194304 | tf_op jit(solution)/shard_map/pallas_call | solution.py:407
  106.8 6.8 %collective-permute-done.6.r1_ref = bf16[8,2,64,128]{3,2,1,0:T(8,128)(2,1)S(1)} collective-permute-done((bf16[8,2,64,128]{3,2,1,0:T(8,128)(2,1)S(1)}, bf16[8,2,64,128]{3,2,1,0:T(8,128)(2,1)S(1)}, u32[]{:S(2)}, u32[]{:S(2)}) %collective-permute-start.6) | collective-permute-done | bytes 262176 | tf_op jit(solution)/shard_map/ppermute | solution.py:410
  113.6 1.5 %shard_map.117 = (bf16[128,1024]{1,0:T(8,128)(2,1)}, bf16[128,1024]{1,0:T(8,128)(2,1)}) custom-call(s32[6]{0:T(128)S(1)} %stack.24.meta, bf16[8,2,64,128]{3,2,1,0:T(8,128)(2,1)S(1)} %collective-permute-done.5.r0_ref, bf16[8,2,64,128]{3,2,1,0:T(8,128)(2,1)S(1)} %collective-permute-done.6.r1_ref), custom_call_target="tpu_custom_call" | custom-call | flops 1000 | bytes 1048576 | tf_op jit(solution)/shard_map/pallas_call | solution.py:412
  (31 shorter events, 2.6 us)
Async XLA Ops:
  0.8 4.8 %copy-start.4 = (bf16[1,128,1024]{2,1,0:T(8,128)(2,1)S(1)}, bf16[1,128,1024]{2,1,0:T(8,128)(2,1)}, u32[]{:S(2)}) copy-start(bf16[1,128,1024]{2,1,0:T(8,128)(2,1)} %param.8) | copy-start | bytes 786436
  0.8 4.8 %copy-start.5 = (bf16[1,128,1024]{2,1,0:T(8,128)(2,1)S(1)}, bf16[1,128,1024]{2,1,0:T(8,128)(2,1)}, u32[]{:S(2)}) copy-start(bf16[1,128,1024]{2,1,0:T(8,128)(2,1)} %param.11) | copy-start | bytes 786436
  2.4 17.0 %collective-permute-start = (bf16[25,128,128]{2,1,0:T(8,128)(2,1)S(1)}, bf16[25,128,128]{2,1,0:T(8,128)(2,1)S(1)}, u32[]{:S(2)}, u32[]{:S(2)}) collective-permute-start(bf16[25,128,128]{2,1,0:T(8,128)(2,1)S(1)} %shard_map.112), channel_id=1, source_target_pairs={{1,5},{3,7},{5,1},{7,3},{9,13},{11,15},{13,9},{15,11},{17,21},{19,... | collective-permute-start | bytes 2457608 | tf_op jit(solution)/shard_map/ppermute | solution.py:365
  19.4 10.0 %copy-start.6 = (bf16[25,128,128]{2,1,0:T(8,128)(2,1)}, bf16[25,128,128]{2,1,0:T(8,128)(2,1)S(1)}, u32[]{:S(2)}) copy-start(bf16[25,128,128]{2,1,0:T(8,128)(2,1)S(1)} %collective-permute-done.got1_ref) | copy-start | bytes 2457604
  19.4 12.8 %collective-permute-start.1 = (bf16[8,2,64,128]{3,2,1,0:T(8,128)(2,1)S(1)}, bf16[8,2,64,128]{3,2,1,0:T(8,128)(2,1)S(1)}, u32[]{:S(2)}, u32[]{:S(2)}) collective-permute-start(bf16[8,2,64,128]{3,2,1,0:T(8,128)(2,1)S(1)} %get-tuple-element.19), channel_id=1, source_target_pairs={{0,0},{4,8},{8,260},{12,268},{16,16},{20,24},{24,276},{28,284},{32... | collective-permute-start | bytes 786440 | tf_op jit(solution)/shard_map/ppermute | solution.py:369
  21.3 13.2 %collective-permute-start.2 = (bf16[8,2,64,128]{3,2,1,0:T(8,128)(2,1)S(1)}, bf16[8,2,64,128]{3,2,1,0:T(8,128)(2,1)S(1)}, u32[]{:S(2)}, u32[]{:S(2)}) collective-permute-start(bf16[8,2,64,128]{3,2,1,0:T(8,128)(2,1)S(1)} %get-tuple-element.20), channel_id=1, source_target_pairs={{0,8},{4,0},{8,268},{12,260},{16,24},{20,16},{24,284},{28,276},{32... | collective-permute-start | bytes 786440 | tf_op jit(solution)/shard_map/ppermute | solution.py:370
  29.5 21.0 %copy-start.10 = (s32[1,64,2]{1,2,0:T(2,128)S(1)}, s32[1,64,2]{1,2,0:T(2,128)}, u32[]{:S(2)}) copy-start(s32[1,64,2]{1,2,0:T(2,128)} %param.12) | copy-start | bytes 1540
  29.5 24.7 %collective-permute-start.3 = (bf16[25,128,128]{2,1,0:T(8,128)(2,1)S(1)}, bf16[25,128,128]{2,1,0:T(8,128)(2,1)}, u32[]{:S(2)}, u32[]{:S(2)}) collective-permute-start(bf16[25,128,128]{2,1,0:T(8,128)(2,1)S(1)} %shard_map.113), channel_id=1, source_target_pairs={{0,4},{2,6},{4,0},{6,2},{8,12},{10,14},{12,8},{14,10},{16,20},{18,... | collective-permute-start | bytes 2457608 | tf_op jit(solution)/shard_map/ppermute | solution.py:365
  35.4 18.8 %copy-start = (bf16[1,32,1,1,128,128]{5,4,3,2,1,0:T(8,128)(2,1)S(1)}, bf16[1,32,1,1,128,128]{5,4,3,2,1,0:T(8,128)(2,1)}, u32[]{:S(2)}) copy-start(bf16[1,32,1,1,128,128]{5,4,3,2,1,0:T(8,128)(2,1)} %param.10) | copy-start | bytes 3145732
  35.4 18.8 %copy-start.1 = (bf16[1,32,1,1,128,128]{5,4,3,2,1,0:T(8,128)(2,1)S(1)}, bf16[1,32,1,1,128,128]{5,4,3,2,1,0:T(8,128)(2,1)}, u32[]{:S(2)}) copy-start(bf16[1,32,1,1,128,128]{5,4,3,2,1,0:T(8,128)(2,1)} %param.9) | copy-start | bytes 3145732
  35.4 18.8 %copy-start.8 = (f32[128,128]{1,0:T(8,128)S(1)}, f32[128,128]{1,0:T(8,128)}, u32[]{:S(2)}) copy-start(f32[128,128]{1,0:T(8,128)} %constant.62.clone.sin_ref) | copy-start | bytes 196612
  35.4 33.5 %all-to-all-start = ((bf16[16,2,64,128]{3,2,1,0:T(8,128)(2,1)}), bf16[16,2,64,128]{3,2,1,0:T(8,128)(2,1)S(1)}, u32[]{:S(2)}, u32[]{:S(2)}) async-start(bf16[16,2,64,128]{3,2,1,0:T(8,128)(2,1)} %pad_maximum_fusion), calls=%async_computation | async-start | bytes 1048576 | tf_op jit(solution)/shard_map/all_to_all | solution.py:378
  50.7 3.5 %copy-start.9 = (f32[128,128]{1,0:T(8,128)S(1)}, f32[128,128]{1,0:T(8,128)}, u32[]{:S(2)}) copy-start(f32[128,128]{1,0:T(8,128)} %constant.61.clone.cos_ref) | copy-start | bytes 196612
  52.3 7.6 %collective-permute-start.4 = (bf16[9,128,128]{2,1,0:T(8,128)(2,1)S(1)}, bf16[9,128,128]{2,1,0:T(8,128)(2,1)}, u32[]{:S(2)}, u32[]{:S(2)}) collective-permute-start(bf16[9,128,128]{2,1,0:T(8,128)(2,1)S(1)} %shard_map.115), channel_id=1, source_target_pairs={{0,4},{4,0},{8,12},{12,8},{1,5},{5,1},{9,13},{13,9},{2,6},{6,2},{1... | collective-permute-start | bytes 884744 | tf_op jit(solution)/shard_map/ppermute | solution.py:373
  54.3 1.1 copy-start.7
  58.3 1.4 %copy-start.2 = (bf16[18,4,128,128]{3,2,1,0:T(8,128)(2,1)}, bf16[18,4,128,128]{3,2,1,0:T(8,128)(2,1)S(1)}, u32[]{:S(2)}) copy-start(bf16[18,4,128,128]{3,2,1,0:T(8,128)(2,1)S(1)} %shard_map.114.kv_hbm) | copy-start | bytes 7077892
  76.7 28.1 %copy-start.3 = (bf16[18,2,128,128]{3,2,1,0:T(8,128)(2,1)S(1)}, bf16[18,2,128,128]{3,2,1,0:T(8,128)(2,1)}, u32[]{:S(2)}) copy-start(bf16[18,2,128,128]{3,2,1,0:T(8,128)(2,1)} %get-tuple-element.26.local_ref) | copy-start | bytes 3538948
  76.7 24.1 %all-to-all-start.1 = ((bf16[16,2,64,128]{3,2,1,0:T(8,128)(2,1)}), bf16[16,2,64,128]{3,2,1,0:T(8,128)(2,1)S(1)}, u32[]{:S(2)}, u32[]{:S(2)}) async-start(bf16[16,2,64,128]{3,2,1,0:T(8,128)(2,1)} %get-tuple-element.23), calls=%async_computation.1 | async-start | bytes 1048576 | tf_op jit(solution)/shard_map/all_to_all | solution.py:404
  82.6 22.1 %collective-permute-start.7 = (bf16[18,2,128,128]{3,2,1,0:T(8,128)(2,1)}, bf16[18,2,128,128]{3,2,1,0:T(8,128)(2,1)S(1)}, u32[]{:S(2)}, u32[]{:S(2)}) collective-permute-start(bf16[18,2,128,128]{3,2,1,0:T(8,128)(2,1)} %get-tuple-element.27), channel_id=1, source_target_pairs={{0,4},{4,0},{8,12},{12,8},{1,5},{5,1},{9,13},{13,9},{2,6},{6,2},{1... | collective-permute-start | bytes 3538952 | tf_op jit(solution)/shard_map/ppermute | solution.py:405
  100.9 12.7 %collective-permute-start.6 = (bf16[8,2,64,128]{3,2,1,0:T(8,128)(2,1)S(1)}, bf16[8,2,64,128]{3,2,1,0:T(8,128)(2,1)S(1)}, u32[]{:S(2)}, u32[]{:S(2)}) collective-permute-start(bf16[8,2,64,128]{3,2,1,0:T(8,128)(2,1)S(1)} %get-tuple-element.38), channel_id=1, source_target_pairs={{8,0},{0,4},{268,8},{260,12},{24,16},{16,20},{284,24},{276,28},{40... | collective-permute-start | bytes 786440 | tf_op jit(solution)/shard_map/ppermute | solution.py:410
  102.9 10.8 %collective-permute-start.5 = (bf16[8,2,64,128]{3,2,1,0:T(8,128)(2,1)S(1)}, bf16[8,2,64,128]{3,2,1,0:T(8,128)(2,1)S(1)}, u32[]{:S(2)}, u32[]{:S(2)}) collective-permute-start(bf16[8,2,64,128]{3,2,1,0:T(8,128)(2,1)S(1)} %get-tuple-element.39), channel_id=1, source_target_pairs={{0,0},{8,4},{260,8},{268,12},{16,16},{24,20},{276,24},{284,28},{32... | collective-permute-start | bytes 786440 | tf_op jit(solution)/shard_map/ppermute | solution.py:409

commit v5 on v4

--- a/solution.py
+++ b/solution.py
@@ -21,7 +21,7 @@
 WINDOWS = N_Z + 1
 GROUP = 6
 SLOTS = 18
-EARLY = 8
+EARLY = 4
 SCALE = 1.0 / math.sqrt(DH)
 BF = jnp.bfloat16
 F32 = jnp.float32
@@ -29,7 +29,7 @@
 SMEM = pl.BlockSpec(memory_space=pltpu.SMEM)
 HBM = pl.BlockSpec(memory_space=pltpu.HBM)
 LIMIT = 12 * 1024 * 1024
-TURN_COST = 49 << 28
+TURN_COST = 53 << 28
 TURN_BYTES = 2 << 20
 
 

time: 116 us -> 117 us (level)
  the two profiles are of different devices: /device:TPU:41 before, /device:TPU:35 now
where the time goes in v5:
time: 117 us
  waiting for transfers between devices  48.8 us (42%)
  starting transfers between devices  44.5 us (38%)
  Pallas kernels  18.7 us (16%)
  local copies, waits for them, and re-layouts  2.92 us (2%)
    all_to_all x1, waiting for transfers between devices, shards(): lax.all_to_all(out, both, 0, 0, axis_index_groups=z_groups(), tiled=True)  16.4 us
    all_to_all x1, starting transfers between devices, shards(): lax.all_to_all(joined, both, 0, 0, axis_index_groups=z_groups(), tiled=True)  15.1 us
    ppermute x2, waiting for transfers between devices, swap_of(): return lax.ppermute(sent, ('tp', 'dp'), pairs)  10.1 us
    pallas_call x1, Pallas kernels, shards(): pl.pallas_call(main_kernel, out_shape=(in_hbm(*row_set), in_hbm(*grads.sh...  7.9 us
    ppermute x1, starting transfers between devices, shards(): r1 = lax.ppermute(back[HEADS_HERE:], both, turned_round(routes_out[1]))  7.64 us
    all_to_all x1, waiting for transfers between devices, shards(): lax.all_to_all(joined, both, 0, 0, axis_index_groups=z_groups(), tiled=True)  7.37 us
    all_to_all x1, starting transfers between devices, shards(): lax.all_to_all(out, both, 0, 0, axis_index_groups=z_groups(), tiled=True)  6.16 us
    ppermute x1, waiting for transfers between devices, shards(): r1 = lax.ppermute(back[HEADS_HERE:], both, turned_round(routes_out[1]))  4.95 us
  transfers between devices with their start and end apart: 10, of which 8 were waited for; matrix products, arithmetic and copies ran while one was open for 1% of the time, Pallas kernels for 7%

profile of v5, /device:TPU:35, one launch (start us, length us, event | category | flops | bytes accessed | tf_op | source)
XLA Modules:
  0.0 116.7 jit_solution(5074796189639862813)
XLA Ops:
  0.8 1.6 %shard_map.112 = bf16[21,128,128]{2,1,0:T(8,128)(2,1)S(1)} custom-call(s32[6]{0:T(128)S(1)} %stack.24.meta, bf16[32,128,128]{2,1,0:T(8,128)(2,1)} %bitcast.21, bf16[32,128,128]{2,1,0:T(8,128)(2,1)} %bitcast.17), custom_call_target="tpu_custom_call" | custom-call | bytes 2097152 | tf_op jit(solution)/shard_map/pallas_call | solution.py:351
  2.4 2.2 %collective-permute-start = (bf16[21,128,128]{2,1,0:T(8,128)(2,1)S(1)}, bf16[21,128,128]{2,1,0:T(8,128)(2,1)S(1)}, u32[]{:S(2)}, u32[]{:S(2)}) collective-permute-start(bf16[21,128,128]{2,1,0:T(8,128)(2,1)S(1)} %shard_map.112), channel_id=1, source_target_pairs={{1,5},{3,7},{5,1},{7,3},{9,13},{11,15},{13,9},{15,11},{17,21},{19,... | collective-permute-start | bytes 2064392 | tf_op jit(solution)/shard_map/ppermute | solution.py:365
  5.3 10.1 %collective-permute-done.got1_ref = bf16[21,128,128]{2,1,0:T(8,128)(2,1)S(1)} collective-permute-done((bf16[21,128,128]{2,1,0:T(8,128)(2,1)S(1)}, bf16[21,128,128]{2,1,0:T(8,128)(2,1)S(1)}, u32[]{:S(2)}, u32[]{:S(2)}) %collective-permute-start) | collective-permute-done | bytes 688160 | tf_op jit(solution)/shard_map/ppermute | solution.py:365
  15.3 2.9 %collective-permute-start.1 = (bf16[8,2,64,128]{3,2,1,0:T(8,128)(2,1)S(1)}, bf16[8,2,64,128]{3,2,1,0:T(8,128)(2,1)S(1)}, u32[]{:S(2)}, u32[]{:S(2)}) collective-permute-start(bf16[8,2,64,128]{3,2,1,0:T(8,128)(2,1)S(1)} %get-tuple-element.19), channel_id=1, source_target_pairs={{0,0},{4,8},{8,260},{12,268},{16,16},{20,24},{24,276},{28,284},{32... | collective-permute-start | bytes 786440 | tf_op jit(solution)/shard_map/ppermute | solution.py:369
  18.3 1.9 %collective-permute-start.2 = (bf16[8,2,64,128]{3,2,1,0:T(8,128)(2,1)S(1)}, bf16[8,2,64,128]{3,2,1,0:T(8,128)(2,1)S(1)}, u32[]{:S(2)}, u32[]{:S(2)}) collective-permute-start(bf16[8,2,64,128]{3,2,1,0:T(8,128)(2,1)S(1)} %get-tuple-element.20), channel_id=1, source_target_pairs={{0,8},{4,0},{8,268},{12,260},{16,24},{20,16},{24,284},{28,276},{32... | collective-permute-start | bytes 786440 | tf_op jit(solution)/shard_map/ppermute | solution.py:370
  20.8 1.5 %collective-permute-start.3 = (bf16[21,128,128]{2,1,0:T(8,128)(2,1)S(1)}, bf16[21,128,128]{2,1,0:T(8,128)(2,1)}, u32[]{:S(2)}, u32[]{:S(2)}) collective-permute-start(bf16[21,128,128]{2,1,0:T(8,128)(2,1)S(1)} %shard_map.113), channel_id=1, source_target_pairs={{0,4},{2,6},{4,0},{6,2},{8,12},{10,14},{12,8},{14,10},{16,20},{18,... | collective-permute-start | bytes 2064392 | tf_op jit(solution)/shard_map/ppermute | solution.py:365
  22.3 4.6 %collective-permute-done.1 = bf16[8,2,64,128]{3,2,1,0:T(8,128)(2,1)S(1)} collective-permute-done((bf16[8,2,64,128]{3,2,1,0:T(8,128)(2,1)S(1)}, bf16[8,2,64,128]{3,2,1,0:T(8,128)(2,1)S(1)}, u32[]{:S(2)}, u32[]{:S(2)}) %collective-permute-start.1) | collective-permute-done | bytes 262176 | tf_op jit(solution)/shard_map/ppermute | solution.py:369
  26.9 1.5 %collective-permute-done.2 = bf16[8,2,64,128]{3,2,1,0:T(8,128)(2,1)S(1)} collective-permute-done((bf16[8,2,64,128]{3,2,1,0:T(8,128)(2,1)S(1)}, bf16[8,2,64,128]{3,2,1,0:T(8,128)(2,1)S(1)}, u32[]{:S(2)}, u32[]{:S(2)}) %collective-permute-start.2) | collective-permute-done | bytes 262176 | tf_op jit(solution)/shard_map/ppermute | solution.py:370
  29.2 15.1 %all-to-all-start = ((bf16[16,2,64,128]{3,2,1,0:T(8,128)(2,1)}), bf16[16,2,64,128]{3,2,1,0:T(8,128)(2,1)S(1)}, u32[]{:S(2)}, u32[]{:S(2)}) async-start(bf16[16,2,64,128]{3,2,1,0:T(8,128)(2,1)} %pad_maximum_fusion), calls=%async_computation | async-start | bytes 1048576 | tf_op jit(solution)/shard_map/all_to_all | solution.py:378
  44.5 1.6 %shard_map.115 = bf16[13,128,128]{2,1,0:T(8,128)(2,1)S(1)} custom-call(s32[6]{0:T(128)S(1)} %stack.24.meta, bf16[32,128,128]{2,1,0:T(8,128)(2,1)} %bitcast.19), custom_call_target="tpu_custom_call" | custom-call | bytes 2097152 | tf_op jit(solution)/shard_map/pallas_call | solution.py:351
  46.1 2.3 %collective-permute-start.4 = (bf16[13,128,128]{2,1,0:T(8,128)(2,1)S(1)}, bf16[13,128,128]{2,1,0:T(8,128)(2,1)}, u32[]{:S(2)}, u32[]{:S(2)}) collective-permute-start(bf16[13,128,128]{2,1,0:T(8,128)(2,1)S(1)} %shard_map.115), channel_id=1, source_target_pairs={{0,4},{4,0},{8,12},{12,8},{1,5},{5,1},{9,13},{13,9},{2,6},{6,2},{1... | collective-permute-start | bytes 1277960 | tf_op jit(solution)/shard_map/ppermute | solution.py:373
  49.6 2.9 %shard_map.114.kv_hbm = bf16[18,4,128,128]{3,2,1,0:T(8,128)(2,1)S(1)} custom-call(s32[6]{0:T(128)S(1)} %stack.24.meta, bf16[32,128,128]{2,1,0:T(8,128)(2,1)S(1)} %bitcast.23, bf16[32,128,128]{2,1,0:T(8,128)(2,1)S(1)} %bitcast.20, bf16[21,128,128]{2,1,0:T(8,128)(2,1)} %collective-permute-done.3.got0_ref, bf16[21,128,128]{2,1,0:T(8,128)(2,1)S(1)} %copy-done.7, ...), custom_call_target="tpu_custom_call" | custom-call | flops 14227079168 | bytes 2097152 | tf_op jit(solution)/shard_map/pallas_call | solution.py:374
  52.5 1.4 %copy-done.2 = bf16[18,4,128,128]{3,2,1,0:T(8,128)(2,1)} copy-done((bf16[18,4,128,128]{3,2,1,0:T(8,128)(2,1)}, bf16[18,4,128,128]{3,2,1,0:T(8,128)(2,1)S(1)}, u32[]{:S(2)}) %copy-start.2) | copy-done | bytes 2359320
  55.1 7.4 %all-to-all-done.x_ref = bf16[16,2,64,128]{3,2,1,0:T(8,128)(2,1)S(1)} async-done(((bf16[16,2,64,128]{3,2,1,0:T(8,128)(2,1)}), bf16[16,2,64,128]{3,2,1,0:T(8,128)(2,1)S(1)}, u32[]{:S(2)}, u32[]{:S(2)}) %all-to-all-start) | async-done | bytes 524320 | tf_op jit(solution)/shard_map/all_to_all | solution.py:378
  62.5 7.9 %shard_map.116 = (bf16[16,2,64,128]{3,2,1,0:T(8,128)(2,1)}, bf16[18,2,128,128]{3,2,1,0:T(8,128)(2,1)}, bf16[18,2,128,128]{3,2,1,0:T(8,128)(2,1)}) custom-call(s32[6]{0:T(128)S(1)} %stack.24.meta, s32[128]{0:T(128)S(1)} %reshape.23.len_ref, bf16[16,2,64,128]{3,2,1,0:T(8,128)(2,1)S(1)} %all-to-all-done.x_ref, bf16[18,4,128,128]{3,2,1,0:T(8,128)(2,1)} %copy-done.2, ...), custom_call_target="tpu_custom_call" | custom-call | flops 536870912 | bytes 6291456 | tf_op jit(solution)/shard_map/pallas_call | solution.py:382
  70.4 6.2 %all-to-all-start.1 = ((bf16[16,2,64,128]{3,2,1,0:T(8,128)(2,1)}), bf16[16,2,64,128]{3,2,1,0:T(8,128)(2,1)S(1)}, u32[]{:S(2)}, u32[]{:S(2)}) async-start(bf16[16,2,64,128]{3,2,1,0:T(8,128)(2,1)} %get-tuple-element.23), calls=%async_computation.1 | async-start | bytes 1048576 | tf_op jit(solution)/shard_map/all_to_all | solution.py:404
  76.5 2.9 %collective-permute-start.7 = (bf16[18,2,128,128]{3,2,1,0:T(8,128)(2,1)}, bf16[18,2,128,128]{3,2,1,0:T(8,128)(2,1)S(1)}, u32[]{:S(2)}, u32[]{:S(2)}) collective-permute-start(bf16[18,2,128,128]{3,2,1,0:T(8,128)(2,1)} %get-tuple-element.27), channel_id=1, source_target_pairs={{0,4},{4,0},{8,12},{12,8},{1,5},{5,1},{9,13},{13,9},{2,6},{6,2},{1... | collective-permute-start | bytes 3538952 | tf_op jit(solution)/shard_map/ppermute | solution.py:405
  79.4 16.4 %all-to-all-done.1 = bf16[16,2,64,128]{3,2,1,0:T(8,128)(2,1)S(1)} async-done(((bf16[16,2,64,128]{3,2,1,0:T(8,128)(2,1)}), bf16[16,2,64,128]{3,2,1,0:T(8,128)(2,1)S(1)}, u32[]{:S(2)}, u32[]{:S(2)}) %all-to-all-start.1) | async-done | bytes 524320 | tf_op jit(solution)/shard_map/all_to_all | solution.py:404
  95.9 7.6 %collective-permute-start.6 = (bf16[8,2,64,128]{3,2,1,0:T(8,128)(2,1)S(1)}, bf16[8,2,64,128]{3,2,1,0:T(8,128)(2,1)S(1)}, u32[]{:S(2)}, u32[]{:S(2)}) collective-permute-start(bf16[8,2,64,128]{3,2,1,0:T(8,128)(2,1)S(1)} %get-tuple-element.38), channel_id=1, source_target_pairs={{8,0},{0,4},{268,8},{260,12},{24,16},{16,20},{284,24},{276,28},{40... | collective-permute-start | bytes 786440 | tf_op jit(solution)/shard_map/ppermute | solution.py:410
  103.5 1.9 %collective-permute-start.5 = (bf16[8,2,64,128]{3,2,1,0:T(8,128)(2,1)S(1)}, bf16[8,2,64,128]{3,2,1,0:T(8,128)(2,1)S(1)}, u32[]{:S(2)}, u32[]{:S(2)}) collective-permute-start(bf16[8,2,64,128]{3,2,1,0:T(8,128)(2,1)S(1)} %get-tuple-element.39), channel_id=1, source_target_pairs={{0,0},{8,4},{260,8},{268,12},{16,16},{24,20},{276,24},{284,28},{32... | collective-permute-start | bytes 786440 | tf_op jit(solution)/shard_map/ppermute | solution.py:409
  105.5 2.0 %shard_map.118 = (bf16[32,128,128]{2,1,0:T(8,128)(2,1)}, bf16[32,128,128]{2,1,0:T(8,128)(2,1)}) custom-call(s32[6]{0:T(128)S(1)} %stack.24.meta, bf16[18,2,128,128]{3,2,1,0:T(8,128)(2,1)S(1)} %copy-done.3, bf16[18,2,128,128]{3,2,1,0:T(8,128)(2,1)S(1)} %collective-permute-done.7.got_ref), custom_call_target="tpu_custom_call" | custom-call | flops 1000 | bytes 4194304 | tf_op jit(solution)/shard_map/pallas_call | solution.py:407
  107.5 4.9 %collective-permute-done.6.r1_ref = bf16[8,2,64,128]{3,2,1,0:T(8,128)(2,1)S(1)} collective-permute-done((bf16[8,2,64,128]{3,2,1,0:T(8,128)(2,1)S(1)}, bf16[8,2,64,128]{3,2,1,0:T(8,128)(2,1)S(1)}, u32[]{:S(2)}, u32[]{:S(2)}) %collective-permute-start.6) | collective-permute-done | bytes 262176 | tf_op jit(solution)/shard_map/ppermute | solution.py:410
  112.4 2.8 %collective-permute-done.5.r0_ref = bf16[8,2,64,128]{3,2,1,0:T(8,128)(2,1)S(1)} collective-permute-done((bf16[8,2,64,128]{3,2,1,0:T(8,128)(2,1)S(1)}, bf16[8,2,64,128]{3,2,1,0:T(8,128)(2,1)S(1)}, u32[]{:S(2)}, u32[]{:S(2)}) %collective-permute-start.5) | collective-permute-done | bytes 262176 | tf_op jit(solution)/shard_map/ppermute | solution.py:409
  115.2 1.5 %shard_map.117 = (bf16[128,1024]{1,0:T(8,128)(2,1)}, bf16[128,1024]{1,0:T(8,128)(2,1)}) custom-call(s32[6]{0:T(128)S(1)} %stack.24.meta, bf16[8,2,64,128]{3,2,1,0:T(8,128)(2,1)S(1)} %collective-permute-done.5.r0_ref, bf16[8,2,64,128]{3,2,1,0:T(8,128)(2,1)S(1)} %collective-permute-done.6.r1_ref), custom_call_target="tpu_custom_call" | custom-call | flops 1000 | bytes 1048576 | tf_op jit(solution)/shard_map/pallas_call | solution.py:412
  (31 shorter events, 4.7 us)
Async XLA Ops:
  0.8 3.8 %copy-start.4 = (bf16[1,128,1024]{2,1,0:T(8,128)(2,1)S(1)}, bf16[1,128,1024]{2,1,0:T(8,128)(2,1)}, u32[]{:S(2)}) copy-start(bf16[1,128,1024]{2,1,0:T(8,128)(2,1)} %param.8) | copy-start | bytes 786436
  0.8 3.8 %copy-start.5 = (bf16[1,128,1024]{2,1,0:T(8,128)(2,1)S(1)}, bf16[1,128,1024]{2,1,0:T(8,128)(2,1)}, u32[]{:S(2)}) copy-start(bf16[1,128,1024]{2,1,0:T(8,128)(2,1)} %param.11) | copy-start | bytes 786436
  2.4 12.9 %collective-permute-start = (bf16[21,128,128]{2,1,0:T(8,128)(2,1)S(1)}, bf16[21,128,128]{2,1,0:T(8,128)(2,1)S(1)}, u32[]{:S(2)}, u32[]{:S(2)}) collective-permute-start(bf16[21,128,128]{2,1,0:T(8,128)(2,1)S(1)} %shard_map.112), channel_id=1, source_target_pairs={{1,5},{3,7},{5,1},{7,3},{9,13},{11,15},{13,9},{15,11},{17,21},{19,... | collective-permute-start | bytes 2064392 | tf_op jit(solution)/shard_map/ppermute | solution.py:365
  15.3 5.4 %copy-start.6 = (bf16[21,128,128]{2,1,0:T(8,128)(2,1)}, bf16[21,128,128]{2,1,0:T(8,128)(2,1)S(1)}, u32[]{:S(2)}) copy-start(bf16[21,128,128]{2,1,0:T(8,128)(2,1)S(1)} %collective-permute-done.got1_ref) | copy-start | bytes 2064388
  15.3 11.6 %collective-permute-start.1 = (bf16[8,2,64,128]{3,2,1,0:T(8,128)(2,1)S(1)}, bf16[8,2,64,128]{3,2,1,0:T(8,128)(2,1)S(1)}, u32[]{:S(2)}, u32[]{:S(2)}) collective-permute-start(bf16[8,2,64,128]{3,2,1,0:T(8,128)(2,1)S(1)} %get-tuple-element.19), channel_id=1, source_target_pairs={{0,0},{4,8},{8,260},{12,268},{16,16},{20,24},{24,276},{28,284},{32... | collective-permute-start | bytes 786440 | tf_op jit(solution)/shard_map/ppermute | solution.py:369
  18.3 10.1 %collective-permute-start.2 = (bf16[8,2,64,128]{3,2,1,0:T(8,128)(2,1)S(1)}, bf16[8,2,64,128]{3,2,1,0:T(8,128)(2,1)S(1)}, u32[]{:S(2)}, u32[]{:S(2)}) collective-permute-start(bf16[8,2,64,128]{3,2,1,0:T(8,128)(2,1)S(1)} %get-tuple-element.20), channel_id=1, source_target_pairs={{0,8},{4,0},{8,268},{12,260},{16,24},{20,16},{24,284},{28,276},{32... | collective-permute-start | bytes 786440 | tf_op jit(solution)/shard_map/ppermute | solution.py:370
  20.8 23.5 %copy-start.10 = (s32[1,64,2]{1,2,0:T(2,128)S(1)}, s32[1,64,2]{1,2,0:T(2,128)}, u32[]{:S(2)}) copy-start(s32[1,64,2]{1,2,0:T(2,128)} %param.12) | copy-start | bytes 1540
  20.8 27.6 %collective-permute-start.3 = (bf16[21,128,128]{2,1,0:T(8,128)(2,1)S(1)}, bf16[21,128,128]{2,1,0:T(8,128)(2,1)}, u32[]{:S(2)}, u32[]{:S(2)}) collective-permute-start(bf16[21,128,128]{2,1,0:T(8,128)(2,1)S(1)} %shard_map.113), channel_id=1, source_target_pairs={{0,4},{2,6},{4,0},{6,2},{8,12},{10,14},{12,8},{14,10},{16,20},{18,... | collective-permute-start | bytes 2064392 | tf_op jit(solution)/shard_map/ppermute | solution.py:365
  29.2 19.2 %copy-start = (bf16[1,32,1,1,128,128]{5,4,3,2,1,0:T(8,128)(2,1)S(1)}, bf16[1,32,1,1,128,128]{5,4,3,2,1,0:T(8,128)(2,1)}, u32[]{:S(2)}) copy-start(bf16[1,32,1,1,128,128]{5,4,3,2,1,0:T(8,128)(2,1)} %param.10) | copy-start | bytes 3145732
  29.2 19.3 %copy-start.1 = (bf16[1,32,1,1,128,128]{5,4,3,2,1,0:T(8,128)(2,1)S(1)}, bf16[1,32,1,1,128,128]{5,4,3,2,1,0:T(8,128)(2,1)}, u32[]{:S(2)}) copy-start(bf16[1,32,1,1,128,128]{5,4,3,2,1,0:T(8,128)(2,1)} %param.9) | copy-start | bytes 3145732
  29.2 19.3 %copy-start.8 = (f32[128,128]{1,0:T(8,128)S(1)}, f32[128,128]{1,0:T(8,128)}, u32[]{:S(2)}) copy-start(f32[128,128]{1,0:T(8,128)} %constant.62.clone.sin_ref) | copy-start | bytes 196612
  29.2 19.3 %copy-start.9 = (f32[128,128]{1,0:T(8,128)S(1)}, f32[128,128]{1,0:T(8,128)}, u32[]{:S(2)}) copy-start(f32[128,128]{1,0:T(8,128)} %constant.61.clone.cos_ref) | copy-start | bytes 196612
  29.2 33.3 %all-to-all-start = ((bf16[16,2,64,128]{3,2,1,0:T(8,128)(2,1)}), bf16[16,2,64,128]{3,2,1,0:T(8,128)(2,1)S(1)}, u32[]{:S(2)}, u32[]{:S(2)}) async-start(bf16[16,2,64,128]{3,2,1,0:T(8,128)(2,1)} %pad_maximum_fusion), calls=%async_computation | async-start | bytes 1048576 | tf_op jit(solution)/shard_map/all_to_all | solution.py:378
  46.1 9.0 %collective-permute-start.4 = (bf16[13,128,128]{2,1,0:T(8,128)(2,1)S(1)}, bf16[13,128,128]{2,1,0:T(8,128)(2,1)}, u32[]{:S(2)}, u32[]{:S(2)}) collective-permute-start(bf16[13,128,128]{2,1,0:T(8,128)(2,1)S(1)} %shard_map.115), channel_id=1, source_target_pairs={{0,4},{4,0},{8,12},{12,8},{1,5},{5,1},{9,13},{13,9},{2,6},{6,2},{1... | collective-permute-start | bytes 1277960 | tf_op jit(solution)/shard_map/ppermute | solution.py:373
  48.5 1.1 copy-start.7
  52.5 1.4 %copy-start.2 = (bf16[18,4,128,128]{3,2,1,0:T(8,128)(2,1)}, bf16[18,4,128,128]{3,2,1,0:T(8,128)(2,1)S(1)}, u32[]{:S(2)}) copy-start(bf16[18,4,128,128]{3,2,1,0:T(8,128)(2,1)S(1)} %shard_map.114.kv_hbm) | copy-start | bytes 7077892
  70.4 35.1 %copy-start.3 = (bf16[18,2,128,128]{3,2,1,0:T(8,128)(2,1)S(1)}, bf16[18,2,128,128]{3,2,1,0:T(8,128)(2,1)}, u32[]{:S(2)}) copy-start(bf16[18,2,128,128]{3,2,1,0:T(8,128)(2,1)} %get-tuple-element.26.local_ref) | copy-start | bytes 3538948
  70.4 25.4 %all-to-all-start.1 = ((bf16[16,2,64,128]{3,2,1,0:T(8,128)(2,1)}), bf16[16,2,64,128]{3,2,1,0:T(8,128)(2,1)S(1)}, u32[]{:S(2)}, u32[]{:S(2)}) async-start(bf16[16,2,64,128]{3,2,1,0:T(8,128)(2,1)} %get-tuple-element.23), calls=%async_computation.1 | async-start | bytes 1048576 | tf_op jit(solution)/shard_map/all_to_all | solution.py:404
  76.5 28.9 %collective-permute-start.7 = (bf16[18,2,128,128]{3,2,1,0:T(8,128)(2,1)}, bf16[18,2,128,128]{3,2,1,0:T(8,128)(2,1)S(1)}, u32[]{:S(2)}, u32[]{:S(2)}) collective-permute-start(bf16[18,2,128,128]{3,2,1,0:T(8,128)(2,1)} %get-tuple-element.27), channel_id=1, source_target_pairs={{0,4},{4,0},{8,12},{12,8},{1,5},{5,1},{9,13},{13,9},{2,6},{6,2},{1... | collective-permute-start | bytes 3538952 | tf_op jit(solution)/shard_map/ppermute | solution.py:405
  95.9 16.6 %collective-permute-start.6 = (bf16[8,2,64,128]{3,2,1,0:T(8,128)(2,1)S(1)}, bf16[8,2,64,128]{3,2,1,0:T(8,128)(2,1)S(1)}, u32[]{:S(2)}, u32[]{:S(2)}) collective-permute-start(bf16[8,2,64,128]{3,2,1,0:T(8,128)(2,1)S(1)} %get-tuple-element.38), channel_id=1, source_target_pairs={{8,0},{0,4},{268,8},{260,12},{24,16},{16,20},{284,24},{276,28},{40... | collective-permute-start | bytes 786440 | tf_op jit(solution)/shard_map/ppermute | solution.py:410
  103.5 11.7 %collective-permute-start.5 = (bf16[8,2,64,128]{3,2,1,0:T(8,128)(2,1)S(1)}, bf16[8,2,64,128]{3,2,1,0:T(8,128)(2,1)S(1)}, u32[]{:S(2)}, u32[]{:S(2)}) collective-permute-start(bf16[8,2,64,128]{3,2,1,0:T(8,128)(2,1)S(1)} %get-tuple-element.39), channel_id=1, source_target_pairs={{0,0},{8,4},{260,8},{268,12},{16,16},{24,20},{276,24},{284,28},{32... | collective-permute-start | bytes 786440 | tf_op jit(solution)/shard_map/ppermute | solution.py:409

commit v6 on v4

--- a/solution.py
+++ b/solution.py
@@ -21,7 +21,7 @@
 WINDOWS = N_Z + 1
 GROUP = 6
 SLOTS = 18
-EARLY = 8
+EARLY = 10
 SCALE = 1.0 / math.sqrt(DH)
 BF = jnp.bfloat16
 F32 = jnp.float32

time: 116 us -> 118 us (1.017)
  waiting for transfers between devices: 48.9 us -> 50.4 us
    ppermute x2, waiting for transfers between devices: 13.2 us -> 14.6 us  [swap_of(): return lax.ppermute(sent, ('tp', 'dp'), pairs)]
where the time goes in v6:
time: 118 us; the launch traced here: 117 us
  waiting for transfers between devices  50.4 us (43%)
  starting transfers between devices  43 us (36%)
  Pallas kernels  18.7 us (16%)
  local copies, waits for them, and re-layouts  3 us (3%)
    all_to_all x1, waiting for transfers between devices, shards(): lax.all_to_all(out, both, 0, 0, axis_index_groups=z_groups(), tiled=True)  16.5 us
    all_to_all x1, starting transfers between devices, shards(): lax.all_to_all(joined, both, 0, 0, axis_index_groups=z_groups(), tiled=True)  15.1 us
    ppermute x2, waiting for transfers between devices, swap_of(): return lax.ppermute(sent, ('tp', 'dp'), pairs)  14.6 us
    all_to_all x1, waiting for transfers between devices, shards(): lax.all_to_all(joined, both, 0, 0, axis_index_groups=z_groups(), tiled=True)  9.09 us
    pallas_call x1, Pallas kernels, shards(): pl.pallas_call(main_kernel, out_shape=(in_hbm(*row_set), in_hbm(*grads.sh...  7.82 us
    ppermute x1, starting transfers between devices, shards(): r1 = lax.ppermute(r1, both, routes_out[1])  7.54 us
    ppermute x1, waiting for transfers between devices, shards(): r1 = lax.ppermute(back[HEADS_HERE:], both, turned_round(routes_out[1]))  6.71 us
    all_to_all x1, starting transfers between devices, shards(): lax.all_to_all(out, both, 0, 0, axis_index_groups=z_groups(), tiled=True)  6.13 us
  transfers between devices with their start and end apart: 10, of which 7 were waited for; matrix products, arithmetic and copies ran while one was open for 1% of the time, Pallas kernels for 7%

profile of v6, /device:TPU:41, one launch (start us, length us, event | category | flops | bytes accessed | tf_op | source)
XLA Modules:
  0.0 116.9 jit_solution(8980178493787930492)
XLA Ops:
  0.8 1.7 %shard_map.112 = bf16[27,128,128]{2,1,0:T(8,128)(2,1)S(1)} custom-call(s32[6]{0:T(128)S(1)} %stack.24.meta, bf16[32,128,128]{2,1,0:T(8,128)(2,1)} %bitcast.21, bf16[32,128,128]{2,1,0:T(8,128)(2,1)} %bitcast.17), custom_call_target="tpu_custom_call" | custom-call | bytes 2097152 | tf_op jit(solution)/shard_map/pallas_call | solution.py:351
  2.5 3.1 %collective-permute-start = (bf16[27,128,128]{2,1,0:T(8,128)(2,1)S(1)}, bf16[27,128,128]{2,1,0:T(8,128)(2,1)S(1)}, u32[]{:S(2)}, u32[]{:S(2)}) collective-permute-start(bf16[27,128,128]{2,1,0:T(8,128)(2,1)S(1)} %shard_map.112), channel_id=1, source_target_pairs={{1,5},{3,7},{5,1},{7,3},{9,13},{11,15},{13,9},{15,11},{17,21},{19,... | collective-permute-start | bytes 2654216 | tf_op jit(solution)/shard_map/ppermute | solution.py:365
  6.3 14.6 %collective-permute-done.got1_ref = bf16[27,128,128]{2,1,0:T(8,128)(2,1)S(1)} collective-permute-done((bf16[27,128,128]{2,1,0:T(8,128)(2,1)S(1)}, bf16[27,128,128]{2,1,0:T(8,128)(2,1)S(1)}, u32[]{:S(2)}, u32[]{:S(2)}) %collective-permute-start) | collective-permute-done | bytes 884768 | tf_op jit(solution)/shard_map/ppermute | solution.py:365
  20.9 1.9 %collective-permute-start.1 = (bf16[8,2,64,128]{3,2,1,0:T(8,128)(2,1)S(1)}, bf16[8,2,64,128]{3,2,1,0:T(8,128)(2,1)S(1)}, u32[]{:S(2)}, u32[]{:S(2)}) collective-permute-start(bf16[8,2,64,128]{3,2,1,0:T(8,128)(2,1)S(1)} %get-tuple-element.19), channel_id=1, source_target_pairs={{0,0},{4,8},{8,260},{12,268},{16,16},{20,24},{24,276},{28,284},{32... | collective-permute-start | bytes 786440 | tf_op jit(solution)/shard_map/ppermute | solution.py:369
  22.8 7.5 %collective-permute-start.2 = (bf16[8,2,64,128]{3,2,1,0:T(8,128)(2,1)S(1)}, bf16[8,2,64,128]{3,2,1,0:T(8,128)(2,1)S(1)}, u32[]{:S(2)}, u32[]{:S(2)}) collective-permute-start(bf16[8,2,64,128]{3,2,1,0:T(8,128)(2,1)S(1)} %get-tuple-element.20), channel_id=1, source_target_pairs={{0,8},{4,0},{8,268},{12,260},{16,24},{20,16},{24,284},{28,276},{32... | collective-permute-start | bytes 786440 | tf_op jit(solution)/shard_map/ppermute | solution.py:370
  30.9 1.6 %collective-permute-start.3 = (bf16[27,128,128]{2,1,0:T(8,128)(2,1)S(1)}, bf16[27,128,128]{2,1,0:T(8,128)(2,1)}, u32[]{:S(2)}, u32[]{:S(2)}) collective-permute-start(bf16[27,128,128]{2,1,0:T(8,128)(2,1)S(1)} %shard_map.113), channel_id=1, source_target_pairs={{0,4},{2,6},{4,0},{6,2},{8,12},{10,14},{12,8},{14,10},{16,20},{18,... | collective-permute-start | bytes 2654216 | tf_op jit(solution)/shard_map/ppermute | solution.py:365
  32.5 1.1 collective-permute-done.1
  33.7 2.3 %collective-permute-done.2 = bf16[8,2,64,128]{3,2,1,0:T(8,128)(2,1)S(1)} collective-permute-done((bf16[8,2,64,128]{3,2,1,0:T(8,128)(2,1)S(1)}, bf16[8,2,64,128]{3,2,1,0:T(8,128)(2,1)S(1)}, u32[]{:S(2)}, u32[]{:S(2)}) %collective-permute-start.2) | collective-permute-done | bytes 262176 | tf_op jit(solution)/shard_map/ppermute | solution.py:370
  36.8 15.1 %all-to-all-start = ((bf16[16,2,64,128]{3,2,1,0:T(8,128)(2,1)}), bf16[16,2,64,128]{3,2,1,0:T(8,128)(2,1)S(1)}, u32[]{:S(2)}, u32[]{:S(2)}) async-start(bf16[16,2,64,128]{3,2,1,0:T(8,128)(2,1)} %pad_maximum_fusion), calls=%async_computation | async-start | bytes 1048576 | tf_op jit(solution)/shard_map/all_to_all | solution.py:378
  52.2 1.5 %shard_map.115 = bf16[7,128,128]{2,1,0:T(8,128)(2,1)S(1)} custom-call(s32[6]{0:T(128)S(1)} %stack.24.meta, bf16[32,128,128]{2,1,0:T(8,128)(2,1)} %bitcast.19), custom_call_target="tpu_custom_call" | custom-call | bytes 2097152 | tf_op jit(solution)/shard_map/pallas_call | solution.py:351
  53.7 1.9 %collective-permute-start.4 = (bf16[7,128,128]{2,1,0:T(8,128)(2,1)S(1)}, bf16[7,128,128]{2,1,0:T(8,128)(2,1)}, u32[]{:S(2)}, u32[]{:S(2)}) collective-permute-start(bf16[7,128,128]{2,1,0:T(8,128)(2,1)S(1)} %shard_map.115), channel_id=1, source_target_pairs={{0,4},{4,0},{8,12},{12,8},{1,5},{5,1},{9,13},{13,9},{2,6},{6,2},{1... | collective-permute-start | bytes 688136 | tf_op jit(solution)/shard_map/ppermute | solution.py:373
  55.7 1.2 copy-done.7
  56.8 2.9 %shard_map.114.kv_hbm = bf16[18,4,128,128]{3,2,1,0:T(8,128)(2,1)S(1)} custom-call(s32[6]{0:T(128)S(1)} %stack.24.meta, bf16[32,128,128]{2,1,0:T(8,128)(2,1)S(1)} %bitcast.23, bf16[32,128,128]{2,1,0:T(8,128)(2,1)S(1)} %bitcast.20, bf16[27,128,128]{2,1,0:T(8,128)(2,1)} %collective-permute-done.3.got0_ref, bf16[27,128,128]{2,1,0:T(8,128)(2,1)S(1)} %copy-done.7, ...), custom_call_target="tpu_custom_call" | custom-call | flops 13153337344 | bytes 2097152 | tf_op jit(solution)/shard_map/pallas_call | solution.py:374
  59.8 1.4 %copy-done.2 = bf16[18,4,128,128]{3,2,1,0:T(8,128)(2,1)} copy-done((bf16[18,4,128,128]{3,2,1,0:T(8,128)(2,1)}, bf16[18,4,128,128]{3,2,1,0:T(8,128)(2,1)S(1)}, u32[]{:S(2)}) %copy-start.2) | copy-done | bytes 2359320
  61.2 9.1 %all-to-all-done.x_ref = bf16[16,2,64,128]{3,2,1,0:T(8,128)(2,1)S(1)} async-done(((bf16[16,2,64,128]{3,2,1,0:T(8,128)(2,1)}), bf16[16,2,64,128]{3,2,1,0:T(8,128)(2,1)S(1)}, u32[]{:S(2)}, u32[]{:S(2)}) %all-to-all-start) | async-done | bytes 524320 | tf_op jit(solution)/shard_map/all_to_all | solution.py:378
  70.3 7.8 %shard_map.116 = (bf16[16,2,64,128]{3,2,1,0:T(8,128)(2,1)}, bf16[18,2,128,128]{3,2,1,0:T(8,128)(2,1)}, bf16[18,2,128,128]{3,2,1,0:T(8,128)(2,1)}) custom-call(s32[6]{0:T(128)S(1)} %stack.24.meta, s32[128]{0:T(128)S(1)} %reshape.23.len_ref, bf16[16,2,64,128]{3,2,1,0:T(8,128)(2,1)S(1)} %all-to-all-done.x_ref, bf16[18,4,128,128]{3,2,1,0:T(8,128)(2,1)} %copy-done.2, ...), custom_call_target="tpu_custom_call" | custom-call | flops 536870912 | bytes 6291456 | tf_op jit(solution)/shard_map/pallas_call | solution.py:382
  78.2 6.1 %all-to-all-start.1 = ((bf16[16,2,64,128]{3,2,1,0:T(8,128)(2,1)}), bf16[16,2,64,128]{3,2,1,0:T(8,128)(2,1)S(1)}, u32[]{:S(2)}, u32[]{:S(2)}) async-start(bf16[16,2,64,128]{3,2,1,0:T(8,128)(2,1)} %get-tuple-element.23), calls=%async_computation.1 | async-start | bytes 1048576 | tf_op jit(solution)/shard_map/all_to_all | solution.py:404
  84.3 1.9 %collective-permute-start.7 = (bf16[18,2,128,128]{3,2,1,0:T(8,128)(2,1)}, bf16[18,2,128,128]{3,2,1,0:T(8,128)(2,1)S(1)}, u32[]{:S(2)}, u32[]{:S(2)}) collective-permute-start(bf16[18,2,128,128]{3,2,1,0:T(8,128)(2,1)} %get-tuple-element.27), channel_id=1, source_target_pairs={{0,4},{4,0},{8,12},{12,8},{1,5},{5,1},{9,13},{13,9},{2,6},{6,2},{1... | collective-permute-start | bytes 3538952 | tf_op jit(solution)/shard_map/ppermute | solution.py:405
  86.2 16.5 %all-to-all-done.1 = bf16[16,2,64,128]{3,2,1,0:T(8,128)(2,1)S(1)} async-done(((bf16[16,2,64,128]{3,2,1,0:T(8,128)(2,1)}), bf16[16,2,64,128]{3,2,1,0:T(8,128)(2,1)S(1)}, u32[]{:S(2)}, u32[]{:S(2)}) %all-to-all-start.1) | async-done | bytes 524320 | tf_op jit(solution)/shard_map/all_to_all | solution.py:404
  102.7 1.9 %collective-permute-start.6 = (bf16[8,2,64,128]{3,2,1,0:T(8,128)(2,1)S(1)}, bf16[8,2,64,128]{3,2,1,0:T(8,128)(2,1)S(1)}, u32[]{:S(2)}, u32[]{:S(2)}) collective-permute-start(bf16[8,2,64,128]{3,2,1,0:T(8,128)(2,1)S(1)} %get-tuple-element.38), channel_id=1, source_target_pairs={{8,0},{0,4},{268,8},{260,12},{24,16},{16,20},{284,24},{276,28},{40... | collective-permute-start | bytes 786440 | tf_op jit(solution)/shard_map/ppermute | solution.py:410
  104.6 1.9 %collective-permute-start.5 = (bf16[8,2,64,128]{3,2,1,0:T(8,128)(2,1)S(1)}, bf16[8,2,64,128]{3,2,1,0:T(8,128)(2,1)S(1)}, u32[]{:S(2)}, u32[]{:S(2)}) collective-permute-start(bf16[8,2,64,128]{3,2,1,0:T(8,128)(2,1)S(1)} %get-tuple-element.39), channel_id=1, source_target_pairs={{0,0},{8,4},{260,8},{268,12},{16,16},{24,20},{276,24},{284,28},{32... | collective-permute-start | bytes 786440 | tf_op jit(solution)/shard_map/ppermute | solution.py:409
  106.6 2.0 %shard_map.118 = (bf16[32,128,128]{2,1,0:T(8,128)(2,1)}, bf16[32,128,128]{2,1,0:T(8,128)(2,1)}) custom-call(s32[6]{0:T(128)S(1)} %stack.24.meta, bf16[18,2,128,128]{3,2,1,0:T(8,128)(2,1)S(1)} %copy-done.3, bf16[18,2,128,128]{3,2,1,0:T(8,128)(2,1)S(1)} %collective-permute-done.7.got_ref), custom_call_target="tpu_custom_call" | custom-call | flops 1000 | bytes 4194304 | tf_op jit(solution)/shard_map/pallas_call | solution.py:407
  108.6 6.7 %collective-permute-done.6.r1_ref = bf16[8,2,64,128]{3,2,1,0:T(8,128)(2,1)S(1)} collective-permute-done((bf16[8,2,64,128]{3,2,1,0:T(8,128)(2,1)S(1)}, bf16[8,2,64,128]{3,2,1,0:T(8,128)(2,1)S(1)}, u32[]{:S(2)}, u32[]{:S(2)}) %collective-permute-start.6) | collective-permute-done | bytes 262176 | tf_op jit(solution)/shard_map/ppermute | solution.py:410
  115.4 1.5 %shard_map.117 = (bf16[128,1024]{1,0:T(8,128)(2,1)}, bf16[128,1024]{1,0:T(8,128)(2,1)}) custom-call(s32[6]{0:T(128)S(1)} %stack.24.meta, bf16[8,2,64,128]{3,2,1,0:T(8,128)(2,1)S(1)} %collective-permute-done.5.r0_ref, bf16[8,2,64,128]{3,2,1,0:T(8,128)(2,1)S(1)} %collective-permute-done.6.r1_ref), custom_call_target="tpu_custom_call" | custom-call | flops 1000 | bytes 1048576 | tf_op jit(solution)/shard_map/pallas_call | solution.py:412
  (31 shorter events, 2.6 us)
Async XLA Ops:
  0.8 4.8 %copy-start.4 = (bf16[1,128,1024]{2,1,0:T(8,128)(2,1)S(1)}, bf16[1,128,1024]{2,1,0:T(8,128)(2,1)}, u32[]{:S(2)}) copy-start(bf16[1,128,1024]{2,1,0:T(8,128)(2,1)} %param.8) | copy-start | bytes 786436
  0.8 4.9 %copy-start.5 = (bf16[1,128,1024]{2,1,0:T(8,128)(2,1)S(1)}, bf16[1,128,1024]{2,1,0:T(8,128)(2,1)}, u32[]{:S(2)}) copy-start(bf16[1,128,1024]{2,1,0:T(8,128)(2,1)} %param.11) | copy-start | bytes 786436
  2.5 18.4 %collective-permute-start = (bf16[27,128,128]{2,1,0:T(8,128)(2,1)S(1)}, bf16[27,128,128]{2,1,0:T(8,128)(2,1)S(1)}, u32[]{:S(2)}, u32[]{:S(2)}) collective-permute-start(bf16[27,128,128]{2,1,0:T(8,128)(2,1)S(1)} %shard_map.112), channel_id=1, source_target_pairs={{1,5},{3,7},{5,1},{7,3},{9,13},{11,15},{13,9},{15,11},{17,21},{19,... | collective-permute-start | bytes 2654216 | tf_op jit(solution)/shard_map/ppermute | solution.py:365
  20.9 10.0 %copy-start.6 = (bf16[27,128,128]{2,1,0:T(8,128)(2,1)}, bf16[27,128,128]{2,1,0:T(8,128)(2,1)S(1)}, u32[]{:S(2)}) copy-start(bf16[27,128,128]{2,1,0:T(8,128)(2,1)S(1)} %collective-permute-done.got1_ref) | copy-start | bytes 2654212
  20.9 12.8 %collective-permute-start.1 = (bf16[8,2,64,128]{3,2,1,0:T(8,128)(2,1)S(1)}, bf16[8,2,64,128]{3,2,1,0:T(8,128)(2,1)S(1)}, u32[]{:S(2)}, u32[]{:S(2)}) collective-permute-start(bf16[8,2,64,128]{3,2,1,0:T(8,128)(2,1)S(1)} %get-tuple-element.19), channel_id=1, source_target_pairs={{0,0},{4,8},{8,260},{12,268},{16,16},{20,24},{24,276},{28,284},{32... | collective-permute-start | bytes 786440 | tf_op jit(solution)/shard_map/ppermute | solution.py:369
  22.8 13.2 %collective-permute-start.2 = (bf16[8,2,64,128]{3,2,1,0:T(8,128)(2,1)S(1)}, bf16[8,2,64,128]{3,2,1,0:T(8,128)(2,1)S(1)}, u32[]{:S(2)}, u32[]{:S(2)}) collective-permute-start(bf16[8,2,64,128]{3,2,1,0:T(8,128)(2,1)S(1)} %get-tuple-element.20), channel_id=1, source_target_pairs={{0,8},{4,0},{8,268},{12,260},{16,24},{20,16},{24,284},{28,276},{32... | collective-permute-start | bytes 786440 | tf_op jit(solution)/shard_map/ppermute | solution.py:370
  30.9 21.0 %copy-start.10 = (s32[1,64,2]{1,2,0:T(2,128)S(1)}, s32[1,64,2]{1,2,0:T(2,128)}, u32[]{:S(2)}) copy-start(s32[1,64,2]{1,2,0:T(2,128)} %param.12) | copy-start | bytes 1540
  30.9 24.7 %collective-permute-start.3 = (bf16[27,128,128]{2,1,0:T(8,128)(2,1)S(1)}, bf16[27,128,128]{2,1,0:T(8,128)(2,1)}, u32[]{:S(2)}, u32[]{:S(2)}) collective-permute-start(bf16[27,128,128]{2,1,0:T(8,128)(2,1)S(1)} %shard_map.113), channel_id=1, source_target_pairs={{0,4},{2,6},{4,0},{6,2},{8,12},{10,14},{12,8},{14,10},{16,20},{18,... | collective-permute-start | bytes 2654216 | tf_op jit(solution)/shard_map/ppermute | solution.py:365
  36.8 18.8 %copy-start = (bf16[1,32,1,1,128,128]{5,4,3,2,1,0:T(8,128)(2,1)S(1)}, bf16[1,32,1,1,128,128]{5,4,3,2,1,0:T(8,128)(2,1)}, u32[]{:S(2)}) copy-start(bf16[1,32,1,1,128,128]{5,4,3,2,1,0:T(8,128)(2,1)} %param.10) | copy-start | bytes 3145732
  36.8 18.8 %copy-start.1 = (bf16[1,32,1,1,128,128]{5,4,3,2,1,0:T(8,128)(2,1)S(1)}, bf16[1,32,1,1,128,128]{5,4,3,2,1,0:T(8,128)(2,1)}, u32[]{:S(2)}) copy-start(bf16[1,32,1,1,128,128]{5,4,3,2,1,0:T(8,128)(2,1)} %param.9) | copy-start | bytes 3145732
  36.8 33.5 %all-to-all-start = ((bf16[16,2,64,128]{3,2,1,0:T(8,128)(2,1)}), bf16[16,2,64,128]{3,2,1,0:T(8,128)(2,1)S(1)}, u32[]{:S(2)}, u32[]{:S(2)}) async-start(bf16[16,2,64,128]{3,2,1,0:T(8,128)(2,1)} %pad_maximum_fusion), calls=%async_computation | async-start | bytes 1048576 | tf_op jit(solution)/shard_map/all_to_all | solution.py:378
  52.2 3.5 %copy-start.8 = (f32[128,128]{1,0:T(8,128)S(1)}, f32[128,128]{1,0:T(8,128)}, u32[]{:S(2)}) copy-start(f32[128,128]{1,0:T(8,128)} %constant.62.clone.sin_ref) | copy-start | bytes 196612
  52.2 3.5 %copy-start.9 = (f32[128,128]{1,0:T(8,128)S(1)}, f32[128,128]{1,0:T(8,128)}, u32[]{:S(2)}) copy-start(f32[128,128]{1,0:T(8,128)} %constant.61.clone.cos_ref) | copy-start | bytes 196612
  53.7 7.5 %collective-permute-start.4 = (bf16[7,128,128]{2,1,0:T(8,128)(2,1)S(1)}, bf16[7,128,128]{2,1,0:T(8,128)(2,1)}, u32[]{:S(2)}, u32[]{:S(2)}) collective-permute-start(bf16[7,128,128]{2,1,0:T(8,128)(2,1)S(1)} %shard_map.115), channel_id=1, source_target_pairs={{0,4},{4,0},{8,12},{12,8},{1,5},{5,1},{9,13},{13,9},{2,6},{6,2},{1... | collective-permute-start | bytes 688136 | tf_op jit(solution)/shard_map/ppermute | solution.py:373
  55.7 1.2 %copy-start.7 = (bf16[27,128,128]{2,1,0:T(8,128)(2,1)S(1)}, bf16[27,128,128]{2,1,0:T(8,128)(2,1)}, u32[]{:S(2)}) copy-start(bf16[27,128,128]{2,1,0:T(8,128)(2,1)} %copy-done.6) | copy-start | bytes 2654212
  59.8 1.4 %copy-start.2 = (bf16[18,4,128,128]{3,2,1,0:T(8,128)(2,1)}, bf16[18,4,128,128]{3,2,1,0:T(8,128)(2,1)S(1)}, u32[]{:S(2)}) copy-start(bf16[18,4,128,128]{3,2,1,0:T(8,128)(2,1)S(1)} %shard_map.114.kv_hbm) | copy-start | bytes 7077892
  78.1 28.4 %copy-start.3 = (bf16[18,2,128,128]{3,2,1,0:T(8,128)(2,1)S(1)}, bf16[18,2,128,128]{3,2,1,0:T(8,128)(2,1)}, u32[]{:S(2)}) copy-start(bf16[18,2,128,128]{3,2,1,0:T(8,128)(2,1)} %get-tuple-element.26.local_ref) | copy-start | bytes 3538948
  78.2 24.5 %all-to-all-start.1 = ((bf16[16,2,64,128]{3,2,1,0:T(8,128)(2,1)}), bf16[16,2,64,128]{3,2,1,0:T(8,128)(2,1)S(1)}, u32[]{:S(2)}, u32[]{:S(2)}) async-start(bf16[16,2,64,128]{3,2,1,0:T(8,128)(2,1)} %get-tuple-element.23), calls=%async_computation.1 | async-start | bytes 1048576 | tf_op jit(solution)/shard_map/all_to_all | solution.py:404
  84.3 22.3 %collective-permute-start.7 = (bf16[18,2,128,128]{3,2,1,0:T(8,128)(2,1)}, bf16[18,2,128,128]{3,2,1,0:T(8,128)(2,1)S(1)}, u32[]{:S(2)}, u32[]{:S(2)}) collective-permute-start(bf16[18,2,128,128]{3,2,1,0:T(8,128)(2,1)} %get-tuple-element.27), channel_id=1, source_target_pairs={{0,4},{4,0},{8,12},{12,8},{1,5},{5,1},{9,13},{13,9},{2,6},{6,2},{1... | collective-permute-start | bytes 3538952 | tf_op jit(solution)/shard_map/ppermute | solution.py:405
  102.7 12.6 %collective-permute-start.6 = (bf16[8,2,64,128]{3,2,1,0:T(8,128)(2,1)S(1)}, bf16[8,2,64,128]{3,2,1,0:T(8,128)(2,1)S(1)}, u32[]{:S(2)}, u32[]{:S(2)}) collective-permute-start(bf16[8,2,64,128]{3,2,1,0:T(8,128)(2,1)S(1)} %get-tuple-element.38), channel_id=1, source_target_pairs={{8,0},{0,4},{268,8},{260,12},{24,16},{16,20},{284,24},{276,28},{40... | collective-permute-start | bytes 786440 | tf_op jit(solution)/shard_map/ppermute | solution.py:410
  104.6 10.8 %collective-permute-start.5 = (bf16[8,2,64,128]{3,2,1,0:T(8,128)(2,1)S(1)}, bf16[8,2,64,128]{3,2,1,0:T(8,128)(2,1)S(1)}, u32[]{:S(2)}, u32[]{:S(2)}) collective-permute-start(bf16[8,2,64,128]{3,2,1,0:T(8,128)(2,1)S(1)} %get-tuple-element.39), channel_id=1, source_target_pairs={{0,0},{8,4},{260,8},{268,12},{16,16},{24,20},{276,24},{284,28},{32... | collective-permute-start | bytes 786440 | tf_op jit(solution)/shard_map/ppermute | solution.py:409
